TPU v7x, 32 devices: a whole 2x2x4 slice. The times are simulated.
32 devices in a mesh: img: 16 (over z, y, core), ch: 2 (over x).
Axes of the slice: x: 2, y: 2, z: 4, core: 2. Of those that a mesh axis runs over, the one named last changes fastest.
Arguments:
- features: bfloat16 [512, 64, 1024], P('ch', 'img'), may hold values from -6 to 6
- latents: bfloat16 [64, 512], P('img'), may hold values from -6 to 6
- skip_rgb: float32 [3, 64, 1024], P(None, 'img'), may hold values from -6 to 6
- noises: float32 [2, 64, 4096], P(None, 'img'), may hold values from -6 to 6
- ada_shift: int32 [64, 2], P('img'), may hold values from -8 to 8
- crop_mask: int32 [64, 4096], P('img'), may hold values 0 or 1
- critic_mix: float32 [64, 3], replicated, may hold values from -3.5 to 3.5
- critic_bias: float32 [64], replicated, may hold values from -3 to 3
- critic_out: float32 [64], replicated, may hold values from -0.75 to 0.75
- upsampler: float32 [512, 9, 512], P('ch', None, 'img'), may hold values from -6 to 6
- upsampler_mean: float32 [512, 9, 512], P('ch', None, 'img'), may hold values from -0.0222 to 0.0222
- upsampler_square: float32 [512, 9, 512], P('ch', None, 'img'), may hold values from 2.525e-05 to 0.000101
- refiner: float32 [512, 9, 512], P('ch', None, 'img'), may hold values from -6 to 6
- refiner_mean: float32 [512, 9, 512], P('ch', None, 'img'), may hold values from -5.0835886 to 5.0835886
- refiner_square: float32 [512, 9, 512], P('ch', None, 'img'), may hold values from 1.3240252 to 5.2961006
- affines: float32 [3, 512, 512], P(None, 'img', 'ch'), may hold values from -6 to 6
- affines_mean: float32 [3, 512, 512], P(None, 'img', 'ch'), may hold values from -2.845607 to 2.845607
- affines_square: float32 [3, 512, 512], P(None, 'img', 'ch'), may hold values from 0.41486356 to 1.6594542
- modbias: float32 [3, 512], P(None, 'ch'), may hold values from 0.5 to 1.5
- modbias_mean: float32 [3, 512], P(None, 'ch'), may hold values from -514.3959 to 514.3959
- modbias_square: float32 [3, 512], P(None, 'ch'), may hold values from 13556.588 to 54226.35
- actbias: float32 [2, 512], P(None, 'ch'), may hold values from -3 to 3
- actbias_mean: float32 [2, 512], P(None, 'ch'), may hold values from -1028.7736 to 1028.7736
- actbias_square: float32 [2, 512], P(None, 'ch'), may hold values from 54224.426 to 216897.7
- rgbmix: float32 [3, 512], P(None, 'ch'), may hold values from -6 to 6
- rgbmix_mean: float32 [3, 512], P(None, 'ch'), may hold values from -363.73035 to 363.73035
- rgbmix_square: float32 [3, 512], P(None, 'ch'), may hold values from 6778.202 to 27112.809
- scalars: float32 [5], replicated, may hold values from -3 to 3
- scalars_mean: float32 [5], replicated, may hold values from -13967.032 to 13967.032
- scalars_square: float32 [5], replicated, may hold values from 238.2889 to 39978243, as said below
Outputs:
- features_grad: float32 [512, 64, 1024], P('ch', 'img')
- upsampler_stepped: float32 [512, 9, 512], P('ch', None, 'img')
- upsampler_moment: float32 [512, 9, 512], P('ch', None, 'img')
- upsampler_variance: float32 [512, 9, 512], P('ch', None, 'img')
- refiner_stepped: float32 [512, 9, 512], P('ch', None, 'img')
- refiner_moment: float32 [512, 9, 512], P('ch', None, 'img')
- refiner_variance: float32 [512, 9, 512], P('ch', None, 'img')
- affines_stepped: float32 [3, 512, 512], P(None, 'img', 'ch')
- affines_moment: float32 [3, 512, 512], P(None, 'img', 'ch')
- affines_variance: float32 [3, 512, 512], P(None, 'img', 'ch')
- modbias_stepped: float32 [3, 512], P(None, 'ch')
- modbias_moment: float32 [3, 512], P(None, 'ch')
- modbias_variance: float32 [3, 512], P(None, 'ch')
- actbias_stepped: float32 [2, 512], P(None, 'ch')
- actbias_moment: float32 [2, 512], P(None, 'ch')
- actbias_variance: float32 [2, 512], P(None, 'ch')
- rgbmix_stepped: float32 [3, 512], P(None, 'ch')
- rgbmix_moment: float32 [3, 512], P(None, 'ch')
- rgbmix_variance: float32 [3, 512], P(None, 'ch')
- scalars_stepped: float32 [5], replicated
- scalars_moment: float32 [5], replicated
- scalars_variance: float32 [5], replicated
Inputs may be any that keep to these rules, and one draw needn't show every extreme that they name: `scalars_square`: positive.
All inputs are finite; a program needn't handle non-finite values. No bound on the sum of `crop_mask` on one device may be relied on, other than what follows from the above.
Results may differ from a plain program's by a relative error of at most 0.006.
The roundings to bfloat16 on the way count: a program that leaves them out, or rounds other values in their place, can miss the bound.
Values may be sent and summed in bfloat16 or wider, within the bound.
No kernel may reach another device: no remote copies, remote signals or barrier semaphores. Data moves between devices by JAX's collectives and lax.ppermute only.
A program may use at most 576 MiB of HBM per device.

v0:
```python
import jax
import jax.numpy as jnp
from jax import lax
from jax.sharding import PartitionSpec as P

C = 512
RES = 32
STEP = 10


PRECISE = lax.Precision.HIGHEST
ROOT_TWO = 1.4142135623730951
BETA_ONE = 0.9
BETA_TWO = 0.99
LEARN_RATE = 0.3
DECAY_RATE = 0.01
ADAM_EPS = 1e-08
DEMOD_EPS = 1e-08
TAP_OFFSETS = ((-1, -1), (-1, 0), (-1, 1), (0, -1), (0, 0), (0, 1), (1, -1), (1, 0), (1, 1))
UP_TAPS = (
    (0, 3, 0, 0),
    (1, 2, 0, 0),
    (2, 3, 0, 1),
    (3, 1, 0, 0),
    (4, 0, 0, 0),
    (5, 1, 0, 1),
    (6, 3, 1, 0),
    (7, 2, 1, 0),
    (8, 3, 1, 1),
)


def shift_grid(values, off_row, off_col, grid_side):
    total_pixels = grid_side * grid_side
    moved_by = off_row * grid_side + off_col
    leading = values.shape[:-1]
    if moved_by > 0:
        shifted = jnp.concatenate(
            [values[..., moved_by:], jnp.zeros(leading + (moved_by,), values.dtype)], axis=-1
        )
    elif moved_by < 0:
        shifted = jnp.concatenate(
            [jnp.zeros(leading + (-moved_by,), values.dtype), values[..., :moved_by]], axis=-1
        )
    else:
        shifted = values
    if off_col != 0:
        column = jnp.arange(total_pixels, dtype=jnp.int32) % grid_side
        inside = (column + off_col >= 0) & (column + off_col < grid_side)
        shifted = jnp.where(inside, shifted, jnp.zeros((), values.dtype))
    return shifted


def leaky(values):
    return 0.2 * values + 0.8 * jax.nn.softplus(values)


def slope(values):
    return 0.2 + 0.8 * jax.nn.sigmoid(values)


def upsample_skip(planes, grid_side):
    lattice = planes.reshape(planes.shape[0], planes.shape[1], grid_side, 1, grid_side, 1)
    lattice = jnp.broadcast_to(
        lattice, (planes.shape[0], planes.shape[1], grid_side, 2, grid_side, 2)
    )
    return lattice.reshape(planes.shape[0], planes.shape[1], 4 * grid_side * grid_side)


def translate(planes, shift_pairs, direction, grid_side):

    def single(plane, shift_pair):
        lattice = plane.reshape(plane.shape[0], grid_side, grid_side)
        lattice = jnp.roll(lattice, direction * shift_pair[0], axis=1)
        lattice = jnp.roll(lattice, direction * shift_pair[1], axis=2)
        return lattice.reshape(plane.shape[0], grid_side * grid_side)

    return jax.vmap(single, in_axes=(1, 0), out_axes=1)(planes, shift_pairs)


def alternate(phases, grid_side):
    row_count, images = (phases[0].shape[0], phases[0].shape[1])
    stacked = jnp.stack(phases, axis=0).reshape(2, 2, row_count, images, grid_side, grid_side)
    ordered = jnp.transpose(stacked, (2, 3, 4, 0, 5, 1))
    return ordered.reshape(row_count, images, 4 * grid_side * grid_side)


def split_phases(values, grid_side):
    row_count, images = (values.shape[0], values.shape[1])
    lattice = values.reshape(row_count, images, grid_side, 2, grid_side, 2)
    return [
        lattice[:, :, :, row_parity, :, col_parity].reshape(
            row_count, images, grid_side * grid_side
        )
        for row_parity in (0, 1)
        for col_parity in (0, 1)
    ]


def small_shifts(values, grid_side):
    return [
        shift_grid(values, row_step, column_step, grid_side)
        for row_step in (0, 1)
        for column_step in (0, 1)
    ]


def conv_up(shifted, kernel, grid_side):
    phases = [None, None, None, None]
    for number, phase_index, row_step, column_step in UP_TAPS:
        tap_term = jnp.einsum(
            "io,ibp->obp",
            kernel[:, number, :],
            shifted[row_step * 2 + column_step],
            preferred_element_type=jnp.float32,
        )
        if phases[phase_index] is None:
            phases[phase_index] = tap_term
        else:
            phases[phase_index] = phases[phase_index] + tap_term
    return alternate(phases, grid_side)


def conv_flat(shifted, kernel):
    summed = None
    for number in range(9):
        tap_term = jnp.einsum(
            "io,ibp->obp", kernel[:, number, :], shifted[number], preferred_element_type=jnp.float32
        )
        summed = tap_term if summed is None else summed + tap_term
    return summed


def up_folder(kernel_all, shifted, grid_side, running, shard_piece):
    grad_input, grad_kernel = running
    pieces = split_phases(shard_piece, grid_side)
    columns = [None] * 9
    for number, phase_index, row_step, column_step in UP_TAPS:
        back_term = jnp.einsum(
            "io,obq->ibq",
            kernel_all[:, number, :],
            pieces[phase_index],
            preferred_element_type=jnp.float32,
        )
        grad_input = grad_input + shift_grid(back_term, -row_step, -column_step, grid_side)
        columns[number] = jnp.einsum(
            "ibq,obq->io",
            shifted[row_step * 2 + column_step],
            pieces[phase_index],
            preferred_element_type=jnp.float32,
        )
    grad_kernel = jnp.stack(columns, axis=1)
    return (grad_input, grad_kernel)


def flat_folder(kernel_all, shifted, grid_side, running, shard_piece):
    grad_input, grad_kernel = running
    columns = []
    for number, offsets in enumerate(TAP_OFFSETS):
        back_term = jnp.einsum(
            "io,obp->ibp", kernel_all[:, number, :], shard_piece, preferred_element_type=jnp.float32
        )
        grad_input = grad_input + shift_grid(back_term, -offsets[0], -offsets[1], grid_side)
        columns.append(
            jnp.einsum(
                "ibp,obp->io", shifted[number], shard_piece, preferred_element_type=jnp.float32
            )
        )
    grad_kernel = jnp.stack(columns, axis=1)
    return (grad_input, grad_kernel)


def demod_back(demod_coef, styles, weight_sq):
    grad_style = 2.0 * styles * jnp.dot(demod_coef, weight_sq.T, precision=PRECISE)
    grad_square = jnp.dot((styles * styles).T, demod_coef, precision=PRECISE)
    return (grad_style, grad_square)


def gather_coef(demod_coef):
    return lax.all_gather(demod_coef, "ch", axis=1, tiled=True)


def adam_step(weight, mean_old, square_old, gradient, count):
    moment = BETA_ONE * mean_old + (1.0 - BETA_ONE) * gradient
    variance = BETA_TWO * square_old + (1.0 - BETA_TWO) * gradient * gradient
    fix_one = 1.0 - BETA_ONE**count
    fix_two = 1.0 - BETA_TWO**count
    update = moment / fix_one / (jnp.sqrt(variance / fix_two) + ADAM_EPS) + DECAY_RATE * weight
    return (weight - LEARN_RATE * update, moment, variance)


def body(
    features,
    latents,
    skip_rgb,
    noises,
    ada_shift,
    crop_mask,
    critic_mix,
    critic_bias,
    critic_out,
    upsampler,
    upsampler_mean,
    upsampler_square,
    refiner,
    refiner_mean,
    refiner_square,
    affines,
    affines_mean,
    affines_square,
    modbias,
    modbias_mean,
    modbias_square,
    actbias,
    actbias_mean,
    actbias_square,
    rgbmix,
    rgbmix_mean,
    rgbmix_square,
    scalars,
    scalars_mean,
    scalars_square,
):
    local_chans = features.shape[0]
    grid_side = RES
    out_side = 2 * RES
    ch_index = lax.axis_index("ch")
    col_start = ch_index * local_chans
    up_full, ref_full, aff_full = (
        lax.all_gather(upsampler.astype(jnp.bfloat16), "img", axis=2, tiled=True),
        lax.all_gather(refiner.astype(jnp.bfloat16), "img", axis=2, tiled=True),
        lax.all_gather(affines.astype(jnp.bfloat16), "img", axis=1, tiled=True),
    )
    style_gain = latents.shape[1] ** (-0.5)
    styles = [
        jnp.dot(latents, aff_full[number], preferred_element_type=jnp.float32) * style_gain
        + modbias[number][None, :]
        for number in range(3)
    ]
    up_square = jnp.sum(jnp.square(up_full.astype(jnp.float32)), axis=1)
    ref_square = jnp.sum(jnp.square(ref_full.astype(jnp.float32)), axis=1)
    mod_one = (features * styles[0].T[:, :, None]).astype(jnp.bfloat16)
    part_two = jnp.dot(styles[1] * styles[1], ref_square, precision=PRECISE)
    demod_parts = (jnp.dot(styles[0] * styles[0], up_square, precision=PRECISE), part_two)
    demod_totals = lax.psum((demod_parts[0], demod_parts[1]), "ch")
    demod_two = lax.rsqrt(
        lax.dynamic_slice_in_dim(demod_totals[1], col_start, local_chans, 1) + DEMOD_EPS
    )
    demod_one = lax.rsqrt(
        lax.dynamic_slice_in_dim(demod_totals[0], col_start, local_chans, 1) + DEMOD_EPS
    )
    shifted_one = small_shifts(mod_one, grid_side)
    raw_one = lax.psum_scatter(
        conv_up(shifted_one, up_full, grid_side), "ch", scatter_dimension=0, tiled=True
    )
    pre_one = (
        raw_one * demod_one.T[:, :, None] + scalars[0] * noises[0][None] + actbias[0][:, None, None]
    )
    act_one = leaky(pre_one) * ROOT_TWO
    mod_two = (act_one * styles[1].T[:, :, None]).astype(jnp.bfloat16)
    shifted_two = [shift_grid(mod_two, offsets[0], offsets[1], out_side) for offsets in TAP_OFFSETS]
    raw_two = lax.psum_scatter(
        conv_flat(shifted_two, ref_full), "ch", scatter_dimension=0, tiled=True
    )
    pre_two = (
        raw_two * demod_two.T[:, :, None] + scalars[1] * noises[1][None] + actbias[1][:, None, None]
    )
    act_two = leaky(pre_two) * ROOT_TWO
    mod_three = (act_two * styles[2].T[:, :, None]).astype(jnp.bfloat16)
    rgb_kernel = (rgbmix * C ** (-0.5)).astype(jnp.bfloat16)
    colors_lin = lax.psum(
        jnp.einsum("ci,ibp->cbp", rgb_kernel, mod_three, preferred_element_type=jnp.float32), "ch"
    )
    colors = colors_lin + scalars[2:5][:, None, None] + upsample_skip(skip_rgb, grid_side)
    moved = translate(colors, ada_shift, 1, out_side)
    hidden = (
        jnp.einsum("kc,cbp->kbp", critic_mix, moved, precision=PRECISE) + critic_bias[:, None, None]
    )
    logits = jnp.einsum("k,kbp->bp", critic_out, leaky(hidden), precision=PRECISE)
    crop_weights = crop_mask.astype(jnp.float32)
    grad_logits = -crop_weights * jax.nn.sigmoid(-logits)
    grad_hidden = critic_out[:, None, None] * grad_logits[None] * slope(hidden)
    grad_moved = jnp.einsum("kc,kbp->cbp", critic_mix, grad_hidden, precision=PRECISE)
    grad_colors = translate(grad_moved, ada_shift, -1, out_side)
    color_bias_grad = jnp.sum(grad_colors, axis=(1, 2))
    grad_colors_low = grad_colors.astype(jnp.bfloat16)
    grad_mod_three = jnp.einsum(
        "ci,cbp->ibp", rgb_kernel, grad_colors_low, preferred_element_type=jnp.float32
    )
    grad_rgbmix = jnp.einsum(
        "cbp,ibp->ci", grad_colors_low, mod_three, preferred_element_type=jnp.float32
    ) * C ** (-0.5)
    grad_style_three = jnp.sum(grad_mod_three * act_two, axis=2).T
    grad_pre_two = grad_mod_three * styles[2].T[:, :, None] * ROOT_TWO * slope(pre_two)
    grad_raw_two = (grad_pre_two * demod_two.T[:, :, None]).astype(jnp.bfloat16)
    coef_two = -0.5 * demod_two * demod_two * demod_two * jnp.sum(grad_pre_two * raw_two, axis=2).T
    style_demod_two, square_grad_two = demod_back(gather_coef(coef_two), styles[1], ref_square)
    grad_mod_two, grad_refiner = flat_folder(
        ref_full,
        shifted_two,
        out_side,
        (jnp.zeros(mod_two.shape, jnp.float32), jnp.zeros(ref_full.shape, jnp.float32)),
        lax.all_gather(grad_raw_two, "ch", axis=0, tiled=True),
    )
    grad_refiner = grad_refiner + 2.0 * ref_full.astype(jnp.float32) * square_grad_two[:, None, :]
    grad_style_two = jnp.sum(grad_mod_two * act_one, axis=2).T + style_demod_two
    grad_pre_one = grad_mod_two * styles[1].T[:, :, None] * ROOT_TWO * slope(pre_one)
    grad_raw_one = (grad_pre_one * demod_one.T[:, :, None]).astype(jnp.bfloat16)
    coef_one = -0.5 * demod_one * demod_one * demod_one * jnp.sum(grad_pre_one * raw_one, axis=2).T
    style_demod_one, square_grad_one = demod_back(gather_coef(coef_one), styles[0], up_square)
    grad_mod_one, grad_upsampler = up_folder(
        up_full,
        shifted_one,
        grid_side,
        (jnp.zeros(mod_one.shape, jnp.float32), jnp.zeros(up_full.shape, jnp.float32)),
        lax.all_gather(grad_raw_one, "ch", axis=0, tiled=True),
    )
    grad_upsampler = (
        grad_upsampler + 2.0 * up_full.astype(jnp.float32) * square_grad_one[:, None, :]
    )
    features_grad = grad_mod_one * styles[0].T[:, :, None]
    grad_style_one = jnp.sum(grad_mod_one * features, axis=2).T + style_demod_one
    style_grads = [
        gradient.astype(jnp.bfloat16)
        for gradient in (grad_style_one, grad_style_two, grad_style_three)
    ]
    grad_affines = jnp.stack(
        [
            jnp.dot(latents.T, gradient, preferred_element_type=jnp.float32) * style_gain
            for gradient in style_grads
        ]
    )
    grad_modbias = jnp.stack(
        [jnp.sum(gradient.astype(jnp.float32), axis=0) for gradient in style_grads]
    )
    grad_actbias = jnp.stack(
        [jnp.sum(grad_pre_one, axis=(1, 2)), jnp.sum(grad_pre_two, axis=(1, 2))]
    )
    noise_grads = jnp.stack(
        [jnp.sum(grad_pre_one * noises[0][None]), jnp.sum(grad_pre_two * noises[1][None])]
    )
    up_grad, ref_grad, aff_grad = (
        lax.psum_scatter(grad_upsampler, "img", scatter_dimension=2, tiled=True),
        lax.psum_scatter(grad_refiner, "img", scatter_dimension=2, tiled=True),
        lax.psum_scatter(grad_affines, "img", scatter_dimension=1, tiled=True),
    )
    small_local = jnp.concatenate([grad_modbias, grad_actbias, grad_rgbmix], axis=0)
    small_padded = lax.dynamic_update_slice_in_dim(
        jnp.zeros((8, C), jnp.float32), small_local, col_start, 1
    )
    scalar_local = jnp.concatenate(
        [noise_grads, color_bias_grad * (ch_index == 0).astype(jnp.float32)]
    )
    small_total, scalar_grad = lax.psum((small_padded, scalar_local), ("img", "ch"))
    small_grad = lax.dynamic_slice_in_dim(small_total, col_start, local_chans, 1)
    count = float(STEP)
    up_new = adam_step(upsampler, upsampler_mean, upsampler_square, up_grad, count)
    ref_new = adam_step(refiner, refiner_mean, refiner_square, ref_grad, count)
    aff_new = adam_step(affines, affines_mean, affines_square, aff_grad, count)
    mod_new = adam_step(modbias, modbias_mean, modbias_square, small_grad[0:3], count)
    act_new = adam_step(actbias, actbias_mean, actbias_square, small_grad[3:5], count)
    rgb_new = adam_step(rgbmix, rgbmix_mean, rgbmix_square, small_grad[5:8], count)
    scal_new = adam_step(scalars, scalars_mean, scalars_square, scalar_grad, count)
    return (
        features_grad,
        up_new[0],
        up_new[1],
        up_new[2],
        ref_new[0],
        ref_new[1],
        ref_new[2],
        aff_new[0],
        aff_new[1],
        aff_new[2],
        mod_new[0],
        mod_new[1],
        mod_new[2],
        act_new[0],
        act_new[1],
        act_new[2],
        rgb_new[0],
        rgb_new[1],
        rgb_new[2],
        scal_new[0],
        scal_new[1],
        scal_new[2],
    )


def solution(mesh):
    placed = (
        P("ch", "img", None),
        P("img", None),
        P(None, "img", None),
        P(None, "img", None),
        P("img", None),
        P("img", None),
        P(),
        P(),
        P(),
        P("ch", None, "img"),
        P("ch", None, "img"),
        P("ch", None, "img"),
        P("ch", None, "img"),
        P("ch", None, "img"),
        P("ch", None, "img"),
        P(None, "img", "ch"),
        P(None, "img", "ch"),
        P(None, "img", "ch"),
        P(None, "ch"),
        P(None, "ch"),
        P(None, "ch"),
        P(None, "ch"),
        P(None, "ch"),
        P(None, "ch"),
        P(None, "ch"),
        P(None, "ch"),
        P(None, "ch"),
        P(),
        P(),
        P(),
    )
    return jax.shard_map(
        body,
        mesh=mesh,
        in_specs=placed,
        out_specs=(
            P("ch", "img", None),
            P("ch", None, "img"),
            P("ch", None, "img"),
            P("ch", None, "img"),
            P("ch", None, "img"),
            P("ch", None, "img"),
            P("ch", None, "img"),
            P(None, "img", "ch"),
            P(None, "img", "ch"),
            P(None, "img", "ch"),
            P(None, "ch"),
            P(None, "ch"),
            P(None, "ch"),
            P(None, "ch"),
            P(None, "ch"),
            P(None, "ch"),
            P(None, "ch"),
            P(None, "ch"),
            P(None, "ch"),
            P(),
            P(),
            P(),
        ),
        check_vma=False,
    )
```

profile of v0, /device:TPU:0, one launch (start us, length us, event | category | flops | bytes accessed | tf_op | source)
XLA Modules:
  0.0 2337.2 jit_solution(17072767444186192801)
XLA Ops:
  13.0 26.8 %all_gather.21 = bf16[3,512,256]{2,1,0:T(8,128)(2,1)S(1)} all-gather(bf16[3,32,256]{2,1,0:T(8,128)(2,1)S(1)} %convert_element_type.77), channel_id=1, replica_groups=mesh['img'=16,'ch'=2] {'img'}, dimensions={1}, use_global_device_ids=true | all-gather | bytes 835584 | tf_op jit(solution)/shard_map/all_gather | solution.py:232
  103.2 23.2 pad_maximum_fusion
  126.4 55.1 %copy.434 = f32[512,4,32,2,32,2]{0,5,4,3,2,1:T(2,128)} copy(f32[512,4,32,2,32,2]{0,4,2,1,5,3:T(8,128)} %bitcast.510) | data formatting | bytes 67108864 | tf_op jit(solution)/shard_map/transpose | solution.py:84
  181.5 39.8 %reshape.83 = f32[512,4,4096]{0,2,1:T(8,128)} reshape(f32[512,4,32,2,32,2]{0,5,4,3,2,1:T(2,128)} %copy.434) | data formatting | bytes 67108864 | tf_op jit(solution)/shard_map/reshape | solution.py:85
  243.6 346.2 %reduce-scatter.5.cloned.1.call-done = f32[256,4,4096]{0,2,1:T(8,128)} async-done(((f32[512,4,4096]{0,2,1:T(8,128)}), f32[256,4,4096]{0,2,1:T(8,128)}) %reduce-scatter.5.cloned.1.call-update) | async-done | bytes 16777232 | tf_op jit(solution)/shard_map/reduce_scatter | solution.py:253
  589.8 15.5 multiply_convert_fusion.3
  675.0 15.6 fusion.56
  721.4 16.6 fusion.14
  738.1 16.5 fusion.10
  754.6 94.6 %add_bitcast_fusion = f32[512,4,4096]{0,2,1:T(8,128)} fusion(f32[4,4096,512]{2,1,0:T(8,128)} %fusion.10, f32[4,4096,512]{2,1,0:T(8,128)} %fusion.54, f32[4,4096,512]{2,1,0:T(8,128)} %fusion.58, f32[4,4096,512]{2,1,0:T(8,128)} %fusion.140, f32[4,4096,512]{2,1,0:T(8,128)} %fusion.56, f32[4,4096,512]{2,1,0:T(8,128)} %fusion.52, f32[4,4096,512]{2,1,0:T(8,128)} %fusion.49, ...), kind=kOutput, calls=%fused_computation.7 | convolution fusion | flops 4366270464 | bytes 310511616 | tf_op jit(solution)/shard_map/io,ibp->obp/dot_general | solution.py:127
  865.1 353.2 %reduce-scatter.7.cloned.1.call-done = f32[256,4,4096]{0,2,1:T(8,128)} async-done(((f32[512,4,4096]{0,2,1:T(8,128)}), f32[256,4,4096]{0,2,1:T(8,128)}) %reduce-scatter.7.cloned.1.call-update) | async-done | bytes 16777232 | tf_op jit(solution)/shard_map/reduce_scatter | solution.py:262
  1218.3 16.3 fusion.47
  1234.9 23.1 all-reduce.31.cloned.1.call-done
  1292.3 27.4 %multiply_reduce_fusion = (f32[]{:T(128)}, f32[256]{0:T(256)}, f32[256,4]{0,1:T(4,128)}, bf16[256,4]{0,1:T(4,128)(2,1)}, f32[256,4,4096]{0,2,1:T(8,128)S(1)}) fusion(f32[4,4096]{1,0:T(4,128)S(1)} %copy-done.59, f32[256,4,4096]{0,2,1:T(8,128)} %reduce-scatter.7.cloned.1.call-done, f32[256]{0:T(256)S(1)} %bitcast.542, f32[4,4096]{1,0:T(4,128)S(1)} %copy-done.56, ...), kind=kOutput, calls=%fused_computation.17 | convolution fusion | flops 142605568 | bytes 33803268 | tf_op jit(solution)/shard_map/ci,cbp->ibp/dot_general | solution.py:287
  1323.9 198.9 %all-gather.9.cloned.1.call-done = bf16[512,4,4096]{0,2,1:T(8,128)(2,1)} async-done(((bf16[256,4,4096]{0,2,1:T(8,128)(2,1)}), bf16[512,4,4096]{0,2,1:T(8,128)(2,1)}) %all-gather.9.cloned.1.call-update) | async-done | bytes 16777232 | tf_op jit(solution)/shard_map/all_gather | solution.py:303
  1522.8 16.3 convolution_bitcast_fusion
  1683.1 63.3 %multiply_reduce_fusion.1 = (f32[]{:T(128)}, f32[256]{0:T(256)}, f32[256,4]{0,1:T(4,128)S(1)}, f32[256,4]{0,1:T(4,128)S(1)}, f32[256,4,4096]{0,2,1:T(8,128)}) fusion(f32[4,4096]{1,0:T(4,128)S(1)} %copy-done.58, f32[256,4,4096]{0,2,1:T(8,128)} %reduce-scatter.5.cloned.1.call-done, f32[256]{0:T(256)S(1)} %bitcast.535, f32[4,4096]{1,0:T(4,128)S(1)} %copy-done.45, ...), kind=kOutput, calls=%fused_computation.18 | convolution fusion | flops 4471126016 | bytes 183461888 | tf_op jit(solution)/shard_map/io,obp->ibp/dot_general | solution.py:160
  1762.4 18.1 fusion.108
  1883.1 71.6 %all-gather.11.cloned.1.call-done = bf16[512,4,4096]{0,2,1:T(8,128)(2,1)} async-done(((bf16[256,4,4096]{0,2,1:T(8,128)(2,1)}), bf16[512,4,4096]{0,2,1:T(8,128)(2,1)}) %all-gather.11.cloned.1.call-update) | async-done | bytes 16777232 | tf_op jit(solution)/shard_map/all_gather | solution.py:316
  1954.6 25.6 %reshape.88 = bf16[512,4,32,2,32,2]{0,5,4,3,2,1:T(2,128)(2,1)} reshape(bf16[512,4,4096]{0,2,1:T(8,128)(2,1)} %all-gather.11.cloned.1.call-done) | data formatting | bytes 33554432 | tf_op jit(solution)/shard_map/reshape | solution.py:90
  1980.2 44.6 %fusion.240 = (bf16[512,4,32,1,32,1]{0,5,4,3,2,1:T(2,128)(2,1)}, bf16[512,4,32,1,32,1]{0,5,4,3,2,1:T(2,128)(2,1)}, bf16[512,4,32,1,32,1]{0,5,4,3,2,1:T(2,128)(2,1)}, bf16[512,4,32,1,32,1]{0,5,4,3,2,1:T(2,128)(2,1)}) fusion(bf16[512,4,32,2,32,2]{0,5,4,3,2,1:T(2,128)(2,1)} %reshape.88), kind=kLoop, calls=%fused_computation.386 | loop fusion | bytes 33554432 | tf_op jit(solution)/shard_map/slice | solution.py:92
  2143.7 16.0 fusion.129
  2169.4 40.0 %all-reduce.26 = (f32[8,512]{1,0:T(8,128)S(1)}, f32[5]{0:T(128)S(1)}) all-reduce(f32[8,512]{1,0:T(8,128)S(1)} %constant_dynamic-update-slice_fusion, f32[5]{0:T(128)S(1)} %pad_maximum_fusion.6), channel_id=1, replica_groups=mesh['img'=16,'ch'=2] {'img','ch'}, use_global_device_ids=true, to_apply=%region_20.23 | all-reduce | flops 4101 | bytes 32808 | tf_op jit(solution)/shard_map/psum | solution.py:354
  2221.7 106.2 %reduce-scatter.9.cloned.1.call-done = f32[256,9,32]{0,1,2:T(8,128)} async-done(((f32[256,9,512]{0,1,2:T(8,128)}), f32[256,9,32]{0,1,2:T(8,128)}) %reduce-scatter.9.cloned.1.call-update) | async-done | bytes 294928 | tf_op jit(solution)/shard_map/reduce_scatter | solution.py:343
  (422 shorter events, 650.5 us)
Async XLA Ops:
  7.2 50.0 %all-gather.5.cloned.1.call-start = ((), (), s32[]{:S(2)}) async-start(), calls=%async_computation.4 | async-start | bytes 2506752 | tf_op jit(solution)/shard_map/all_gather | solution.py:230
  8.9 216.4 %all-gather.7.cloned.1.call-start = ((), (), s32[]{:S(2)}) async-start(), calls=%async_computation.6 | async-start | bytes 2506752 | tf_op jit(solution)/shard_map/all_gather | solution.py:231
  10.6 579.1 %reduce-scatter.5.cloned.1.call-start = ((), (), s32[]{:S(2)}) async-start(), calls=%async_computation.5 | async-start | bytes 50331648 | tf_op jit(solution)/shard_map/reduce_scatter | solution.py:253
  39.7 183.4 %copy-start.32 = (bf16[3,512,256]{2,1,0:T(8,128)(2,1)}, bf16[3,512,256]{2,1,0:T(8,128)(2,1)S(1)}, u32[]{:S(2)}) copy-start(bf16[3,512,256]{2,1,0:T(8,128)(2,1)S(1)} %all_gather.21) | copy-start | bytes 2359300
  44.5 185.6 %copy-start.46 = (f32[4,256]{1,0:T(4,128)}, f32[4,256]{1,0:T(4,128)S(1)}, u32[]{:S(2)}) copy-start(f32[4,256]{1,0:T(4,128)S(1)} %fusion.124) | copy-start | bytes 12292
  221.3 997.0 %reduce-scatter.7.cloned.1.call-start = ((), (), s32[]{:S(2)}) async-start(), calls=%async_computation.7 | async-start | bytes 50331648 | tf_op jit(solution)/shard_map/reduce_scatter | solution.py:262
  222.5 483.6 %copy-start.37 = (pred[4096]{0:T(1024)(128)(4,1)}, pred[4096]{0:T(1024)(128)(4,1)S(1)}, u32[]{:S(2)}) copy-start(pred[4096]{0:T(1024)(128)(4,1)S(1)} %get-tuple-element.209) | copy-start | bytes 12292
  222.5 532.1 %copy-start.35 = (pred[4096]{0:T(1024)(128)(4,1)}, pred[4096]{0:T(1024)(128)(4,1)S(1)}, u32[]{:S(2)}) copy-start(pred[4096]{0:T(1024)(128)(4,1)S(1)} %get-tuple-element.210) | copy-start | bytes 12292
  223.1 382.2 %copy-start.85 = (f32[1,256]{1,0:T(1,128)}, f32[1,256]{1,0:T(1,128)S(1)}, u32[]{:S(2)}) copy-start(f32[1,256]{1,0:T(1,128)S(1)} %get-tuple-element.194) | copy-start | bytes 3076
  223.3 382.0 %copy-start.53 = (f32[4,256]{1,0:T(4,128)}, f32[4,256]{1,0:T(4,128)S(1)}, u32[]{:S(2)}) copy-start(f32[4,256]{1,0:T(4,128)S(1)} %get-tuple-element.202) | copy-start | bytes 12292
  225.3 380.1 %copy-start.44 = (f32[4,4096]{1,0:T(4,128)}, f32[4,4096]{1,0:T(4,128)S(1)}, u32[]{:S(2)}) copy-start(f32[4,4096]{1,0:T(4,128)S(1)} %get-tuple-element.186) | copy-start | bytes 196612
  243.6 361.8 %copy-start.70 = (f32[4,512]{1,0:T(4,128)}, f32[4,512]{1,0:T(4,128)S(1)}, u32[]{:S(2)}) copy-start(f32[4,512]{1,0:T(4,128)S(1)} %get-tuple-element.144) | copy-start | bytes 24580
  243.6 361.8 %copy-start.61 = (f32[256,4]{0,1:T(4,128)}, f32[256,4]{0,1:T(4,128)S(1)}, u32[]{:S(2)}) copy-start(f32[256,4]{0,1:T(4,128)S(1)} %fusion.178) | copy-start | bytes 12292
  849.3 369.0 %copy-start.56 = (f32[4,4096]{1,0:T(4,128)S(1)}, f32[4,4096]{1,0:T(4,128)}, u32[]{:S(2)}) copy-start(f32[4,4096]{1,0:T(4,128)} %get-tuple-element.183) | copy-start | bytes 196612
  849.3 369.0 %copy-start.79 = (f32[3,256]{1,0:T(4,128)S(1)}, f32[3,256]{1,0:T(4,128)}, u32[]{:S(2)}) copy-start(f32[3,256]{1,0:T(4,128)} %param.58) | copy-start | bytes 9220
  849.3 369.0 %copy-start.95 = (f32[1,256]{1,0:T(1,128)S(1)}, f32[1,256]{1,0:T(1,128)}, u32[]{:S(2)}) copy-start(f32[1,256]{1,0:T(1,128)} %get-tuple-element.193) | copy-start | bytes 3076
  849.3 408.7 %all-reduce.31.cloned.1.call-start = ((), (), s32[]{:S(2)}) async-start(), calls=%async_computation.8 | async-start | bytes 524288 | tf_op jit(solution)/shard_map/psum | solution.py:271
  865.0 369.6 %copy-start.103 = (f32[256,4]{0,1:T(4,128)}, f32[256,4]{0,1:T(4,128)S(1)}, u32[]{:S(2)}) copy-start(f32[256,4]{0,1:T(4,128)S(1)} %get-tuple-element.203) | copy-start | bytes 12292
  865.1 454.6 %copy-start.63 = (f32[256,4]{0,1:T(4,128)}, f32[256,4]{0,1:T(4,128)S(1)}, u32[]{:S(2)}) copy-start(f32[256,4]{0,1:T(4,128)S(1)} %fusion.179) | copy-start | bytes 12292
  1234.7 288.2 %all-gather.9.cloned.1.call-start = ((), (), s32[]{:S(2)}) async-start(), calls=%async_computation.9 | async-start | bytes 25165824 | tf_op jit(solution)/shard_map/all_gather | solution.py:303
  1323.9 630.8 %all-gather.11.cloned.1.call-start = ((), (), s32[]{:S(2)}) async-start(), calls=%async_computation.10 | async-start | bytes 25165824 | tf_op jit(solution)/shard_map/all_gather | solution.py:316
  1755.6 405.9 %reduce-scatter.11.cloned.1.call-start = ((), (), s32[]{:S(2)}) async-start(), calls=%async_computation.12 | async-start | bytes 8912896 | tf_op jit(solution)/shard_map/reduce_scatter | solution.py:344
  1883.0 337.0 %all-reduce.33.cloned.1.call-start = ((), (), s32[]{:S(2)}) async-start(), calls=%async_computation.13 | async-start | bytes 4194304
  2121.7 206.2 %reduce-scatter.9.cloned.1.call-start = ((), (), s32[]{:S(2)}) async-start(), calls=%async_computation.11 | async-start | bytes 8912896 | tf_op jit(solution)/shard_map/reduce_scatter | solution.py:343
  (105 other events, 2456.7 us)
Sparse Core Ops, SparseCore 0:
  10.8 46.3 all-gather.4
  60.0 41.0 all-gather.6
  221.4 368.3 reduce-scatter.4
  849.3 368.8 reduce-scatter.6
  1234.8 23.1 all-reduce.30
  1324.0 198.8 all-gather.8
  1755.7 198.9 all-gather.10
  1959.3 104.7 reduce-scatter.10
  2121.9 98.0 all-reduce.32
  2223.9 103.9 reduce-scatter.8
where the time goes:
time: 2350 us; the launch traced here: 2340 us
  waiting for transfers between devices  1110 us (47%)
  matrix products  651 us (28%)
  local copies, waits for them, and re-layouts  379 us (16%)
  other arithmetic  92.8 us (4%)
  blocking collectives  84.5 us (4%)
    reduce_scatter x1, waiting for transfers between devices, body(): lax.psum_scatter(conv_flat(shifted_two, ref_full), 'ch', scatter_dimensio...  353 us
    reduce_scatter x1, waiting for transfers between devices, body(): lax.psum_scatter(conv_up(shifted_one, up_full, grid_side), 'ch', scatter_...  346 us
    dot_general x9, matrix products, conv_flat(): jnp.einsum('io,ibp->obp', kernel[:, number, :], shifted[number], preferre...  218 us
    all_gather x1, waiting for transfers between devices, body(): lax.all_gather(grad_raw_two, 'ch', axis=0, tiled=True)  199 us
    dot_general x9, matrix products, flat_folder(): jnp.einsum('io,obp->ibp', kernel_all[:, number, :], shard_piece, preferre...  144 us
    reduce_scatter x1, waiting for transfers between devices, body(): lax.psum_scatter(grad_upsampler, 'img', scatter_dimension=2, tiled=True)  106 us
    dot_general x9, matrix products, flat_folder(): jnp.einsum('ibp,obp->io', shifted[number], shard_piece, preferred_element...  99.4 us
    all_gather x1, waiting for transfers between devices, body(): lax.all_gather(grad_raw_one, 'ch', axis=0, tiled=True)  71.6 us
  transfers between devices with their start and end apart: 10, of which 8 were waited for; matrix products, arithmetic and copies ran while one was open for 23% of the time, Pallas kernels for 0%

commit v1 on v0

v1 whole, which is shorter than its diff:
```python
import functools

import jax
import jax.numpy as jnp
from jax import lax
from jax.experimental import pallas as pl
from jax.experimental.pallas import tpu as pltpu
from jax.sharding import PartitionSpec as P

C = 512
RES = 32
STEP = 10

PRECISE = lax.Precision.HIGHEST
ROOT_TWO = 1.4142135623730951
BETA_ONE = 0.9
BETA_TWO = 0.99
LEARN_RATE = 0.3
DECAY_RATE = 0.01
ADAM_EPS = 1e-08
DEMOD_EPS = 1e-08
VMEM_LIMIT = 60 * 2**20
BOTH = ("img", "ch")

PAD = RES
PIX = RES * RES
ROWS = PIX + 2 * PAD
TILE = 256
TAPS = tuple((3 * (dy + 1) + dx + 1, dy, dx) for dy in (-1, 0, 1) for dx in (-1, 0, 1))
UP_TAPS = (
    ((4, 0, 0),),
    ((3, 0, 0), (5, 1, 0)),
    ((1, 0, 0), (7, 0, 1)),
    ((0, 0, 0), (2, 1, 0), (6, 0, 1), (8, 1, 1)),
)
NT = (((1,), (1,)), ((), ()))
TN = (((0,), (0,)), ((), ()))
NN = (((1,), (0,)), ((), ()))


def params(**more):
    return pltpu.CompilerParams(vmem_limit_bytes=VMEM_LIMIT, **more)


def mul(left, right, dims):
    return lax.dot_general(left, right, dims, preferred_element_type=jnp.float32)


def exact(left, right, dims):
    return lax.dot_general(
        left, right, dims, precision=PRECISE, preferred_element_type=jnp.float32
    )


def softplus(values):
    return jnp.maximum(values, 0.0) + jnp.log(1.0 + jnp.exp(-jnp.abs(values)))


def activate(values):
    return (0.2 * ROOT_TWO) * values + (0.8 * ROOT_TWO) * softplus(values)


def slope(values):
    return 0.6 + 0.4 * jnp.tanh(0.5 * values)


def side_copy(values, odd):
    column = lax.broadcasted_iota(jnp.int32, values.shape, 0) & (RES - 1)
    if odd:
        return jnp.where(column == 0, 0.0, pltpu.roll(values, 1, 0))
    return jnp.where(column == RES - 1, 0.0, pltpu.roll(values, values.shape[0] - 1, 0))


def column_sums(values):
    return jnp.sum(values, axis=0, keepdims=True)


def square_sums(weight_ref, out_ref):
    chans = weight_ref.shape[1]
    for start in range(0, chans, 64):
        total = None
        for tap in range(9):
            part = weight_ref[tap, pl.ds(start, 64), :].astype(jnp.float32)
            total = part * part if total is None else total + part * part
        out_ref[pl.ds(start, 64), :] = total


def demod_of(style, squares):
    spread = jnp.broadcast_to(style * style, (8, style.shape[1]))
    return lax.rsqrt(exact(spread, squares, NT)[0:1] + DEMOD_EPS)


def phase_taps(row_parity, col_parity, sign):
    found = []
    for tap, dy, dx in TAPS:
        across = col_parity + sign * dx + 2
        down = row_parity + sign * dy + 2
        copy = 1 if across in (1, 4) else 0
        phase = 2 * (down & 1) + (across & 1)
        first = PAD * (down >> 1)
        found.append((tap, phase, copy, first))
    return found


def tap_rows(ref, phase, copy, first, offset, count):
    start = first + offset
    if not isinstance(start, int):
        start = pl.multiple_of(start, PAD)
    return ref[0, phase, copy, pl.ds(start, count), :]


def write_map(ref, phase, rows_at, values, odd):
    ref[0, phase, 0, rows_at, :] = values.astype(jnp.bfloat16)
    ref[0, phase, 1, rows_at, :] = side_copy(values, odd).astype(jnp.bfloat16)


def clear_pads(ref, phase, both=True):
    empty = jnp.zeros((PAD, ref.shape[-1]), jnp.bfloat16)
    for copy in (0, 1):
        ref[0, phase, copy, 0:PAD, :] = empty
        if both:
            ref[0, phase, copy, PAD + PIX :, :] = empty


def up_forward(
    scal_ref, feat_ref, vec_ref, noise_ref, weight_ref, raw_ref, map_ref, xs_ref, sq_ref, demod_ref
):
    @pl.when(pl.program_id(0) == 0)
    def _():
        square_sums(weight_ref, sq_ref)

    style_one = vec_ref[0, 0:1, :]
    style_two = vec_ref[0, 1:2, :]
    bias = vec_ref[0, 3:4, :]
    demod = demod_of(style_one, sq_ref[...])
    demod_ref[0] = jnp.broadcast_to(demod, demod_ref.shape[1:])
    chans = feat_ref.shape[-1]
    for start in range(0, PIX, TILE):
        values = feat_ref[0, pl.ds(start, TILE), :].astype(jnp.float32) * style_one
        xs_ref[0, 0, pl.ds(start, TILE), :] = values.astype(jnp.bfloat16)
        xs_ref[0, 1, pl.ds(start, TILE), :] = side_copy(values, False).astype(jnp.bfloat16)
    xs_ref[0, 0, PIX:, :] = jnp.zeros((PAD, chans), jnp.bfloat16)
    xs_ref[0, 1, PIX:, :] = jnp.zeros((PAD, chans), jnp.bfloat16)
    strength = scal_ref[0]
    for phase in range(4):
        noise_cols = jnp.transpose(noise_ref[0, 0, phase // 2]) * strength
        clear_pads(map_ref, phase)
        for start in range(0, PIX, TILE):
            raw = None
            for tap, col_step, row_step in UP_TAPS[phase]:
                part = mul(
                    xs_ref[0, col_step, pl.ds(start + PAD * row_step, TILE), :], weight_ref[tap], NT
                )
                raw = part if raw is None else raw + part
            raw_ref[0, phase, pl.ds(start, TILE), :] = raw
            noise = noise_cols[start : start + TILE, phase % 2 : phase % 2 + 1]
            pre = raw * demod + noise + bias
            write_map(
                map_ref, phase, pl.ds(PAD + start, TILE), activate(pre) * style_two, phase % 2 == 1
            )


def flat_forward(
    scal_ref,
    map_ref,
    vec_ref,
    noise_ref,
    base_ref,
    mask_ref,
    critic_ref,
    rgb_ref,
    weight_ref,
    grad_ref,
    sums_ref,
    color_ref,
    raw_buf,
    slope_buf,
    act_buf,
    sq_buf,
):
    row_parity = pl.program_id(1)

    @pl.when((pl.program_id(0) == 0) & (row_parity == 0))
    def _():
        square_sums(weight_ref, sq_buf)

    @pl.when(row_parity == 0)
    def _():
        sums_ref[...] = jnp.zeros_like(sums_ref)
        color_ref[...] = jnp.zeros_like(color_ref)

    style_two = vec_ref[0, 1:2, :]
    style_three = vec_ref[0, 2:3, :]
    bias = vec_ref[0, 4:5, :]
    demod = demod_of(style_two, sq_buf[...])
    strength = scal_ref[1]
    noise_all = jnp.transpose(noise_ref[0, 0, 0])
    rgb = rgb_ref[...]
    for col_parity in (0, 1):
        taps = phase_taps(row_parity, col_parity, 1)
        lines = []
        for start in range(0, PIX, TILE):
            raw = None
            for tap, phase, copy, first in taps:
                part = mul(
                    tap_rows(map_ref, phase, copy, first, start, TILE), weight_ref[tap], NT
                )
                raw = part if raw is None else raw + part
            here = pl.ds(start, TILE)
            raw_buf[here, :] = raw
            noise = noise_all[start : start + TILE, col_parity : col_parity + 1]
            pre = raw * demod + strength * noise + bias
            act = activate(pre)
            act_buf[here, :] = act
            slope_buf[here, :] = slope(pre)
            lines.append(mul(rgb, (act * style_three).astype(jnp.bfloat16), NT))
        colors = jnp.concatenate(lines, axis=1)[0:8] + base_ref[0]
        mix = critic_ref[...]
        hidden = mix[:, 3:4]
        for color in range(3):
            hidden = hidden + mix[:, color : color + 1] * colors[color : color + 1]
        out = mix[:, 4:5]
        unit = 0.2 * hidden + 0.8 * softplus(hidden)
        logits = column_sums(out * unit)
        mask = mask_ref[0, 0, col_parity : col_parity + 1, :]
        grad_logits = -mask / (1.0 + jnp.exp(logits))
        grad_hidden = out * grad_logits * slope(hidden)
        grad_colors = jnp.concatenate(
            [column_sums(mix[:, color : color + 1] * grad_hidden) for color in range(3)]
            + [jnp.zeros((5, PIX), jnp.float32)],
            axis=0,
        )
        total = None
        for lane in range(0, PIX, 128):
            piece = grad_colors[:, lane : lane + 128]
            total = piece if total is None else total + piece
        color_ref[0] += total
        grad_low = jnp.concatenate(
            [grad_colors, jnp.zeros((8, PIX), jnp.float32)], axis=0
        ).astype(jnp.bfloat16)
        clear_pads(grad_ref, col_parity)
        sums = [None] * 4
        rgb_sum = None
        for start in range(0, PIX, TILE):
            here = pl.ds(start, TILE)
            colors_here = grad_low[:, start : start + TILE]
            grad_map = mul(colors_here, rgb, TN)
            act = act_buf[here, :]
            grad_pre = grad_map * (style_three * ROOT_TWO) * slope_buf[here, :]
            write_map(grad_ref, col_parity, pl.ds(PAD + start, TILE), grad_pre * demod, col_parity == 1)
            noise = noise_all[start : start + TILE, col_parity : col_parity + 1]
            found = (
                column_sums(grad_map * act),
                column_sums(grad_pre * raw_buf[here, :]),
                column_sums(grad_pre),
                column_sums(grad_pre * noise),
            )
            sums = [f if s is None else s + f for s, f in zip(sums, found)]
            mixed = mul(colors_here, (act * style_three).astype(jnp.bfloat16), NN)
            rgb_sum = mixed if rgb_sum is None else rgb_sum + mixed
        for row in range(4):
            sums_ref[0, row : row + 1, :] += sums[row]
        sums_ref[0, 8:16, :] += rgb_sum[0:8]

    @pl.when(row_parity == 1)
    def _():
        coef = -0.5 * demod * demod * demod * sums_ref[0, 1:2, :]
        sums_ref[0, 4:5, :] = coef
        back = exact(jnp.broadcast_to(coef, (8, coef.shape[1])), sq_buf[...], NN)[0:1]
        sums_ref[0, 5:6, :] = 2.0 * style_two * back


def spread_out(acc_ref, weight_ref, coef_ref, style_ref, out_ref):
    squares = exact(coef_ref[...], style_ref[...], TN)
    blocks, _, rows, cols = out_ref.shape
    if len(out_ref.shape) == 4 and cols % 128 == 0:
        across = weight_ref.shape[2] // cols
        for tap in range(9):
            grad = acc_ref[tap] + 2.0 * weight_ref[tap].astype(jnp.float32) * squares
            for block in range(blocks):
                row, col = (block // across) * rows, (block % across) * cols
                out_ref[block, tap] = grad[row : row + rows, col : col + cols].astype(out_ref.dtype)
    else:
        for tap in range(9):
            grad = acc_ref[tap] + 2.0 * weight_ref[tap].astype(jnp.float32) * squares
            out_ref[0, tap] = grad.astype(out_ref.dtype)


def flat_weight(grad_ref, map_ref, weight_ref, coef_ref, style_ref, out_ref, acc_ref):
    row_parity = pl.program_id(1)

    @pl.when((pl.program_id(0) == 0) & (row_parity == 0))
    def _():
        acc_ref[...] = jnp.zeros_like(acc_ref)

    for col_parity in (0, 1):
        grad = grad_ref[0, col_parity, 0, PAD : PAD + PIX, :]
        for tap, phase, copy, first in phase_taps(row_parity, col_parity, 1):
            acc_ref[tap] += mul(grad, tap_rows(map_ref, phase, copy, first, 0, PIX), TN)

    @pl.when((pl.program_id(0) == pl.num_programs(0) - 1) & (row_parity == 1))
    def _():
        spread_out(acc_ref, weight_ref, coef_ref, style_ref, out_ref)


def up_weight(grad_ref, xs_ref, weight_ref, coef_ref, style_ref, out_ref, acc_ref):
    @pl.when(pl.program_id(0) == 0)
    def _():
        acc_ref[...] = jnp.zeros_like(acc_ref)

    for phase in range(4):
        grad = grad_ref[0, phase, 0, PAD:, :]
        for tap, col_step, row_step in UP_TAPS[phase]:
            acc_ref[tap] += mul(grad, xs_ref[0, col_step, pl.ds(PAD * row_step, PIX), :], TN)

    @pl.when(pl.program_id(0) == pl.num_programs(0) - 1)
    def _():
        spread_out(acc_ref, weight_ref, coef_ref, style_ref, out_ref)


def flat_back(
    scal_ref, grad_ref, raw_ref, vec_ref, demod_ref, noise_ref, weight_ref, out_ref, sums_ref
):
    row_parity = pl.program_id(1)

    @pl.when(row_parity == 0)
    def _():
        sums_ref[...] = jnp.zeros_like(sums_ref)

    style_two = vec_ref[0, 1:2, :]
    bias = vec_ref[0, 3:4, :]
    demod = demod_ref[0, 0:1, :]
    strength = scal_ref[0]
    noise_all = jnp.transpose(noise_ref[0, 0, 0])
    for col_parity in (0, 1):
        taps = phase_taps(row_parity, col_parity, -1)
        clear_pads(out_ref, col_parity, False)
        sums = [None] * 4
        for start in range(0, PIX, TILE):
            grad_map = None
            for tap, phase, copy, first in taps:
                part = mul(
                    tap_rows(grad_ref, phase, copy, first, start, TILE), weight_ref[tap], NN
                )
                grad_map = part if grad_map is None else grad_map + part
            raw = raw_ref[0, col_parity, pl.ds(start, TILE), :]
            noise = noise_all[start : start + TILE, col_parity : col_parity + 1]
            pre = raw * demod + strength * noise + bias
            grad_pre = grad_map * (style_two * ROOT_TWO) * slope(pre)
            write_map(out_ref, col_parity, pl.ds(PAD + start, TILE), grad_pre * demod, col_parity == 1)
            found = (
                column_sums(grad_map * activate(pre)),
                column_sums(grad_pre * raw),
                column_sums(grad_pre),
                column_sums(grad_pre * noise),
            )
            sums = [f if s is None else s + f for s, f in zip(sums, found)]
        for row in range(4):
            sums_ref[0, row : row + 1, :] += sums[row]


def up_back(grad_ref, feat_ref, vec_ref, weight_ref, out_ref, sums_ref):
    style_one = vec_ref[0, 0:1, :]
    total = None
    for start in range(0, PIX, TILE):
        grad_map = None
        for phase in range(4):
            for tap, col_step, row_step in UP_TAPS[phase]:
                rows = grad_ref[0, phase, col_step, pl.ds(PAD + start - PAD * row_step, TILE), :]
                part = mul(rows, weight_ref[tap], NN)
                grad_map = part if grad_map is None else grad_map + part
        found = column_sums(grad_map * feat_ref[0, pl.ds(start, TILE), :].astype(jnp.float32))
        total = found if total is None else total + found
        out_ref[0, :, pl.ds(start, TILE)] = jnp.transpose(grad_map * style_one)
    sums_ref[0] = jnp.broadcast_to(total, sums_ref.shape[1:])


def whole(shape):
    zeros = (0,) * len(shape)
    return pl.BlockSpec(shape, lambda *ids: zeros)


def per_image(shape):
    zeros = (0,) * (len(shape) - 1)
    return pl.BlockSpec((1,) + tuple(shape[1:]), lambda image, *ids: (image,) + zeros)


SMEM = pl.BlockSpec(memory_space=pltpu.SMEM)


def cost(flops, moved):
    return pl.CostEstimate(flops=int(flops), bytes_accessed=int(moved), transcendentals=0)


def half_phases(shape):
    zeros = (0,) * (len(shape) - 2)
    return pl.BlockSpec(
        (1, 2) + tuple(shape[2:]), lambda image, parity: (image, parity) + zeros
    )


def noise_spec(layer):
    return pl.BlockSpec((1, 1, 1, 8, PIX), lambda image, parity: (image, layer, parity, 0, 0))


def call_up_forward(scalars, feat, vecs, noise, weight):
    images, _, chans = feat.shape
    out_shape = (
        jax.ShapeDtypeStruct((images, 4, PIX, chans), jnp.float32),
        jax.ShapeDtypeStruct((images, 4, 2, ROWS, chans), jnp.bfloat16),
        jax.ShapeDtypeStruct((images, 2, PIX + PAD, chans), jnp.bfloat16),
        jax.ShapeDtypeStruct((chans, chans), jnp.float32),
        jax.ShapeDtypeStruct((images, 8, chans), jnp.float32),
    )
    return pl.pallas_call(
        up_forward,
        grid=(images,),
        in_specs=[
            SMEM,
            per_image(feat.shape),
            per_image(vecs.shape),
            pl.BlockSpec((1, 1, 2, 8, PIX), lambda image: (image, 0, 0, 0, 0)),
            whole(weight.shape),
        ],
        out_specs=[
            per_image(out_shape[0].shape),
            per_image(out_shape[1].shape),
            per_image(out_shape[2].shape),
            whole(out_shape[3].shape),
            per_image(out_shape[4].shape),
        ],
        out_shape=out_shape,
        compiler_params=params(),
        cost_estimate=cost(18 * images * PIX * chans * chans, 60e6),
        name="up_forward",
    )(scalars, feat, vecs, noise, weight)


def call_flat_forward(scalars, maps, vecs, noise, base, mask, critic, rgb, weight):
    images, chans = maps.shape[0], maps.shape[-1]
    out_shape = (
        jax.ShapeDtypeStruct((images, 4, 2, ROWS, chans), jnp.bfloat16),
        jax.ShapeDtypeStruct((images, 16, chans), jnp.float32),
        jax.ShapeDtypeStruct((images, 8, 128), jnp.float32),
    )
    return pl.pallas_call(
        flat_forward,
        grid=(images, 2),
        in_specs=[
            SMEM,
            per_image(maps.shape),
            per_image(vecs.shape),
            noise_spec(1),
            per_image(base.shape),
            pl.BlockSpec((1, 1, 8, PIX), lambda image, parity: (image, parity, 0, 0)),
            whole(critic.shape),
            whole(rgb.shape),
            whole(weight.shape),
        ],
        out_specs=[
            half_phases(out_shape[0].shape),
            per_image(out_shape[1].shape),
            per_image(out_shape[2].shape),
        ],
        out_shape=out_shape,
        scratch_shapes=[pltpu.VMEM((PIX, chans), jnp.float32)] * 3
        + [pltpu.VMEM((chans, chans), jnp.float32)],
        compiler_params=params(),
        cost_estimate=cost(72 * images * PIX * chans * chans, 60e6),
        name="flat_forward",
    )(scalars, maps, vecs, noise, base, mask, critic, rgb, weight)


def gradient_shape(chans, blocks, rows, cols, dtype):
    if cols % 128 == 0:
        return jax.ShapeDtypeStruct((blocks, 9, rows, cols), dtype)
    return jax.ShapeDtypeStruct((1, 9, chans, chans), dtype)


def call_flat_weight(grad, maps, weight, coef, style_sq, out_shape):
    images, chans = maps.shape[0], maps.shape[-1]
    return pl.pallas_call(
        flat_weight,
        grid=(images, 2),
        in_specs=[
            pl.BlockSpec((1, 2, 1, ROWS, chans), lambda image, parity: (image, parity, 0, 0, 0)),
            per_image(maps.shape),
            whole(weight.shape),
            whole(coef.shape),
            whole(style_sq.shape),
        ],
        out_specs=whole(out_shape.shape),
        out_shape=out_shape,
        scratch_shapes=[pltpu.VMEM((9, chans, chans), jnp.float32)],
        compiler_params=params(),
        cost_estimate=cost(72 * images * PIX * chans * chans, 50e6),
        name="flat_weight",
    )(grad, maps, weight, coef, style_sq)


def call_flat_back(scalars, grad, raw, vecs, demod, noise, weight):
    images, chans = grad.shape[0], grad.shape[-1]
    out_shape = (
        jax.ShapeDtypeStruct((images, 4, 2, PIX + PAD, chans), jnp.bfloat16),
        jax.ShapeDtypeStruct((images, 8, chans), jnp.float32),
    )
    return pl.pallas_call(
        flat_back,
        grid=(images, 2),
        in_specs=[
            SMEM,
            per_image(grad.shape),
            half_phases(raw.shape),
            per_image(vecs.shape),
            per_image(demod.shape),
            noise_spec(0),
            whole(weight.shape),
        ],
        out_specs=[half_phases(out_shape[0].shape), per_image(out_shape[1].shape)],
        out_shape=out_shape,
        compiler_params=params(),
        cost_estimate=cost(72 * images * PIX * chans * chans, 60e6),
        name="flat_back",
    )(scalars, grad, raw, vecs, demod, noise, weight)


def call_up_weight(grad, xs, weight, coef, style_sq, out_shape):
    images, chans = xs.shape[0], xs.shape[-1]
    return pl.pallas_call(
        up_weight,
        grid=(images,),
        in_specs=[
            pl.BlockSpec((1, 4, 1, PIX + PAD, chans), lambda image: (image, 0, 0, 0, 0)),
            per_image(xs.shape),
            whole(weight.shape),
            whole(coef.shape),
            whole(style_sq.shape),
        ],
        out_specs=whole(out_shape.shape),
        out_shape=out_shape,
        scratch_shapes=[pltpu.VMEM((9, chans, chans), jnp.float32)],
        compiler_params=params(),
        cost_estimate=cost(18 * images * PIX * chans * chans, 30e6),
        name="up_weight",
    )(grad, xs, weight, coef, style_sq)


def call_up_back(grad, feat, vecs, weight):
    images, _, chans = feat.shape
    out_shape = (
        jax.ShapeDtypeStruct((images, chans, PIX), jnp.float32),
        jax.ShapeDtypeStruct((images, 8, chans), jnp.float32),
    )
    return pl.pallas_call(
        up_back,
        grid=(images,),
        in_specs=[
            per_image(grad.shape),
            per_image(feat.shape),
            per_image(vecs.shape),
            whole(weight.shape),
        ],
        out_specs=[per_image(out_shape[0].shape), per_image(out_shape[1].shape)],
        out_shape=out_shape,
        compiler_params=params(),
        cost_estimate=cost(18 * images * PIX * chans * chans, 30e6),
        name="up_back",
    )(grad, feat, vecs, weight)


def gather_weight(weight, n_img, n_ch):
    block = jnp.transpose(weight.astype(jnp.bfloat16), (1, 2, 0))
    _, rows, cols = block.shape
    every = lax.all_gather(block, BOTH, axis=0, tiled=False)
    every = every.reshape(n_img, n_ch, 9, rows, cols)
    return jnp.transpose(every, (2, 0, 3, 1, 4)).reshape(9, n_img * rows, n_ch * cols)


def scatter_gradient(grad, n_img, n_ch, rows, cols):
    if grad.shape[0] == 1:
        grad = grad.reshape(9, n_img, rows, n_ch, cols)
        grad = jnp.transpose(grad, (1, 3, 0, 2, 4)).reshape(n_img * n_ch, 9, rows, cols)
    block = lax.psum_scatter(grad, BOTH, scatter_dimension=0, tiled=False)
    return jnp.transpose(block.astype(jnp.float32), (2, 0, 1))


def adam_step(weight, mean_old, square_old, gradient, count):
    moment = BETA_ONE * mean_old + (1.0 - BETA_ONE) * gradient
    variance = BETA_TWO * square_old + (1.0 - BETA_TWO) * gradient * gradient
    fix_one = 1.0 - BETA_ONE**count
    fix_two = 1.0 - BETA_TWO**count
    update = moment / fix_one / (jnp.sqrt(variance / fix_two) + ADAM_EPS) + DECAY_RATE * weight
    return (weight - LEARN_RATE * update, moment, variance)


def phases_of_lanes(side):
    column = jnp.arange(side, dtype=jnp.int32)
    target = (column % 2) * (side // 2) + column // 2
    return (target[:, None] == column[None, :]).astype(jnp.float32)


def padded(values, rows):
    short = rows - values.shape[-2]
    shape = values.shape[:-2] + (short, values.shape[-1])
    return jnp.concatenate([values, jnp.zeros(shape, values.dtype)], axis=-2)


def body(
    n_img,
    n_ch,
    features,
    latents,
    skip_rgb,
    noises,
    ada_shift,
    crop_mask,
    critic_mix,
    critic_bias,
    critic_out,
    upsampler,
    upsampler_mean,
    upsampler_square,
    refiner,
    refiner_mean,
    refiner_square,
    affines,
    affines_mean,
    affines_square,
    modbias,
    modbias_mean,
    modbias_square,
    actbias,
    actbias_mean,
    actbias_square,
    rgbmix,
    rgbmix_mean,
    rgbmix_square,
    scalars,
    scalars_mean,
    scalars_square,
):
    local_chans, group_images = features.shape[0], features.shape[1]
    chans = local_chans * n_ch
    rows_own = upsampler.shape[2]
    side = 2 * RES
    share = max(1, n_ch // group_images)
    images = group_images * share // n_ch
    ch_index = lax.axis_index("ch")
    img_index = lax.axis_index("img")
    first = (ch_index // share) * images
    col_start = ch_index * local_chans

    def mine(values, axis):
        return lax.dynamic_slice_in_dim(values, first, images, axis)

    def my_chans(values, axis):
        return lax.dynamic_slice_in_dim(values, col_start, local_chans, axis)

    up_full = gather_weight(upsampler, n_img, n_ch)
    ref_full = gather_weight(refiner, n_img, n_ch)
    aff_full = lax.all_gather(
        lax.all_gather(affines.astype(jnp.bfloat16), "ch", axis=2, tiled=True), "img", axis=1, tiled=True
    )
    small = lax.all_gather(
        jnp.concatenate([modbias, actbias, rgbmix], axis=0), "ch", axis=1, tiled=True
    )
    lat_all = lax.all_gather(latents, "img", axis=0, tiled=True)
    style_gain = latents.shape[1] ** (-0.5)
    lat_own = mine(latents, 0)
    styles = [
        jnp.dot(lat_own, aff_full[number], preferred_element_type=jnp.float32) * style_gain
        + small[number][None, :]
        for number in range(3)
    ]
    vecs = padded(
        jnp.concatenate(
            [jnp.stack(styles, axis=1), jnp.broadcast_to(small[None, 3:5], (images, 2, chans))], axis=1
        ),
        8,
    )
    rgb_low = padded(small[5:8] * C ** (-0.5), 16).astype(jnp.bfloat16)
    if share == 1:
        feat = lax.all_to_all(features, "ch", split_axis=1, concat_axis=0, tiled=True)
    else:
        feat = mine(lax.all_gather(features, "ch", axis=0, tiled=True), 1)
    feat = jnp.transpose(feat, (1, 2, 0))
    noise = jnp.dot(
        mine(noises, 1).reshape(2 * images * side, side), phases_of_lanes(side), precision=PRECISE
    )
    noise = jnp.transpose(noise.reshape(2, images, RES, 2, 2, RES), (1, 0, 3, 4, 2, 5))
    noise = padded(noise.reshape(images, 2, 2, 2, PIX), 8)
    order = jnp.arange(side, dtype=jnp.int32)
    order = 2 * (order % RES) + order // RES
    shifts = mine(ada_shift, 0)
    picks = [
        (((order[None, :] + shifts[:, axis : axis + 1]) % side)[:, :, None] == jnp.arange(side)).astype(
            jnp.bfloat16
        )
        for axis in (0, 1)
    ]
    mask = mine(crop_mask, 0).reshape(images, side, side).astype(jnp.bfloat16)
    mask = jnp.einsum("byz,bzx->byx", picks[0], mask, preferred_element_type=jnp.bfloat16)
    mask = jnp.einsum("byx,bwx->byw", mask, picks[1], preferred_element_type=jnp.float32) / share
    mask = jnp.transpose(mask.reshape(images, 2, RES, 2, RES), (0, 1, 3, 2, 4))
    mask = padded(mask.reshape(images, 2, 2, PIX), 8)
    base = padded(
        jnp.transpose(mine(skip_rgb, 1), (1, 0, 2)) + scalars[2:5][None, :, None], 8
    )
    critic = jnp.concatenate(
        [critic_mix, critic_bias[:, None], critic_out[:, None], jnp.zeros((critic_mix.shape[0], 3))], axis=1
    )

    raw_one, maps, xs, up_square, demod_one = call_up_forward(scalars, feat, vecs, noise, up_full)
    grad_two, sums_two, color_sums = call_flat_forward(
        scalars, maps, vecs, noise, base, mask, critic, rgb_low, ref_full
    )
    blocks = n_img * n_ch
    out_shape = gradient_shape(chans, blocks, rows_own, local_chans, jnp.float32)
    ref_grad = call_flat_weight(
        grad_two,
        maps,
        ref_full,
        padded(sums_two[:, 4], 8),
        padded(styles[1] * styles[1], 8),
        out_shape,
    )
    ref_grad = scatter_gradient(ref_grad, n_img, n_ch, rows_own, local_chans)
    grad_one, sums_one = call_flat_back(scalars, grad_two, raw_one, vecs, demod_one, noise, ref_full)
    demod_row = demod_one[:, 0]
    coef_one = -0.5 * demod_row * demod_row * demod_row * sums_one[:, 1]
    up_grad = call_up_weight(
        grad_one, xs, up_full, padded(coef_one, 8), padded(styles[0] * styles[0], 8), out_shape
    )
    up_grad = scatter_gradient(up_grad, n_img, n_ch, rows_own, local_chans)
    feat_grad, feat_sums = call_up_back(grad_one, feat, vecs, up_full)
    style_demod_one = 2.0 * styles[0] * jnp.dot(coef_one, up_square, precision=PRECISE)

    if share == 1:
        feat_grad = lax.all_to_all(
            feat_grad.astype(jnp.bfloat16), "ch", split_axis=1, concat_axis=0, tiled=True
        ).astype(jnp.float32)
    else:
        feat_grad = lax.all_gather(feat_grad, "ch", axis=0, tiled=True)[::share] * share
        feat_grad = my_chans(feat_grad, 1)
    features_grad = jnp.transpose(feat_grad, (1, 0, 2))

    style_grads = jnp.stack(
        [feat_sums[:, 0] + style_demod_one, sums_one[:, 0] + sums_two[:, 5], sums_two[:, 0]]
    )
    style_grads = style_grads.astype(jnp.bfloat16).astype(jnp.float32)
    color_sum = jnp.sum(color_sums[:, 0:3], axis=(0, 2))
    scalar_row = jnp.concatenate(
        [
            jnp.sum(sums_one[:, 3])[None],
            jnp.sum(sums_two[:, 3])[None],
            color_sum,
            jnp.zeros((chans - 5,), jnp.float32),
        ]
    )
    packed = jnp.concatenate(
        [
            style_grads.reshape(3 * images, chans),
            jnp.sum(sums_one[:, 2], axis=0)[None],
            jnp.sum(sums_two[:, 2], axis=0)[None],
            jnp.sum(sums_two[:, 8:11], axis=0) * C ** (-0.5),
            scalar_row[None],
        ],
        axis=0,
    )
    every = lax.all_gather(packed, BOTH, axis=0, tiled=False)
    scalar_grad = jnp.sum(every[:, 3 * images + 5, 0:5], axis=0)
    every = my_chans(every, 2)
    small_grad = jnp.sum(every[:, 3 * images : 3 * images + 5], axis=0)
    style_all = every[:, : 3 * images].reshape(n_img, n_ch // share, share, 3, images, local_chans)
    style_all = jnp.transpose(jnp.sum(style_all, axis=2), (2, 0, 1, 3, 4))
    style_all = style_all.reshape(3, n_img * group_images, local_chans)
    lat_rows = affines.shape[1]
    lat_cols = lax.dynamic_slice_in_dim(lat_all, img_index * lat_rows, lat_rows, 1)
    aff_grad = (
        jnp.einsum(
            "bj,kbi->kji", lat_cols, style_all.astype(jnp.bfloat16), preferred_element_type=jnp.float32
        )
        * style_gain
    )
    mod_grad = jnp.sum(style_all, axis=1)

    count = float(STEP)
    up_new = adam_step(upsampler, upsampler_mean, upsampler_square, up_grad, count)
    ref_new = adam_step(refiner, refiner_mean, refiner_square, ref_grad, count)
    aff_new = adam_step(affines, affines_mean, affines_square, aff_grad, count)
    mod_new = adam_step(modbias, modbias_mean, modbias_square, mod_grad, count)
    act_new = adam_step(actbias, actbias_mean, actbias_square, small_grad[0:2], count)
    rgb_new = adam_step(rgbmix, rgbmix_mean, rgbmix_square, small_grad[2:5], count)
    scal_new = adam_step(scalars, scalars_mean, scalars_square, scalar_grad, count)
    return (
        (features_grad,) + up_new + ref_new + aff_new + mod_new + act_new + rgb_new + scal_new
    )


def solution(mesh):
    conv = P("ch", None, "img")
    aff = P(None, "img", "ch")
    row = P(None, "ch")
    images = P(None, "img", None)
    return jax.shard_map(
        functools.partial(body, mesh.shape["img"], mesh.shape["ch"]),
        mesh=mesh,
        in_specs=(P("ch", "img", None), P("img", None), images, images, P("img", None), P("img", None))
        + (P(),) * 3
        + (conv,) * 6
        + (aff,) * 3
        + (row,) * 9
        + (P(),) * 3,
        out_specs=(P("ch", "img", None),) + (conv,) * 6 + (aff,) * 3 + (row,) * 9 + (P(),) * 3,
        check_vma=False,
    )
```

time: 2350 us -> 739 us (0.31)
  waiting for transfers between devices: 1110 us -> 185 us
  matrix products: 651 us -> 7.04 us
  local copies, waits for them, and re-layouts: 379 us -> 84.7 us
  Pallas kernels: 0 us -> 259 us
  other arithmetic: 92.8 us -> 20.8 us
  blocking collectives: 84.5 us -> 148 us
    reduce_scatter x4 -> x2, waiting for transfers between devices: 806 us -> 86.6 us  [scatter_gradient(): block = lax.psum_scatter(grad, BOTH, scatter_dimension=0, tiled=False)]
    dot_general x72 -> x7, matrix products: 651 us -> 7.04 us  [the longest x3 3.66 us: body(): jnp.dot(lat_own, aff_full[number], preferred_element_type=jnp.float32)]
    pallas_call x0 -> x6, Pallas kernels: none -> 259 us  [the longest x1 77.2 us: call_flat_forward(): pl.pallas_call(flat_forward, grid=(images, 2), in_specs=[SMEM, per_image(...]
    all_gather x4 -> x3, waiting for transfers between devices: 276 us -> 98.1 us  [the longest x2 98.1 us: gather_weight(): every = lax.all_gather(block, BOTH, axis=0, tiled=False)]
    slice x22 -> x5, local copies, waits for them, and re-layouts: 168 us -> 0.81 us  [the longest x1 0.72 us: body(): every[:, :3 * images]]
    all_gather x3 -> x4, blocking collectives: 35.5 us -> 148 us  [the longest x1 99.2 us: body(): every = lax.all_gather(packed, BOTH, axis=0, tiled=False)]
    psum x2 -> x0, blocking collectives: 49 us -> none  [the longest x1 40 us: body(): lax.psum((small_padded, scalar_local), ('img', 'ch'))]
    transpose x1 -> x2, local copies, waits for them, and re-layouts: 55.1 us -> 11.2 us  [body(): features_grad = jnp.transpose(feat_grad, (1, 0, 2))]
  transfers between devices with their start and end apart: 10 -> 7, of which waited for: 8 -> 3; matrix products, arithmetic and copies ran while one was open for 23% -> 11% of each run, Pallas kernels for 0% -> 5%
where the time goes in v1:
time: 739 us; the launch traced here: 728 us
  Pallas kernels  259 us (35%)
  waiting for transfers between devices  185 us (25%)
  blocking collectives  148 us (20%)
  local copies, waits for them, and re-layouts  84.7 us (11%)
  other arithmetic  20.8 us (3%)
  between operations  14.7 us (2%)
  starting transfers between devices  8.05 us (1%)
    all_gather x1, blocking collectives, body(): every = lax.all_gather(packed, BOTH, axis=0, tiled=False)  99.2 us
    all_gather x2, waiting for transfers between devices, gather_weight(): every = lax.all_gather(block, BOTH, axis=0, tiled=False)  98.1 us
    reduce_scatter x2, waiting for transfers between devices, scatter_gradient(): block = lax.psum_scatter(grad, BOTH, scatter_dimension=0, tiled=False)  86.6 us
    pallas_call x1, Pallas kernels, call_flat_forward(): pl.pallas_call(flat_forward, grid=(images, 2), in_specs=[SMEM, per_image(...  77.2 us
    pallas_call x1, Pallas kernels, call_flat_back(): pl.pallas_call(flat_back, grid=(images, 2), in_specs=[SMEM, per_image(gra...  60.6 us
    pallas_call x1, Pallas kernels, call_flat_weight(): pl.pallas_call(flat_weight, grid=(images, 2), in_specs=[pl.BlockSpec((1,...  52 us
    pallas_call x1, Pallas kernels, call_up_forward(): pl.pallas_call(up_forward, grid=(images,), in_specs=[SMEM, per_image(feat...  31.1 us
    reshape x2, local copies, waits for them, and re-layouts, gather_weight(): every = every.reshape(n_img, n_ch, 9, rows, cols)  28.1 us
  transfers between devices with their start and end apart: 7, of which 3 were waited for; matrix products, arithmetic and copies ran while one was open for 11% of the time, Pallas kernels for 5%

profile of v1, /device:TPU:0, one launch (start us, length us, event | category | flops | bytes accessed | tf_op | source)
XLA Modules:
  0.0 727.8 jit_solution(11447154117060334437)
XLA Ops:
  8.2 5.8 all_gather.30
  17.5 3.6 copy.97
  21.1 3.9 all-to-all-start
  26.3 23.1 %all_gather.32 = f32[8,512]{1,0:T(8,128)S(1)} all-gather(f32[8,256]{1,0:T(8,128)S(1)} %pad_maximum_fusion), channel_id=1, replica_groups=mesh['img'=16,'ch'=2] {'ch'}, dimensions={1}, use_global_device_ids=true | all-gather | bytes 24576 | tf_op jit(solution)/shard_map/all_gather | solution.py:664
  53.6 3.8 copy.98
  57.4 4.4 all_to_all.23
  66.8 54.9 %all-gather.11.cloned.1.call-done = bf16[288,32,256]{2,1,0:T(8,128)(2,1)} async-done(((bf16[9,32,256]{2,1,0:T(8,128)(2,1)}), bf16[288,32,256]{2,1,0:T(8,128)(2,1)}) %all-gather.11.cloned.1.call-update) | async-done | bytes 4718608 | tf_op jit(solution)/shard_map/all_gather | solution.py:574
  121.7 14.1 %copy.140 = bf16[16,2,9,32,256]{4,1,3,0,2:T(2,128)(2,1)} copy(bf16[16,2,9,32,256]{4,3,2,1,0:T(8,128)(2,1)} %bitcast.139) | data formatting | bytes 9437184 | tf_op jit(solution)/shard_map/reshape | solution.py:575
  135.8 8.7 %reshape.251.weight_ref = bf16[9,512,512]{2,1,0:T(8,128)(2,1)} reshape(bf16[9,16,32,2,256]{4,3,2,1,0:T(2,128)(2,1)} %bitcast.134) | data formatting | bytes 9437184 | tf_op jit(solution)/shard_map/reshape | solution.py:576
  144.6 43.2 %all-gather.13.cloned.1.call-done = bf16[288,32,256]{2,1,0:T(8,128)(2,1)} async-done(((bf16[9,32,256]{2,1,0:T(8,128)(2,1)}), bf16[288,32,256]{2,1,0:T(8,128)(2,1)}) %all-gather.13.cloned.1.call-update) | async-done | bytes 4718608 | tf_op jit(solution)/shard_map/all_gather | solution.py:574
  187.7 14.0 %copy.139 = bf16[16,2,9,32,256]{4,1,3,0,2:T(2,128)(2,1)} copy(bf16[16,2,9,32,256]{4,3,2,1,0:T(8,128)(2,1)} %bitcast.140) | data formatting | bytes 9437184 | tf_op jit(solution)/shard_map/reshape | solution.py:575
  201.8 8.6 %reshape.255.weight_ref = bf16[9,512,512]{2,1,0:T(8,128)(2,1)} reshape(bf16[9,16,32,2,256]{4,3,2,1,0:T(2,128)(2,1)} %bitcast.135) | data formatting | bytes 9437184 | tf_op jit(solution)/shard_map/reshape | solution.py:576
  210.3 31.1 %up_forward.1 = (f32[2,4,1024,512]{3,2,1,0:T(8,128)}, bf16[2,4,2,1088,512]{4,3,2,1,0:T(8,128)(2,1)}, bf16[2,2,1056,512]{3,2,1,0:T(8,128)(2,1)}, f32[512,512]{1,0:T(8,128)}, f32[2,8,512]{2,1,0:T(8,128)}) custom-call(f32[5]{0:T(128)} %scal_ref.5, bf16[2,1024,512]{2,1,0:T(8,128)(2,1)} %bitcast.142, f32[2,8,512]{2,1,0:T(8,128)} %concatenate.40.vec_ref, ...), custom_call_target="tpu_custom_call" | custom-call | flops 9663676416 | bytes 60000000 | tf_op jit(solution)/shard_map/up_forward/pallas_call | solution.py:415
  241.4 77.2 %flat_forward.1 = (bf16[2,4,2,1088,512]{4,3,2,1,0:T(8,128)(2,1)}, f32[2,16,512]{2,1,0:T(8,128)}, f32[2,8,128]{2,1,0:T(8,128)}) custom-call(f32[5]{0:T(128)} %scal_ref.5, bf16[2,4,2,1088,512]{4,3,2,1,0:T(8,128)(2,1)} %get-tuple-element.34.map_ref, f32[2,8,512]{2,1,0:T(8,128)} %concatenate.40.vec_ref, f32[2,2,2,8,1024]{4,3,2,1,0:T(8,128)} %concatenate.41.noise_ref, ...), custom_call_target="tpu_custom_call" | custom-call | flops 38654705664 | bytes 60000000 | tf_op jit(solution)/shard_map/flat_forward/pallas_call | solution.py:446
  318.6 60.6 %flat_back.1 = (bf16[2,4,2,1056,512]{4,3,2,1,0:T(8,128)(2,1)}, f32[2,8,512]{2,1,0:T(8,128)}) custom-call(f32[5]{0:T(128)} %scal_ref.5, bf16[2,4,2,1088,512]{4,3,2,1,0:T(8,128)(2,1)} %get-tuple-element.35.grad_ref, f32[2,4,1024,512]{3,2,1,0:T(8,128)} %get-tuple-element.36.raw_ref, f32[2,8,512]{2,1,0:T(8,128)} %concatenate.40.vec_ref, ...), custom_call_target="tpu_custom_call" | custom-call | flops 38654705664 | bytes 60000000 | tf_op jit(solution)/shard_map/flat_back/pallas_call | solution.py:507
  380.7 52.0 %flat_weight.1 = f32[32,9,32,256]{3,2,1,0:T(8,128)} custom-call(bf16[2,4,2,1088,512]{4,3,2,1,0:T(8,128)(2,1)} %get-tuple-element.35.grad_ref, bf16[2,4,2,1088,512]{4,3,2,1,0:T(8,128)(2,1)} %get-tuple-element.34.map_ref, bf16[9,512,512]{2,1,0:T(8,128)(2,1)} %reshape.255.weight_ref, f32[8,512]{1,0:T(8,128)} %concatenate.48.coef_ref, ...), custom_call_target="tpu_custom_call" | custom-call | flops 38654705664 | bytes 50000000 | tf_op jit(solution)/shard_map/flat_weight/pallas_call | solution.py:482
  434.2 21.1 %up_weight.1 = f32[32,9,32,256]{3,2,1,0:T(8,128)} custom-call(bf16[2,4,2,1056,512]{4,3,2,1,0:T(8,128)(2,1)} %get-tuple-element.38.grad_ref, bf16[2,2,1056,512]{3,2,1,0:T(8,128)(2,1)} %get-tuple-element.40.xs_ref, bf16[9,512,512]{2,1,0:T(8,128)(2,1)} %reshape.251.weight_ref, f32[8,512]{1,0:T(8,128)} %concatenate.46.coef_ref, f32[8,512]{1,0:T(8,128)} %concatenate.47.style_ref), custom_call_target="tpu_custom_call" | custom-call | flops 9663676416 | bytes 30000000 | tf_op jit(solution)/shard_map/up_weight/pallas_call | solution.py:529
  456.0 20.1 %all-gather.4 = bf16[16,4,512]{2,1,0:T(4,128)(2,1)S(1)} all-gather(bf16[1,4,512]{2,1,0:T(4,128)(2,1)S(1)} %bitcast.149), channel_id=1, replica_groups=mesh['img'=16,'ch'=2] {'img'}, dimensions={0}, use_global_device_ids=true | all-gather | bytes 69632 | tf_op jit(solution)/shard_map/all_gather | solution.py:667
  476.1 17.4 %up_back.1 = (f32[2,512,1024]{2,1,0:T(8,128)}, f32[2,8,512]{2,1,0:T(8,128)}) custom-call(bf16[2,4,2,1056,512]{4,3,2,1,0:T(8,128)(2,1)} %get-tuple-element.38.grad_ref, bf16[2,1024,512]{2,1,0:T(8,128)(2,1)} %bitcast.143, f32[2,8,512]{2,1,0:T(8,128)} %concatenate.40.vec_ref, bf16[9,512,512]{2,1,0:T(8,128)(2,1)} %reshape.251.weight_ref), custom_call_target="tpu_custom_call" | custom-call | flops 9663676416 | bytes 30000000 | tf_op jit(solution)/shard_map/up_back/pallas_call | solution.py:554
  501.0 3.9 all-to-all-start.1
  508.6 99.2 %all-gather.3 = f32[32,12,512]{2,1,0:T(8,128)S(1)} all-gather(f32[1,12,512]{2,1,0:T(8,128)S(1)} %bitcast.147), channel_id=4, replica_groups=mesh['img'=16,'ch'=2] {'img','ch'}, dimensions={0}, use_global_device_ids=true | all-gather | bytes 811008 | tf_op jit(solution)/shard_map/all_gather | solution.py:770
  618.9 4.5 copy.110
  623.4 6.8 reshape.257
  632.2 86.6 %reduce-scatter.3.cloned.1.call-done = f32[1,9,32,256]{3,2,1,0:T(8,128)} async-done(((f32[32,9,32,256]{3,2,1,0:T(8,128)}), f32[1,9,32,256]{3,2,1,0:T(8,128)}) %reduce-scatter.3.cloned.1.call-update) | async-done | bytes 294928 | tf_op jit(solution)/shard_map/reduce_scatter | solution.py:583
  (164 shorter events, 44.4 us)
Async XLA Ops:
  7.2 54.6 %all-gather.9.cloned.1.call-start = ((), (), s32[]{:S(2)}) async-start(), calls=%async_computation.4 | async-start | bytes 1671168 | tf_op jit(solution)/shard_map/all_gather | solution.py:661
  14.0 107.8 %all-gather.11.cloned.1.call-start = ((), (), s32[]{:S(2)}) async-start(), calls=%async_computation.7 | async-start | bytes 4866048 | tf_op jit(solution)/shard_map/all_gather | solution.py:574
  15.7 172.0 %all-gather.13.cloned.1.call-start = ((), (), s32[]{:S(2)}) async-start(), calls=%async_computation.8 | async-start | bytes 4866048 | tf_op jit(solution)/shard_map/all_gather | solution.py:574
  21.0 30.3 %copy-start.27 = (f32[5]{0:T(128)S(1)}, f32[5]{0:T(128)}, u32[]{:S(2)}) copy-start(f32[5]{0:T(128)} %scal_ref.5) | copy-start | bytes 64
  21.0 30.3 %copy-start.20 = (f32[3,4,1024]{2,1,0:T(4,128)S(1)}, f32[3,4,1024]{2,1,0:T(4,128)}, u32[]{:S(2)}) copy-start(f32[3,4,1024]{2,1,0:T(4,128)} %param.32) | copy-start | bytes 147460
  21.0 31.1 %copy-start.25 = (f32[64,3]{0,1:T(4,128)S(1)}, f32[64,3]{0,1:T(4,128)}, u32[]{:S(2)}) copy-start(f32[64,3]{0,1:T(4,128)} %param.36) | copy-start | bytes 2308
  21.0 31.1 %copy-start.31 = (f32[64]{0:T(128)S(1)}, f32[64]{0:T(128)}, u32[]{:S(2)}) copy-start(f32[64]{0:T(128)} %param.38) | copy-start | bytes 772
  21.0 31.1 %copy-start.32 = (f32[64]{0:T(128)S(1)}, f32[64]{0:T(128)}, u32[]{:S(2)}) copy-start(f32[64]{0:T(128)} %param.37) | copy-start | bytes 772
  21.1 32.5 %all-to-all-start = ((bf16[256,4,1024]{2,0,1:T(8,128)(2,1)}), bf16[256,4,1024]{2,0,1:T(8,128)(2,1)S(1)}, u32[]{:S(2)}, u32[]{:S(2)}) async-start(bf16[256,4,1024]{2,0,1:T(8,128)(2,1)} %copy.97), calls=%async_computation | async-start | bytes 4194304 | tf_op jit(solution)/shard_map/all_to_all | solution.py:683
  25.0 605.2 %reduce-scatter.5.cloned.1.call-start = ((), (), s32[]{:S(2)}) async-start(), calls=%async_computation.6 | async-start | bytes 9732096 | tf_op jit(solution)/shard_map/reduce_scatter | solution.py:583
  318.6 61.4 %copy-start.9 = (f32[2,16,512]{2,1,0:T(8,128)S(1)}, f32[2,16,512]{2,1,0:T(8,128)}, u32[]{:S(2)}) copy-start(f32[2,16,512]{2,1,0:T(8,128)} %get-tuple-element.42) | copy-start | bytes 196612
  432.8 286.1 %reduce-scatter.3.cloned.1.call-start = ((), (), s32[]{:S(2)}) async-start(), calls=%async_computation.5 | async-start | bytes 9732096 | tf_op jit(solution)/shard_map/reduce_scatter | solution.py:583
  497.5 110.3 %copy-start.28 = (f32[5]{0:T(128)S(1)}, f32[5]{0:T(128)}, u32[]{:S(2)}) copy-start(f32[5]{0:T(128)} %scal_ref.5) | copy-start | bytes 64
  497.5 110.3 %copy-start.29 = (f32[5]{0:T(128)S(1)}, f32[5]{0:T(128)}, u32[]{:S(2)}) copy-start(f32[5]{0:T(128)} %param.58) | copy-start | bytes 64
  497.6 110.3 %copy-start.30 = (f32[5]{0:T(128)S(1)}, f32[5]{0:T(128)}, u32[]{:S(2)}) copy-start(f32[5]{0:T(128)} %param.59) | copy-start | bytes 64
  501.0 110.4 %copy-start.22 = (f32[2,256]{1,0:T(2,128)S(1)}, f32[2,256]{1,0:T(2,128)}, u32[]{:S(2)}) copy-start(f32[2,256]{1,0:T(2,128)} %param.51) | copy-start | bytes 6148
  501.0 111.7 %copy-start.17 = (f32[3,256]{1,0:T(4,128)S(1)}, f32[3,256]{1,0:T(4,128)}, u32[]{:S(2)}) copy-start(f32[3,256]{1,0:T(4,128)} %param.48) | copy-start | bytes 9220
  501.0 111.7 %copy-start.23 = (f32[3,256]{1,0:T(4,128)S(1)}, f32[3,256]{1,0:T(4,128)}, u32[]{:S(2)}) copy-start(f32[3,256]{1,0:T(4,128)} %param.49) | copy-start | bytes 9220
  501.0 113.0 %copy-start.19 = (f32[3,256]{1,0:T(4,128)S(1)}, f32[3,256]{1,0:T(4,128)}, u32[]{:S(2)}) copy-start(f32[3,256]{1,0:T(4,128)} %param.54) | copy-start | bytes 9220
  501.0 116.4 %all-to-all-start.1 = ((bf16[2,512,1024]{2,0,1:T(2,128)(2,1)}), bf16[2,512,1024]{2,0,1:T(2,128)(2,1)S(1)}, u32[]{:S(2)}, u32[]{:S(2)}) async-start(bf16[2,512,1024]{2,0,1:T(2,128)(2,1)} %copy.109), calls=%async_computation.1 | async-start | bytes 4194304 | tf_op jit(solution)/shard_map/all_to_all | solution.py:739
  618.9 102.0 %copy-start.1 = (f32[2,4,4096]{2,1,0:T(4,128)S(1)}, f32[2,4,4096]{2,1,0:T(4,128)}, u32[]{:S(2)}) copy-start(f32[2,4,4096]{2,1,0:T(4,128)} %param.33) | copy-start | bytes 393220
  623.4 95.5 %copy-start.3 = (f32[256,9,32]{0,2,1:T(8,128)S(1)}, f32[256,9,32]{0,2,1:T(8,128)}, u32[]{:S(2)}) copy-start(f32[256,9,32]{0,2,1:T(8,128)} %param.39) | copy-start | bytes 884740
  623.4 95.5 %copy-start.7 = (f32[256,9,32]{0,2,1:T(8,128)S(1)}, f32[256,9,32]{0,2,1:T(8,128)}, u32[]{:S(2)}) copy-start(f32[256,9,32]{0,2,1:T(8,128)} %param.40) | copy-start | bytes 884740
  623.4 95.5 %copy-start.8 = (f32[256,9,32]{0,2,1:T(8,128)S(1)}, f32[256,9,32]{0,2,1:T(8,128)}, u32[]{:S(2)}) copy-start(f32[256,9,32]{0,2,1:T(8,128)} %param.41) | copy-start | bytes 884740
  (16 other events, 137.5 us)
Sparse Core Ops, SparseCore 0:
  14.1 41.5 all-gather.8
  59.2 62.5 all-gather.10
  125.2 62.4 all-gather.12
  432.9 145.1 reduce-scatter.4
  584.9 133.9 reduce-scatter.2

commit v2 on v1

v2 whole, which is shorter than its diff:
```python
import functools

import jax
import jax.numpy as jnp
from jax import lax
from jax.experimental import pallas as pl
from jax.experimental.pallas import tpu as pltpu
from jax.sharding import PartitionSpec as P

C = 512
RES = 32
STEP = 10

PRECISE = lax.Precision.HIGHEST
ROOT_TWO = 1.4142135623730951
BETA_ONE = 0.9
BETA_TWO = 0.99
LEARN_RATE = 0.3
DECAY_RATE = 0.01
ADAM_EPS = 1e-08
DEMOD_EPS = 1e-08
VMEM_LIMIT = 60 * 2**20
BOTH = ("img", "ch")

PAD = RES
PIX = RES * RES
ROWS = PIX + 2 * PAD
TILE = 256
TAPS = tuple((3 * (dy + 1) + dx + 1, dy, dx) for dy in (-1, 0, 1) for dx in (-1, 0, 1))
UP_TAPS = (
    ((4, 0, 0),),
    ((3, 0, 0), (5, 1, 0)),
    ((1, 0, 0), (7, 0, 1)),
    ((0, 0, 0), (2, 1, 0), (6, 0, 1), (8, 1, 1)),
)
NT = (((1,), (1,)), ((), ()))
TN = (((0,), (0,)), ((), ()))
NN = (((1,), (0,)), ((), ()))


def params(**more):
    return pltpu.CompilerParams(vmem_limit_bytes=VMEM_LIMIT, **more)


def mul(left, right, dims):
    return lax.dot_general(left, right, dims, preferred_element_type=jnp.float32)


def exact(left, right, dims):
    return lax.dot_general(
        left, right, dims, precision=PRECISE, preferred_element_type=jnp.float32
    )


def softplus(values):
    return jnp.maximum(values, 0.0) + jnp.log(1.0 + jnp.exp(-jnp.abs(values)))


def activate(values):
    return (0.2 * ROOT_TWO) * values + (0.8 * ROOT_TWO) * softplus(values)


def slope(values):
    return 0.6 + 0.4 * jnp.tanh(0.5 * values)


def side_copy(values, odd):
    column = lax.broadcasted_iota(jnp.int32, values.shape, 0) & (RES - 1)
    if odd:
        return jnp.where(column == 0, 0.0, pltpu.roll(values, 1, 0))
    return jnp.where(column == RES - 1, 0.0, pltpu.roll(values, values.shape[0] - 1, 0))


def column_sums(values):
    return jnp.sum(values, axis=0, keepdims=True)


def square_sums(weight_ref, out_ref):
    chans = weight_ref.shape[1]
    for start in range(0, chans, 64):
        total = None
        for tap in range(9):
            part = weight_ref[tap, pl.ds(start, 64), :].astype(jnp.float32)
            total = part * part if total is None else total + part * part
        out_ref[pl.ds(start, 64), :] = total


def demod_of(style, squares):
    spread = jnp.broadcast_to(style * style, (8, style.shape[1]))
    return lax.rsqrt(exact(spread, squares, NT)[0:1] + DEMOD_EPS)


def phase_taps(row_parity, col_parity, sign):
    found = []
    for tap, dy, dx in TAPS:
        across = col_parity + sign * dx + 2
        down = row_parity + sign * dy + 2
        copy = 1 if across in (1, 4) else 0
        phase = 2 * (down & 1) + (across & 1)
        first = PAD * (down >> 1)
        found.append((tap, phase, copy, first))
    return found


def tap_rows(ref, phase, copy, first, offset, count):
    start = first + offset
    if not isinstance(start, int):
        start = pl.multiple_of(start, PAD)
    return ref[0, phase, copy, pl.ds(start, count), :]


def write_map(ref, phase, rows_at, values, odd):
    ref[0, phase, 0, rows_at, :] = values.astype(jnp.bfloat16)
    ref[0, phase, 1, rows_at, :] = side_copy(values, odd).astype(jnp.bfloat16)


def clear_pads(ref, phase, both=True):
    empty = jnp.zeros((PAD, ref.shape[-1]), jnp.bfloat16)
    for copy in (0, 1):
        ref[0, phase, copy, 0:PAD, :] = empty
        if both:
            ref[0, phase, copy, PAD + PIX :, :] = empty


def place_of(device, shape, layout):
    across, rows, cols = layout
    row = pl.multiple_of((device // across) * rows, rows)
    col = pl.multiple_of((device % across) * cols, cols)
    return pl.ds(row, rows), pl.ds(col, cols)


def weight_copies(me, pieces, piece_refs, layout, target, sems):
    if layout is None:
        return [pltpu.make_async_copy(piece_refs[0], target, sems.at[0])]
    copies = []
    for offsets, ref in zip(pieces, piece_refs):
        for index, offset in enumerate(offsets):
            rows, cols = place_of(me ^ offset, target.shape, layout)
            copies.append(
                pltpu.make_async_copy(
                    ref.at[index], target.at[:, rows, cols], sems.at[len(copies)]
                )
            )
    return copies


def first_step():
    return (pl.program_id(0) == 0) & (pl.program_id(1) == 0)


def last_step():
    return (pl.program_id(0) == pl.num_programs(0) - 1) & (
        pl.program_id(1) == pl.num_programs(1) - 1
    )


def add_rows(total_ref, row, values):
    total_ref[row] += jnp.sum(values.reshape(values.shape[0] // 8, 8, values.shape[1]), axis=0)


def up_forward(pieces, layout, gain, waits, *refs):
    count, refs = len(pieces), refs[waits:]
    me_ref, scal_ref, feat_ref, lat_ref, small_ref, noise_ref = refs[:6]
    piece_refs = refs[6 : 6 + count]
    raw_ref, map_ref, xs_ref, sq_ref, vec_ref, whole_ref = refs[6 + count : 12 + count]
    raw_buf, weight_ref, sems, out_sem = refs[12 + count :]
    turn = pl.program_id(1)
    chans = feat_ref.shape[-1]

    @pl.when(first_step())
    def _():
        copies = weight_copies(me_ref[0], pieces, piece_refs, layout, weight_ref, sems)
        for copy in copies:
            copy.start()
        for copy in copies:
            copy.wait()
        pltpu.make_async_copy(weight_ref.at[0:9], whole_ref, out_sem).start()
        square_sums(weight_ref, sq_ref)

    @pl.when(turn == 0)
    def _():
        latent = jnp.broadcast_to(lat_ref[0], (16, lat_ref.shape[2]))
        for number in range(3):
            style = mul(latent, weight_ref[9 + number], NN)[0:1] * gain
            vec_ref[0, number : number + 1, :] = style + small_ref[number : number + 1, :]
        vec_ref[0, 3:5, :] = small_ref[3:5, :]
        vec_ref[0, 5:6, :] = demod_of(vec_ref[0, 0:1, :], sq_ref[...])
        vec_ref[0, 6:8, :] = jnp.zeros((2, chans), jnp.float32)
        style_one = vec_ref[0, 0:1, :]
        for start in range(0, PIX, TILE):
            values = feat_ref[0, pl.ds(start, TILE), :].astype(jnp.float32) * style_one
            xs_ref[0, 0, pl.ds(start, TILE), :] = values.astype(jnp.bfloat16)
            xs_ref[0, 1, pl.ds(start, TILE), :] = side_copy(values, False).astype(jnp.bfloat16)
        xs_ref[0, 0, PIX:, :] = jnp.zeros((PAD, chans), jnp.bfloat16)
        xs_ref[0, 1, PIX:, :] = jnp.zeros((PAD, chans), jnp.bfloat16)

    def one_phase(phase):
        style_two = vec_ref[0, 1:2, :]
        bias = vec_ref[0, 3:4, :]
        demod = vec_ref[0, 5:6, :]
        noise_cols = jnp.transpose(noise_ref[0, 0, phase // 2]) * scal_ref[0]
        clear_pads(map_ref, 0)

        def convolve(index):
            start = index * TILE
            raw = None
            for tap, col_step, row_step in UP_TAPS[phase]:
                part = mul(
                    xs_ref[0, col_step, pl.ds(start + PAD * row_step, TILE), :], weight_ref[tap], NT
                )
                raw = part if raw is None else raw + part
            raw_buf[index % 2] = raw

        def finish(index):
            start = index * TILE
            raw = raw_buf[index % 2]
            raw_ref[0, 0, pl.ds(start, TILE), :] = raw
            noise = noise_cols[start : start + TILE, phase % 2 : phase % 2 + 1]
            pre = raw * demod + noise + bias
            write_map(
                map_ref, 0, pl.ds(PAD + start, TILE), activate(pre) * style_two, phase % 2 == 1
            )

        steps = PIX // TILE
        for index in range(steps + 1):
            if index < steps:
                convolve(index)
            if index > 0:
                finish(index - 1)

    for phase in range(4):
        pl.when(turn == phase)(functools.partial(one_phase, phase))

    @pl.when(last_step())
    def _():
        pltpu.make_async_copy(weight_ref.at[0:9], whole_ref, out_sem).wait()


def flat_forward(pieces, layout, *refs):
    count = len(pieces)
    me_ref, scal_ref, map_ref, vec_ref, noise_ref, base_ref, mask_ref, critic_ref, rgb_ref = refs[:9]
    piece_refs = refs[9 : 9 + count]
    grad_ref, sums_ref, color_ref, whole_ref = refs[9 + count : 13 + count]
    raw_buf, sq_buf, total_buf, weight_ref, sems, out_sem = refs[13 + count :]
    row_parity = pl.program_id(1)

    @pl.when(first_step())
    def _():
        copies = weight_copies(me_ref[0], pieces, piece_refs, layout, weight_ref, sems)
        for copy in copies:
            copy.start()
        for copy in copies:
            copy.wait()
        pltpu.make_async_copy(weight_ref, whole_ref, out_sem).start()
        square_sums(weight_ref, sq_buf)

    @pl.when(row_parity == 0)
    def _():
        vec_row = demod_of(vec_ref[0, 1:2, :], sq_buf[...])
        sums_ref[0] = jnp.zeros(sums_ref.shape[1:], jnp.float32)
        sums_ref[0, 6:7, :] = vec_row
        color_ref[...] = jnp.zeros_like(color_ref)
        total_buf[...] = jnp.zeros_like(total_buf)

    style_two = vec_ref[0, 1:2, :]
    style_three = vec_ref[0, 2:3, :]
    bias = vec_ref[0, 4:5, :]
    demod = sums_ref[0, 6:7, :]
    noise_all = jnp.transpose(noise_ref[0, 0, 0])
    strength = scal_ref[1]
    rgb = rgb_ref[...]
    mix = critic_ref[...]
    out = mix[:, 4:5]
    taps = [phase_taps(row_parity, col_parity, 1) for col_parity in (0, 1)]
    per_phase = PIX // TILE
    clear_pads(grad_ref, 0)
    clear_pads(grad_ref, 1)

    def convolve(index):
        start = (index % per_phase) * TILE
        raw = None
        for tap, phase, copy, first in taps[index // per_phase]:
            part = mul(tap_rows(map_ref, phase, copy, first, start, TILE), weight_ref[tap], NT)
            raw = part if raw is None else raw + part
        raw_buf[index % 2] = raw

    def finish(index):
        col_parity = index // per_phase
        start = (index % per_phase) * TILE
        raw = raw_buf[index % 2]
        noise = noise_all[start : start + TILE, col_parity : col_parity + 1]
        pre = raw * demod + strength * noise + bias
        act = activate(pre)
        modulated = (act * style_three).astype(jnp.bfloat16)
        colors = mul(rgb, modulated, NT)[0:8] + base_ref[0, :, start : start + TILE]
        hidden = mix[:, 3:4]
        for color in range(3):
            hidden = hidden + mix[:, color : color + 1] * colors[color : color + 1]
        unit = 0.2 * hidden + 0.8 * softplus(hidden)
        logits = column_sums(out * unit)
        mask = mask_ref[0, 0, col_parity : col_parity + 1, start : start + TILE]
        grad_logits = -mask / (1.0 + jnp.exp(logits))
        grad_hidden = out * grad_logits * slope(hidden)
        grad_colors = jnp.concatenate(
            [column_sums(mix[:, color : color + 1] * grad_hidden) for color in range(3)]
            + [jnp.zeros((5, TILE), jnp.float32)],
            axis=0,
        )
        for lane in range(0, TILE, 128):
            color_ref[0] += grad_colors[:, lane : lane + 128]
        grad_low = jnp.concatenate(
            [grad_colors, jnp.zeros((8, TILE), jnp.float32)], axis=0
        ).astype(jnp.bfloat16)
        grad_map = mul(grad_low, rgb, TN)
        grad_pre = grad_map * (style_three * ROOT_TWO) * slope(pre)
        write_map(grad_ref, col_parity, pl.ds(PAD + start, TILE), grad_pre * demod, col_parity == 1)
        add_rows(total_buf, 0, grad_map * act)
        add_rows(total_buf, 1, grad_pre * raw)
        add_rows(total_buf, 2, grad_pre)
        add_rows(total_buf, 3, grad_pre * noise)
        total_buf[4] += mul(grad_low, modulated, NN)[0:8]

    steps = 2 * per_phase
    for index in range(steps + 1):
        if index < steps:
            convolve(index)
        if index > 0:
            finish(index - 1)

    @pl.when(row_parity == 1)
    def _():
        for row in range(4):
            sums_ref[0, row : row + 1, :] = column_sums(total_buf[row])
        sums_ref[0, 8:16, :] = total_buf[4]
        coef = -0.5 * demod * demod * demod * sums_ref[0, 1:2, :]
        sums_ref[0, 4:5, :] = coef
        back = exact(jnp.broadcast_to(coef, (8, coef.shape[1])), sq_buf[...], NN)[0:1]
        sums_ref[0, 5:6, :] = 2.0 * style_two * back

    @pl.when(last_step())
    def _():
        pltpu.make_async_copy(weight_ref, whole_ref, out_sem).wait()


def outer(lefts, rights):
    short = -len(lefts) % 8
    empty = [jnp.zeros((short, lefts[0].shape[1]), jnp.float32)] if short else []
    return exact(jnp.concatenate(lefts + empty), jnp.concatenate(rights + empty), TN)


def spread_out(me, order, layout, acc_ref, weight_ref, squares, out_refs):
    for tap in range(acc_ref.shape[0]):
        acc_ref[tap] += 2.0 * weight_ref[tap].astype(jnp.float32) * squares
    if layout is None:
        out_refs[0][0] = acc_ref[...].astype(out_refs[0].dtype)
        return
    for offsets, out_ref in zip(order, out_refs):
        for index, offset in enumerate(offsets):
            rows, cols = place_of(me ^ offset, acc_ref.shape, layout)
            out_ref[index] = acc_ref[:, rows, cols].astype(out_ref.dtype)


def flat_weight(order, layout, part, waits, *refs):
    me_ref, grad_ref, map_ref, weight_ref, vec_ref, sums_ref = refs[waits : waits + 6]
    out_refs, token_ref, acc_ref = refs[waits + 6 : -2], refs[-2], refs[-1]
    row_parity = pl.program_id(1)
    first = pl.multiple_of(PAD * ((row_parity + part + 1) >> 1), PAD)

    @pl.when(first_step())
    def _():
        acc_ref[...] = jnp.zeros_like(acc_ref)

    for col_parity in (0, 1):
        grad = grad_ref[0, col_parity, 0, PAD : PAD + PIX, :]
        for tap in range(3):
            across_to = col_parity + tap + 1
            copy = 1 if across_to in (1, 4) else 0
            acc_ref[tap] += mul(grad, map_ref[0, across_to & 1, copy, pl.ds(first, PIX), :], TN)

    @pl.when(last_step())
    def _():
        images = range(vec_ref.shape[0])
        squares = outer(
            [sums_ref[image, 4:5, :] for image in images],
            [vec_ref[image, 1:2, :] * vec_ref[image, 1:2, :] for image in images],
        )
        spread_out(me_ref[0], order, layout, acc_ref, weight_ref, squares, out_refs)
        token_ref[...] = squares[0:8, 0:128]


def coef_of(vec_ref, sums_ref, image):
    demod = vec_ref[image, 5:6, :]
    return -0.5 * demod * demod * demod * sums_ref[image, 1:2, :]


def up_weight(order, layout, *refs):
    me_ref, grad_ref, xs_ref, weight_ref, vec_ref, sums_ref = refs[:6]
    out_refs, acc_ref = refs[6:-1], refs[-1]

    @pl.when(pl.program_id(0) == 0)
    def _():
        acc_ref[...] = jnp.zeros_like(acc_ref)

    for phase in range(4):
        grad = grad_ref[0, phase, 0, PAD:, :]
        for tap, col_step, row_step in UP_TAPS[phase]:
            acc_ref[tap] += mul(grad, xs_ref[0, col_step, pl.ds(PAD * row_step, PIX), :], TN)

    @pl.when(pl.program_id(0) == pl.num_programs(0) - 1)
    def _():
        images = range(vec_ref.shape[0])
        squares = outer(
            [coef_of(vec_ref, sums_ref, image) for image in images],
            [vec_ref[image, 0:1, :] * vec_ref[image, 0:1, :] for image in images],
        )
        spread_out(me_ref[0], order, layout, acc_ref, weight_ref, squares, out_refs)


def flat_back(
    scal_ref, grad_ref, raw_ref, vec_ref, noise_ref, weight_ref, out_ref, sums_ref, back_buf, total_buf
):
    row_parity = pl.program_id(1)

    @pl.when(row_parity == 0)
    def _():
        total_buf[...] = jnp.zeros_like(total_buf)

    style_two = vec_ref[0, 1:2, :]
    bias = vec_ref[0, 3:4, :]
    demod = vec_ref[0, 5:6, :]
    noise_all = jnp.transpose(noise_ref[0, 0, 0])
    strength = scal_ref[0]
    taps = [phase_taps(row_parity, col_parity, -1) for col_parity in (0, 1)]
    per_phase = PIX // TILE
    clear_pads(out_ref, 0, False)
    clear_pads(out_ref, 1, False)

    def convolve(index):
        start = (index % per_phase) * TILE
        total = None
        for tap, phase, copy, first in taps[index // per_phase]:
            part = mul(tap_rows(grad_ref, phase, copy, first, start, TILE), weight_ref[tap], NN)
            total = part if total is None else total + part
        back_buf[index % 2] = total

    def finish(index):
        col_parity = index // per_phase
        start = (index % per_phase) * TILE
        grad_map = back_buf[index % 2]
        raw = raw_ref[0, col_parity, pl.ds(start, TILE), :]
        noise = noise_all[start : start + TILE, col_parity : col_parity + 1]
        pre = raw * demod + strength * noise + bias
        grad_pre = grad_map * (style_two * ROOT_TWO) * slope(pre)
        write_map(out_ref, col_parity, pl.ds(PAD + start, TILE), grad_pre * demod, col_parity == 1)
        add_rows(total_buf, 0, grad_map * activate(pre))
        add_rows(total_buf, 1, grad_pre * raw)
        add_rows(total_buf, 2, grad_pre)
        add_rows(total_buf, 3, grad_pre * noise)

    steps = 2 * per_phase
    for index in range(steps + 1):
        if index < steps:
            convolve(index)
        if index > 0:
            finish(index - 1)

    @pl.when(row_parity == 1)
    def _():
        for row in range(4):
            sums_ref[0, row : row + 1, :] = column_sums(total_buf[row])
        sums_ref[0, 4:8, :] = jnp.zeros((4, sums_ref.shape[2]), jnp.float32)


def up_back(_, grad_ref, feat_ref, vec_ref, sums_in_ref, sq_ref, weight_ref, out_ref, sums_ref):
    style_one = vec_ref[0, 0:1, :]
    total = None
    for start in range(0, PIX, TILE):
        grad_map = None
        for phase in range(4):
            for tap, col_step, row_step in UP_TAPS[phase]:
                rows = grad_ref[0, phase, col_step, pl.ds(PAD + start - PAD * row_step, TILE), :]
                part = mul(rows, weight_ref[tap], NN)
                grad_map = part if grad_map is None else grad_map + part
        found = column_sums(grad_map * feat_ref[0, pl.ds(start, TILE), :].astype(jnp.float32))
        total = found if total is None else total + found
        out_ref[0, :, pl.ds(start, TILE)] = jnp.transpose(grad_map * style_one)
    coef = coef_of(vec_ref, sums_in_ref, 0)
    back = exact(jnp.broadcast_to(coef, (8, coef.shape[1])), sq_ref[...], NN)
    sums_ref[0] = total + 2.0 * style_one * back


def small_finish(images, layout, gain, count, *refs):
    across_count, rows_own, cols_own = layout
    me_ref, row_refs = refs[0], refs[1 : 1 + count]
    old_refs = refs[1 + count : 16 + count]
    new_refs = refs[16 + count : 31 + count]
    total_ref, cross_ref = refs[31 + count :]
    device = me_ref[0]
    rows, cols = place_of(device, None, layout)
    each = total_ref.shape[0]
    stacked = jnp.concatenate([ref[...] for ref in row_refs])
    chans = stacked.shape[1]
    total_ref[...] = jnp.sum(stacked.reshape(stacked.shape[0] // each, each, chans), axis=0)
    row = lax.broadcasted_iota(jnp.int32, stacked.shape, 0) & (each - 1)
    latent_row = 3 * images
    latents = jnp.where((row >= latent_row) & (row < latent_row + images), stacked, 0.0)
    latents = latents.astype(jnp.bfloat16)

    def step(number, gradient, old=None, new=None):
        found = adam_step(*[ref[...] if old is None else ref[old] for ref in old_refs[3 * number : 3 * number + 3]], gradient, float(STEP))
        for ref, value in zip(new_refs[3 * number : 3 * number + 3], found):
            if old is None:
                ref[...] = value
            else:
                ref[old] = value

    for number in range(3):
        moved = pltpu.roll(stacked, latent_row - number * images, 0) if number < 3 else stacked
        cross_ref[...] = mul(latents, moved.astype(jnp.bfloat16), TN)
        step(0, cross_ref[rows, cols] * gain, number)
    mine = total_ref[:, cols]
    step(
        1,
        jnp.concatenate(
            [
                jnp.sum(mine[number * images : (number + 1) * images], axis=0, keepdims=True)
                for number in range(3)
            ]
        ),
    )
    first = 4 * images
    step(2, mine[first : first + 2])
    step(3, mine[first + 2 : first + 5])
    step(4, total_ref[first + 5 : first + 6, 0:5])


def call_small_finish(me, row_arrays, olds, images, layout, gain):
    chans = row_arrays[0].shape[1]
    olds = [old if old.ndim > 1 else old[None] for old in olds]
    out_shape = tuple(jax.ShapeDtypeStruct(old.shape, old.dtype) for old in olds)
    found = pl.pallas_call(
        functools.partial(small_finish, images, layout, gain, len(row_arrays)),
        in_specs=[SMEM] + [pl.BlockSpec(memory_space=pltpu.VMEM)] * (len(row_arrays) + len(olds)),
        out_specs=[pl.BlockSpec(memory_space=pltpu.VMEM)] * len(olds),
        out_shape=out_shape,
        scratch_shapes=[
            pltpu.VMEM((row_arrays[0].shape[0], chans), jnp.float32),
            pltpu.VMEM((chans, chans), jnp.float32),
        ],
        compiler_params=params(),
        name="small_finish",
    )(me, *row_arrays, *olds)
    return tuple(found[:-3]) + tuple(value[0] for value in found[-3:])


def whole(shape):
    zeros = (0,) * len(shape)
    return pl.BlockSpec(shape, lambda *ids: zeros)


def per_image(shape):
    zeros = (0,) * (len(shape) - 1)
    return pl.BlockSpec((1,) + tuple(shape[1:]), lambda image, *ids: (image,) + zeros)


SMEM = pl.BlockSpec(memory_space=pltpu.SMEM)
ANY = pl.BlockSpec(memory_space=pl.ANY)


def cost(flops, moved):
    return pl.CostEstimate(flops=int(flops), bytes_accessed=int(moved), transcendentals=0)


def half_phases(shape, count=2):
    zeros = (0,) * (len(shape) - 2)
    return pl.BlockSpec(
        (1, count) + tuple(shape[2:]), lambda image, turn: (image, turn) + zeros
    )


def noise_spec(layer):
    return pl.BlockSpec((1, 1, 1, 8, PIX), lambda image, parity: (image, layer, parity, 0, 0))


def offsets_of(weight):
    return tuple(offsets for offsets, _ in weight[0])


def call_up_forward(after, me, scalars, feat, lat, small, noise, weight):
    images, _, chans = feat.shape
    arrays, layout = [array for _, array in weight[0]], weight[1]
    out_shape = (
        jax.ShapeDtypeStruct((images, 4, PIX, chans), jnp.float32),
        jax.ShapeDtypeStruct((images, 4, 2, ROWS, chans), jnp.bfloat16),
        jax.ShapeDtypeStruct((images, 2, PIX + PAD, chans), jnp.bfloat16),
        jax.ShapeDtypeStruct((chans, chans), jnp.float32),
        jax.ShapeDtypeStruct((images, 8, chans), jnp.float32),
        jax.ShapeDtypeStruct((9, chans, chans), jnp.bfloat16),
    )
    return pl.pallas_call(
        functools.partial(
            up_forward, offsets_of(weight), layout, lat.shape[2] ** (-0.5), len(after)
        ),
        grid=(images, 4),
        in_specs=[ANY] * len(after)
        + [
            SMEM,
            SMEM,
            per_image(feat.shape),
            per_image(lat.shape),
            whole(small.shape),
            pl.BlockSpec((1, 1, 2, 8, PIX), lambda image, turn: (image, 0, 0, 0, 0)),
        ]
        + [ANY] * len(arrays),
        out_specs=[
            half_phases(out_shape[0].shape, 1),
            half_phases(out_shape[1].shape, 1),
            per_image(out_shape[2].shape),
            whole(out_shape[3].shape),
            per_image(out_shape[4].shape),
            ANY,
        ],
        out_shape=out_shape,
        scratch_shapes=[
            pltpu.VMEM((2, TILE, chans), jnp.float32),
            pltpu.VMEM((12, chans, chans), jnp.bfloat16),
            pltpu.SemaphoreType.DMA((sum(len(o) for o in offsets_of(weight)),)),
            pltpu.SemaphoreType.DMA,
        ],
        compiler_params=params(),
        cost_estimate=cost(18 * images * PIX * chans * chans, 60e6),
        name="up_forward",
    )(*after, me, scalars, feat, lat, small, noise, *arrays)


def call_flat_forward(me, scalars, maps, vecs, noise, base, mask, critic, rgb, weight):
    images, chans = maps.shape[0], maps.shape[-1]
    arrays, layout = [array for _, array in weight[0]], weight[1]
    out_shape = (
        jax.ShapeDtypeStruct((images, 4, 2, ROWS, chans), jnp.bfloat16),
        jax.ShapeDtypeStruct((images, 16, chans), jnp.float32),
        jax.ShapeDtypeStruct((images, 8, 128), jnp.float32),
        jax.ShapeDtypeStruct((9, chans, chans), jnp.bfloat16),
    )
    return pl.pallas_call(
        functools.partial(flat_forward, offsets_of(weight), layout),
        grid=(images, 2),
        in_specs=[
            SMEM,
            SMEM,
            per_image(maps.shape),
            per_image(vecs.shape),
            noise_spec(1),
            per_image(base.shape),
            pl.BlockSpec((1, 1, 8, PIX), lambda image, parity: (image, parity, 0, 0)),
            whole(critic.shape),
            whole(rgb.shape),
        ]
        + [ANY] * len(arrays),
        out_specs=[
            half_phases(out_shape[0].shape),
            per_image(out_shape[1].shape),
            per_image(out_shape[2].shape),
            ANY,
        ],
        out_shape=out_shape,
        scratch_shapes=[
            pltpu.VMEM((2, TILE, chans), jnp.float32),
            pltpu.VMEM((chans, chans), jnp.float32),
            pltpu.VMEM((5, 8, chans), jnp.float32),
            pltpu.VMEM((9, chans, chans), jnp.bfloat16),
            pltpu.SemaphoreType.DMA((sum(len(o) for o in offsets_of(weight)),)),
            pltpu.SemaphoreType.DMA,
        ],
        compiler_params=params(),
        cost_estimate=cost(72 * images * PIX * chans * chans, 60e6),
        name="flat_forward",
    )(me, scalars, maps, vecs, noise, base, mask, critic, rgb, *arrays)


def gradient_shapes(chans, taps, layout):
    if layout is None:
        return (jax.ShapeDtypeStruct((1, taps, chans, chans), jnp.float32),)
    _, rows, cols = layout
    shape = (16, taps, rows, cols)
    return (jax.ShapeDtypeStruct(shape, jnp.float32), jax.ShapeDtypeStruct(shape, jnp.bfloat16))


def call_flat_weight(me, after, grad, maps, weight, vecs, sums, order, layout, part):
    images, chans = maps.shape[0], maps.shape[-1]
    out_shape = gradient_shapes(chans, 3, layout) + (jax.ShapeDtypeStruct((8, 128), jnp.float32),)
    return pl.pallas_call(
        functools.partial(flat_weight, order, layout, part, len(after)),
        grid=(images, 2),
        in_specs=[ANY] * len(after)
        + [
            SMEM,
            pl.BlockSpec((1, 2, 1, ROWS, chans), lambda image, parity: (image, parity, 0, 0, 0)),
            pl.BlockSpec(
                (1, 2, 2, ROWS, chans), lambda image, parity: (image, (parity + part + 1) & 1, 0, 0, 0)
            ),
            pl.BlockSpec((3, chans, chans), lambda image, parity: (part, 0, 0)),
            whole(vecs.shape),
            whole(sums.shape),
        ],
        out_specs=[whole(s.shape) for s in out_shape],
        out_shape=out_shape,
        scratch_shapes=[pltpu.VMEM((3, chans, chans), jnp.float32)],
        compiler_params=params(),
        cost_estimate=cost(24 * images * PIX * chans * chans, 40e6),
        name="flat_weight_" + str(part),
    )(*after, me, grad, maps, weight, vecs, sums)


def call_flat_back(scalars, grad, raw, vecs, noise, weight):
    images, chans = grad.shape[0], grad.shape[-1]
    out_shape = (
        jax.ShapeDtypeStruct((images, 4, 2, PIX + PAD, chans), jnp.bfloat16),
        jax.ShapeDtypeStruct((images, 8, chans), jnp.float32),
    )
    return pl.pallas_call(
        flat_back,
        grid=(images, 2),
        in_specs=[
            SMEM,
            per_image(grad.shape),
            half_phases(raw.shape),
            per_image(vecs.shape),
            noise_spec(0),
            whole(weight.shape),
        ],
        out_specs=[half_phases(out_shape[0].shape), per_image(out_shape[1].shape)],
        out_shape=out_shape,
        scratch_shapes=[
            pltpu.VMEM((2, TILE, chans), jnp.float32),
            pltpu.VMEM((4, 8, chans), jnp.float32),
        ],
        compiler_params=params(),
        cost_estimate=cost(72 * images * PIX * chans * chans, 60e6),
        name="flat_back",
    )(scalars, grad, raw, vecs, noise, weight)


def call_up_weight(me, grad, xs, weight, vecs, sums, order, layout):
    images, chans = xs.shape[0], xs.shape[-1]
    out_shape = gradient_shapes(chans, 9, layout)
    return pl.pallas_call(
        functools.partial(up_weight, order, layout),
        grid=(images,),
        in_specs=[
            SMEM,
            pl.BlockSpec((1, 4, 1, PIX + PAD, chans), lambda image: (image, 0, 0, 0, 0)),
            per_image(xs.shape),
            whole(weight.shape),
            whole(vecs.shape),
            whole(sums.shape),
        ],
        out_specs=[whole(s.shape) for s in out_shape],
        out_shape=out_shape,
        scratch_shapes=[pltpu.VMEM((9, chans, chans), jnp.float32)],
        compiler_params=params(),
        cost_estimate=cost(18 * images * PIX * chans * chans, 30e6),
        name="up_weight",
    )(me, grad, xs, weight, vecs, sums)


def call_up_back(after, grad, feat, vecs, sums, squares, weight):
    images, _, chans = feat.shape
    out_shape = (
        jax.ShapeDtypeStruct((images, chans, PIX), jnp.float32),
        jax.ShapeDtypeStruct((images, 8, chans), jnp.float32),
    )
    return pl.pallas_call(
        up_back,
        grid=(images,),
        in_specs=[
            ANY,
            per_image(grad.shape),
            per_image(feat.shape),
            per_image(vecs.shape),
            per_image(sums.shape),
            whole(squares.shape),
            whole(weight.shape),
        ],
        out_specs=[per_image(out_shape[0].shape), per_image(out_shape[1].shape)],
        out_shape=out_shape,
        compiler_params=params(),
        cost_estimate=cost(18 * images * PIX * chans * chans, 30e6),
        name="up_back",
    )(after, grad, feat, vecs, sums, squares, weight)


BIT_X, BIT_CORE, BIT_Y, BIT_LOW, BIT_HIGH = 1, 2, 4, 8, 16
Z_OFFSETS = ((0, BIT_LOW), (BIT_HIGH, BIT_HIGH + BIT_LOW))


def across(values, bits, devices):
    return lax.ppermute(values, BOTH, [(device, device ^ bits) for device in range(devices)])


def gather_along_z(block, devices):
    move = lambda values, bits: across(values, bits, devices)
    low = jnp.stack([block, move(block, BIT_LOW)])
    return low, jnp.stack([move(block, BIT_HIGH), move(block, BIT_HIGH + BIT_LOW)])


def gather_in_turn(low, high, devices, ahead):
    move = lambda values, bits: across(values, bits, devices)
    high_y, low_y = move(high, BIT_Y), move(low, BIT_Y)
    low_ahead, high_ahead, _ = lax.optimization_barrier((low, high, ahead))
    low_x, high_x = move(low_ahead, BIT_X), move(high_ahead, BIT_X)
    low_xy, high_xy = move(low_x, BIT_Y), move(high_y, BIT_X)
    found = []
    for offsets, arrays in zip(
        Z_OFFSETS, ((low, low_x, low_y, low_xy), (high, high_x, high_y, high_xy))
    ):
        for bits, array in zip((0, BIT_X, BIT_Y, BIT_X + BIT_Y), arrays):
            found.append((tuple(o ^ bits for o in offsets), array))
    return found


def gather_at_once(along, devices):
    found = []
    offsets = Z_OFFSETS[0] + Z_OFFSETS[1]
    for bits in (0, BIT_X + BIT_Y, BIT_X, BIT_Y):
        array = across(along, bits, devices) if bits else along
        found.append((tuple(o ^ bits for o in offsets), array))
    return found


def with_other_core(found, devices):
    return found + [
        (tuple(o ^ BIT_CORE for o in offsets), across(array, BIT_CORE, devices))
        for offsets, array in found
    ]


def tie(values, token):
    return values if token is None else lax.optimization_barrier((values, token))[0]


def gather_rows(rows, devices):
    move = lambda values, bits: across(values, bits, devices)
    token = yield (rows,)
    found = [rows] + tie([move(rows, b) for b in (BIT_LOW, BIT_HIGH, BIT_LOW + BIT_HIGH)], token)
    for bits in (BIT_X, BIT_Y, BIT_CORE):
        joined = jnp.concatenate(found)
        token = yield (joined,)
        found = found + tie([move(joined, bits)], token)
    yield found


def scatter_order():
    kept = []
    for high in (0, 1):
        one, two = (BIT_X, BIT_Y) if high == 0 else (BIT_Y, BIT_X)
        for a in (0, 1):
            for b in (0, 1):
                for low in (0, 1):
                    kept.append(high * BIT_HIGH + low * BIT_LOW + a * one + b * two)
    return tuple(kept), tuple(offset ^ BIT_CORE for offset in kept)


def scatter_blocks(kept, sent, devices):
    low = lambda values: values.astype(jnp.bfloat16)

    def swap(values, bits, token):
        found = tie([across(v, b, devices) for v, b in zip(values, bits)], token)
        return [f.astype(jnp.float32) for f in found]

    token = yield (sent,)
    total = kept + swap((sent,), (BIT_CORE,), token)[0]
    total = total.reshape((2, 2, 2, 2) + kept.shape[1:])
    sends = low(total[0, 1]), low(total[1, 1])
    token = yield sends
    found = swap(sends, (BIT_X, BIT_Y), token)
    halves = total[0, 0] + found[0], total[1, 0] + found[1]
    sends = low(halves[0][1]), low(halves[1][1])
    token = yield sends
    found = swap(sends, (BIT_Y, BIT_X), token)
    halves = halves[0][0] + found[0], halves[1][0] + found[1]
    sends = low(halves[0][1]), low(halves[1][0]), low(halves[1][1])
    token = yield sends
    total = halves[0][0]
    for found in swap(sends, (BIT_LOW, BIT_HIGH, BIT_HIGH + BIT_LOW), token):
        total = total + found
    yield total


def gather_whole(block, n_img, n_ch):
    _, rows, cols = block.shape
    every = lax.all_gather(block, BOTH, axis=0, tiled=False)
    every = every.reshape(n_img, n_ch, -1, rows, cols)
    return jnp.transpose(every, (2, 0, 3, 1, 4)).reshape(-1, n_img * rows, n_ch * cols)


def scatter_whole(grad, n_img, n_ch, rows, cols):
    grad = grad.reshape(-1, n_img, rows, n_ch, cols)
    grad = jnp.transpose(grad, (1, 3, 0, 2, 4)).reshape(n_img * n_ch, -1, rows, cols)
    return lax.psum_scatter(grad, BOTH, scatter_dimension=0, tiled=False)


def adam_step(weight, mean_old, square_old, gradient, count):
    moment = BETA_ONE * mean_old + (1.0 - BETA_ONE) * gradient
    variance = BETA_TWO * square_old + (1.0 - BETA_TWO) * gradient * gradient
    fix_one = 1.0 - BETA_ONE**count
    fix_two = 1.0 - BETA_TWO**count
    update = moment / fix_one / (jnp.sqrt(variance / fix_two) + ADAM_EPS) + DECAY_RATE * weight
    return (weight - LEARN_RATE * update, moment, variance)


def phases_of_lanes(side):
    column = jnp.arange(side, dtype=jnp.int32)
    target = (column % 2) * (side // 2) + column // 2
    return (target[:, None] == column[None, :]).astype(jnp.float32)


def padded(values, rows):
    short = rows - values.shape[-2]
    shape = values.shape[:-2] + (short, values.shape[-1])
    return jnp.concatenate([values, jnp.zeros(shape, values.dtype)], axis=-2)


def body(
    n_img,
    n_ch,
    features,
    latents,
    skip_rgb,
    noises,
    ada_shift,
    crop_mask,
    critic_mix,
    critic_bias,
    critic_out,
    upsampler,
    upsampler_mean,
    upsampler_square,
    refiner,
    refiner_mean,
    refiner_square,
    affines,
    affines_mean,
    affines_square,
    modbias,
    modbias_mean,
    modbias_square,
    actbias,
    actbias_mean,
    actbias_square,
    rgbmix,
    rgbmix_mean,
    rgbmix_square,
    scalars,
    scalars_mean,
    scalars_square,
):
    local_chans, group_images = features.shape[0], features.shape[1]
    chans = local_chans * n_ch
    rows_own = upsampler.shape[2]
    side = 2 * RES
    devices = n_img * n_ch
    by_hand = devices == 32 and n_ch == 2 and group_images % n_ch == 0
    share = max(1, n_ch // group_images)
    images = group_images * share // n_ch
    ch_index = lax.axis_index("ch")
    img_index = lax.axis_index("img")
    me = (img_index * n_ch + ch_index).astype(jnp.int32)[None]
    first = (ch_index // share) * images
    col_start = ch_index * local_chans

    def mine(values, axis):
        return lax.dynamic_slice_in_dim(values, first, images, axis)

    def my_chans(values, axis):
        return lax.dynamic_slice_in_dim(values, col_start, local_chans, axis)

    up_block = jnp.concatenate([jnp.transpose(upsampler, (1, 2, 0)), affines]).astype(jnp.bfloat16)
    ref_block = jnp.transpose(refiner, (1, 2, 0)).astype(jnp.bfloat16)
    small_own = jnp.concatenate([modbias, actbias, rgbmix], axis=0)
    if by_hand:
        layout, order = (n_ch, rows_own, local_chans), scatter_order()
        other = lax.dynamic_slice_in_dim(features, images - first, images, 1)
        other = across(other, BIT_X, devices)
        up_low, up_high = gather_along_z(up_block, devices)
        ref_along = jnp.concatenate(gather_along_z(ref_block, devices))
        up_weight_all = (
            with_other_core(gather_in_turn(up_low, up_high, devices, other), devices), layout
        )
        here = mine(features, 1)
        feat = jnp.where(
            ch_index == 0, jnp.concatenate([here, other]), jnp.concatenate([other, here])
        )
        small_other = across(small_own, BIT_X, devices)
        small = jnp.where(
            ch_index == 0,
            jnp.concatenate([small_own, small_other], axis=1),
            jnp.concatenate([small_other, small_own], axis=1),
        )
        ref_plane = gather_at_once(ref_along, devices)
        ahead = (ref_along,)
    else:
        layout, order, ahead = None, None, ()
        up_weight_all = ([((0,), gather_whole(up_block, n_img, n_ch))], None)
        ref_weight_all = ([((0,), gather_whole(ref_block, n_img, n_ch))], None)
        small = lax.all_gather(small_own, "ch", axis=1, tiled=True)
        feat = mine(lax.all_gather(features, "ch", axis=0, tiled=True), 1)
    feat = jnp.transpose(feat, (1, 2, 0))
    lat_own = mine(latents, 0)
    rgb_low = padded(small[5:8] * C ** (-0.5), 16).astype(jnp.bfloat16)
    noise = jnp.dot(
        mine(noises, 1).reshape(2 * images * side, side), phases_of_lanes(side), precision=PRECISE
    )
    noise = jnp.transpose(noise.reshape(2, images, RES, 2, 2, RES), (1, 0, 3, 4, 2, 5))
    noise = padded(noise.reshape(images, 2, 2, 2, PIX), 8)
    order_in = jnp.arange(side, dtype=jnp.int32)
    order_in = 2 * (order_in % RES) + order_in // RES
    shifts = mine(ada_shift, 0)
    picks = [
        (((order_in[None, :] + shifts[:, axis : axis + 1]) % side)[:, :, None] == jnp.arange(side)).astype(
            jnp.bfloat16
        )
        for axis in (0, 1)
    ]
    mask = mine(crop_mask, 0).reshape(images, side, side).astype(jnp.bfloat16)
    mask = jnp.einsum("byz,bzx->byx", picks[0], mask, preferred_element_type=jnp.bfloat16)
    mask = jnp.einsum("byx,bwx->byw", mask, picks[1], preferred_element_type=jnp.float32) / share
    mask = jnp.transpose(mask.reshape(images, 2, RES, 2, RES), (0, 1, 3, 2, 4))
    mask = padded(mask.reshape(images, 2, 2, PIX), 8)
    base = padded(
        jnp.transpose(mine(skip_rgb, 1), (1, 0, 2)) + scalars[2:5][None, :, None], 8
    )
    critic = jnp.concatenate(
        [critic_mix, critic_bias[:, None], critic_out[:, None], jnp.zeros((critic_mix.shape[0], 3))], axis=1
    )

    raw_one, maps, xs, up_square, vecs, up_full = call_up_forward(
        ahead, me, scalars, feat, lat_own[:, None, :], small, noise, up_weight_all
    )
    if by_hand:
        arrays, _ = lax.optimization_barrier(([array for _, array in ref_plane], vecs))
        ref_plane = [(offsets, array) for (offsets, _), array in zip(ref_plane, arrays)]
        ref_weight_all = (with_other_core(ref_plane, devices), layout)
    grad_two, sums_two, color_sums, ref_full = call_flat_forward(
        me, scalars, maps, vecs, noise, base, mask, critic, rgb_low, ref_weight_all
    )
    grad_one, sums_one = call_flat_back(scalars, grad_two, raw_one, vecs, noise, ref_full)
    up_parts = call_up_weight(me, grad_one, xs, up_full, vecs, sums_one, order, layout)
    feat_grad, feat_sums = call_up_back(
        up_parts[0], grad_one, feat, vecs, sums_one, up_square, up_full
    )

    style_grads = jnp.stack(
        [feat_sums[:, 0], sums_one[:, 0] + sums_two[:, 5], sums_two[:, 0]]
    )
    style_grads = style_grads.astype(jnp.bfloat16).astype(jnp.float32)
    color_sum = jnp.sum(color_sums[:, 0:3], axis=(0, 2))
    scalar_row = jnp.concatenate(
        [
            jnp.sum(sums_one[:, 3])[None],
            jnp.sum(sums_two[:, 3])[None],
            color_sum,
            jnp.zeros((chans - 5,), jnp.float32),
        ]
    )
    packed = jnp.concatenate(
        [
            style_grads.reshape(3 * images, chans),
            lat_own.astype(jnp.float32),
            jnp.sum(sums_one[:, 2], axis=0)[None],
            jnp.sum(sums_two[:, 2], axis=0)[None],
            jnp.sum(sums_two[:, 8:11], axis=0) * C ** (-0.5),
            scalar_row[None],
        ],
        axis=0,
    )
    packed = padded(packed, 16)

    def ref_part(after, part):
        return call_flat_weight(
            me, after, grad_two, maps, ref_full, vecs, sums_two, order, layout, part
        )

    if by_hand:
        other = lax.dynamic_slice_in_dim(feat_grad, local_chans - col_start, local_chans, 1)
        other = other.astype(jnp.bfloat16)
        row_steps = gather_rows(packed, devices)
        up_steps = scatter_blocks(*up_parts, devices)
        next(up_steps)
        kept, sent, token = ref_part(up_steps.send(feat_sums) + next(row_steps) + (other,), 0)
        other = tie(across(other, BIT_X, devices), token)
        steps = [scatter_blocks(kept, sent, devices)]
        next(steps[0])
        kept, sent, token = ref_part(up_steps.send(token) + row_steps.send(token) + (token,), 1)
        steps.append(scatter_blocks(kept, sent, devices))
        next(steps[1])
        kept, sent, token = ref_part(
            up_steps.send(token) + steps[0].send(token) + row_steps.send(token) + (token,), 2
        )
        steps.append(scatter_blocks(kept, sent, devices))
        up_grad = up_steps.send(token)
        row_steps.send(token)
        all_rows = next(row_steps)
        steps[0].send(token)
        next(steps[1])
        ref_grad = jnp.concatenate([list(step)[-1] for step in steps])
    else:
        up_grad = scatter_whole(up_parts[0], n_img, n_ch, rows_own, local_chans)
        ref_grad = jnp.concatenate(
            [
                scatter_whole(ref_part((), part)[0], n_img, n_ch, rows_own, local_chans)
                for part in range(3)
            ]
        )
    up_grad = jnp.transpose(up_grad, (2, 0, 1))
    ref_grad = jnp.transpose(ref_grad, (2, 0, 1))

    if by_hand:
        kept = my_chans(feat_grad, 1)
        other = other.astype(jnp.float32)
        feat_grad = jnp.where(
            ch_index == 0, jnp.concatenate([kept, other]), jnp.concatenate([other, kept])
        )
    else:
        feat_grad = lax.all_gather(feat_grad, "ch", axis=0, tiled=True)[::share] * share
        feat_grad = my_chans(feat_grad, 1)
    features_grad = jnp.transpose(feat_grad, (1, 0, 2))

    count = float(STEP)
    style_gain = latents.shape[1] ** (-0.5)
    small_old = (
        affines,
        affines_mean,
        affines_square,
        modbias,
        modbias_mean,
        modbias_square,
        actbias,
        actbias_mean,
        actbias_square,
        rgbmix,
        rgbmix_mean,
        rgbmix_square,
        scalars,
        scalars_mean,
        scalars_square,
    )
    if by_hand:
        small_new = call_small_finish(
            me, all_rows, small_old, images, layout, style_gain
        )
    else:
        every = lax.all_gather(packed, BOTH, axis=0, tiled=False)
        first_sum = 4 * images
        sums = jnp.sum(every[:, first_sum : first_sum + 6], axis=0)
        lat_rows = affines.shape[1]
        lat_cols = every[:, 3 * images : first_sum]
        lat_cols = lax.dynamic_slice_in_dim(lat_cols, img_index * lat_rows, lat_rows, 2)
        style_all = my_chans(every[:, : 3 * images], 2)
        style_all = style_all.reshape(devices, 3, images, local_chans)
        aff_grad = style_gain * jnp.einsum(
            "dbj,dkbi->kji",
            lat_cols.astype(jnp.bfloat16),
            style_all.astype(jnp.bfloat16),
            preferred_element_type=jnp.float32,
        )
        small_grad = my_chans(sums[0:5], 1)
        small_new = ()
        for number, gradient in enumerate(
            (aff_grad, jnp.sum(style_all, axis=(0, 2)), small_grad[0:2], small_grad[2:5], sums[5, 0:5])
        ):
            small_new += adam_step(*small_old[3 * number : 3 * number + 3], gradient, count)

    up_new = adam_step(upsampler, upsampler_mean, upsampler_square, up_grad, count)
    ref_new = adam_step(refiner, refiner_mean, refiner_square, ref_grad, count)
    return (features_grad,) + up_new + ref_new + tuple(small_new)


def solution(mesh):
    conv = P("ch", None, "img")
    aff = P(None, "img", "ch")
    row = P(None, "ch")
    images = P(None, "img", None)
    return jax.shard_map(
        functools.partial(body, mesh.shape["img"], mesh.shape["ch"]),
        mesh=mesh,
        in_specs=(P("ch", "img", None), P("img", None), images, images, P("img", None), P("img", None))
        + (P(),) * 3
        + (conv,) * 6
        + (aff,) * 3
        + (row,) * 9
        + (P(),) * 3,
        out_specs=(P("ch", "img", None),) + (conv,) * 6 + (aff,) * 3 + (row,) * 9 + (P(),) * 3,
        check_vma=False,
    )
```

time: 739 us -> 469 us (0.63)
  blocking collectives: 148 us -> 0 us
  waiting for transfers between devices: 185 us -> 49.2 us
  starting transfers between devices: 8.05 us -> 66.2 us
  local copies, waits for them, and re-layouts: 84.7 us -> 42.8 us
  between operations: 14.7 us -> 2.3 us
  other arithmetic: 20.8 us -> 32.8 us
  Pallas kernels: 259 us -> 269 us
    all_gather x4 -> x0, blocking collectives: 148 us -> none  [the longest x1 99.2 us: body(): every = lax.all_gather(packed, BOTH, axis=0, tiled=False)]
    all_gather x3 -> x0, waiting for transfers between devices: 98.1 us -> none  [the longest x2 98.1 us: gather_weight(): every = lax.all_gather(block, BOTH, axis=0, tiled=False)]
    reduce_scatter x2 -> x0, waiting for transfers between devices: 86.6 us -> none  [scatter_gradient(): block = lax.psum_scatter(grad, BOTH, scatter_dimension=0, tiled=False)]
    ppermute x0 -> x68, starting transfers between devices: none -> 66.2 us  [across(): lax.ppermute(values, BOTH, [(device, device ^ bits) for device in range(d...]
    ppermute x0 -> x68, waiting for transfers between devices: none -> 49.2 us  [across(): lax.ppermute(values, BOTH, [(device, device ^ bits) for device in range(d...]
    reshape x4 -> x0, local copies, waits for them, and re-layouts: 45.4 us -> none  [the longest x2 28.1 us: gather_weight(): every = every.reshape(n_img, n_ch, 9, rows, cols)]
    add x1 -> x15, other arithmetic: 0.01 us -> 12.7 us  [the longest x4 7.48 us: scatter_blocks(): total = kept + swap((sent,), (BIT_CORE,), token)[0]]
    transpose x2 -> x0, local copies, waits for them, and re-layouts: 11.2 us -> none  [body(): features_grad = jnp.transpose(feat_grad, (1, 0, 2))]
  transfers between devices with their start and end apart: 7 -> 68, of which waited for: 3 -> 21; matrix products, arithmetic and copies ran while one was open for 11% -> 15% of each run, Pallas kernels for 5% -> 24%
where the time goes in v2:
time: 469 us; the launch traced here: 463 us
  Pallas kernels  269 us (57%)
  starting transfers between devices  66.2 us (14%)
  waiting for transfers between devices  49.2 us (10%)
  local copies, waits for them, and re-layouts  42.8 us (9%)
  other arithmetic  32.8 us (7%)
    pallas_call x1, Pallas kernels, call_flat_forward(): pl.pallas_call(functools.partial(flat_forward, offsets_of(weight), layout...  74.4 us
    ppermute x68, starting transfers between devices, across(): lax.ppermute(values, BOTH, [(device, device ^ bits) for device in range(d...  66.2 us
    pallas_call x3, Pallas kernels, call_flat_weight(): pl.pallas_call(functools.partial(flat_weight, order, layout, part, len(af...  61.9 us
    pallas_call x1, Pallas kernels, call_flat_back(): pl.pallas_call(flat_back, grid=(images, 2), in_specs=[SMEM, per_image(gra...  60.9 us
    ppermute x68, waiting for transfers between devices, across(): lax.ppermute(values, BOTH, [(device, device ^ bits) for device in range(d...  49.2 us
    pallas_call x1, Pallas kernels, call_up_forward(): pl.pallas_call(functools.partial(up_forward, offsets_of(weight), layout,...  29.8 us
    pallas_call x1, Pallas kernels, call_up_weight(): pl.pallas_call(functools.partial(up_weight, order, layout), grid=(images,...  20.8 us
    pallas_call x1, Pallas kernels, call_up_back(): pl.pallas_call(up_back, grid=(images,), in_specs=[ANY, per_image(grad.sha...  18.2 us
  transfers between devices with their start and end apart: 68, of which 21 were waited for; matrix products, arithmetic and copies ran while one was open for 15% of the time, Pallas kernels for 24%

profile of v2, /device:TPU:0, one launch (start us, length us, event | category | flops | bytes accessed | tf_op | source)
XLA Modules:
  0.0 463.1 jit_solution(6984571027074261397)
XLA Ops:
  2.6 4.1 collective-permute-start.6
  8.3 4.4 constant_dynamic-slice_fusion.6
  27.2 12.3 %collective-permute-done.3 = bf16[256,2,1024]{0,2,1:T(8,128)(2,1)S(1)} collective-permute-done((bf16[256,2,1024]{0,2,1:T(8,128)(2,1)}, bf16[256,2,1024]{0,2,1:T(8,128)(2,1)S(1)}, u32[]{:S(2)}, u32[]{:S(2)}) %collective-permute-start.3) | collective-permute-done | bytes 1048608 | tf_op jit(solution)/shard_map/ppermute | solution.py:798
  42.7 2.6 collective-permute-start.2
  45.4 5.1 %collective-permute-done.2 = bf16[9,32,256]{2,1,0:T(8,128)(2,1)} collective-permute-done((bf16[9,32,256]{2,1,0:T(8,128)(2,1)}, bf16[9,32,256]{2,1,0:T(8,128)(2,1)}, u32[]{:S(2)}, u32[]{:S(2)}) %collective-permute-start.2) | collective-permute-done | bytes 147488 | tf_op jit(solution)/shard_map/ppermute | solution.py:798
  59.8 2.9 collective-permute-done.13.refs_14_
  63.3 7.5 %collective-permute-done.11.refs_12_ = bf16[2,12,32,256]{3,2,1,0:T(8,128)(2,1)} collective-permute-done((bf16[2,12,32,256]{3,2,1,0:T(8,128)(2,1)}, bf16[2,12,32,256]{3,2,1,0:T(8,128)(2,1)}, u32[]{:S(2)}, u32[]{:S(2)}) %collective-permute-start.11) | collective-permute-done | bytes 393248 | tf_op jit(solution)/shard_map/ppermute | solution.py:798
  80.8 29.8 %up_forward.1 = (f32[2,4,1024,512]{3,2,1,0:T(8,128)}, bf16[2,4,2,1088,512]{4,3,2,1,0:T(8,128)(2,1)}, bf16[2,2,1056,512]{3,2,1,0:T(8,128)(2,1)}, f32[512,512]{1,0...) custom-call(bf16[4,9,32,256]{3,2,1,0:T(8,128)(2,1)} %copy-done.16, s32[1]{0:T(128)} %bitcast.refs_1_.refs_0_.refs_4_.refs_7_, ...), custom_call_target="tpu_custom_call" | custom-call | flops 9663676416 | bytes 60000000 | tf_op jit(solution)/shard_map/up_forward/pallas_call | solution.py:600
  115.4 74.4 %flat_forward.1 = (bf16[2,4,2,1088,512]{4,3,2,1,0:T(8,128)(2,1)}, f32[2,16,512]{2,1,0:T(8,128)}, f32[2,8,128]{2,1,0:T(8,128)}, bf16[9,512,512]{2,1,0:T(8,128)(2,1)}) custom-call(s32[1]{0:T(128)} %bitcast.refs_1_.refs_0_.refs_4_.refs_7_, f32[5]{0:T(128)} %scal_ref.1, bf16[2,4,2,1088,512]{4,3,2,1,0:T(8,128)(2,1)} %get-tuple-element.87.refs_2_.refs_6_.refs_9_, ...), custom_call_target="tpu_custom_call" | custom-call | flops 38654705664 | bytes 60000000 | tf_op jit(solution)/shard_map/flat_forward/pallas_call | solution.py:645
  189.8 60.9 %flat_back.1 = (bf16[2,4,2,1056,512]{4,3,2,1,0:T(8,128)(2,1)}, f32[2,8,512]{2,1,0:T(8,128)}) custom-call(f32[5]{0:T(128)} %scal_ref.1, bf16[2,4,2,1088,512]{4,3,2,1,0:T(8,128)(2,1)} %get-tuple-element.93.grad_ref.refs_5_.refs_8_, f32[2,4,1024,512]{3,2,1,0:T(8,128)} %get-tuple-element.94.raw_ref, ...), custom_call_target="tpu_custom_call" | custom-call | flops 38654705664 | bytes 60000000 | tf_op jit(solution)/shard_map/flat_back/pallas_call | solution.py:721
  250.7 20.8 %up_weight.1 = (f32[16,9,32,256]{3,2,1,0:T(8,128)}, bf16[16,9,32,256]{3,2,1,0:T(8,128)(2,1)}) custom-call(s32[1]{0:T(128)} %bitcast.refs_1_.refs_0_.refs_4_.refs_7_, bf16[2,4,2,1056,512]{4,3,2,1,0:T(8,128)(2,1)} %get-tuple-element.96.refs_1_.grad_ref, bf16[2,2,1056,512]{3,2,1,0:T(8,128)(2,1)} %get-tuple-element.97.refs_2_, ...), custom_call_target="tpu_custom_call" | custom-call | flops 9663676416 | bytes 30000000 | tf_op jit(solution)/shard_map/up_weight/pallas_call | solution.py:747
  273.2 18.2 %up_back.1 = (f32[2,512,1024]{2,1,0:T(8,128)}, f32[2,8,512]{2,1,0:T(8,128)}) custom-call(f32[16,9,32,256]{3,2,1,0:T(8,128)} %get-tuple-element.100._, bf16[2,4,2,1056,512]{4,3,2,1,0:T(8,128)(2,1)} %get-tuple-element.96.refs_1_.grad_ref, bf16[2,1024,512]{2,1,0:T(8,128)(2,1)} %fusion.1.refs_3_.feat_ref, ...), custom_call_target="tpu_custom_call" | custom-call | flops 9663676416 | bytes 30000000 | tf_op jit(solution)/shard_map/up_back/pallas_call | solution.py:773
  293.8 2.9 collective-permute-start.35
  299.2 2.9 dynamic-slice_convert_fusion.refs_3_
  304.3 2.9 convert_add_fusion
  312.5 20.5 %flat_weight_0.1 = (f32[16,3,32,256]{3,2,1,0:T(8,128)}, bf16[16,3,32,256]{3,2,1,0:T(8,128)(2,1)}, f32[8,128]{1,0:T(8,128)}) custom-call(bf16[2,2,9,32,256]{4,3,2,1,0:T(8,128)(2,1)} %get-tuple-element.271.refs_0_, bf16[2,2,9,32,256]{4,3,2,1,0:T(8,128)(2,1)} %get-tuple-element.270.refs_1_, f32[16,512]{1,0:T(8,128)} %copy-done.26, ...), custom_call_target="tpu_custom_call" | custom-call | flops 12884901888 | bytes 40000000 | tf_op jit(solution)/shard_map/flat_weight_0/pallas_call | solution.py:692
  334.7 4.7 %copy.106 = f32[256,4,1024]{2,1,0:T(4,128)} copy(f32[256,4,1024]{2,0,1:T(8,128)S(1)} %fusion) | data formatting | bytes 8388608
  345.8 20.7 %flat_weight_1.1 = (f32[16,3,32,256]{3,2,1,0:T(8,128)}, bf16[16,3,32,256]{3,2,1,0:T(8,128)(2,1)}, f32[8,128]{1,0:T(8,128)}) custom-call(bf16[2,9,32,256]{3,2,1,0:T(8,128)(2,1)} %fusion.18.refs_0_, bf16[2,9,32,256]{3,2,1,0:T(8,128)(2,1)} %fusion.19.refs_1_, f32[64,512]{1,0:T(8,128)} %copy-done.27, f32[8,128]{1,0:T(8,128)} %get-tuple-element.108.refs_3_, ...), custom_call_target="tpu_custom_call" | custom-call | flops 12884901888 | bytes 40000000 | tf_op jit(solution)/shard_map/flat_weight_1/pallas_call | solution.py:692
  367.5 3.8 concatenate.98.refs_5_
  382.7 20.7 %flat_weight_2.1 = (f32[16,3,32,256]{3,2,1,0:T(8,128)}, bf16[16,3,32,256]{3,2,1,0:T(8,128)(2,1)}, f32[8,128]{1,0:T(8,128)}) custom-call(bf16[9,32,256]{2,1,0:T(8,128)(2,1)} %fusion.33.refs_0_, bf16[9,32,256]{2,1,0:T(8,128)(2,1)} %get-tuple-element.287.refs_1_, bf16[9,32,256]{2,1,0:T(8,128)(2,1)} %get-tuple-element.286.refs_2_, ...), custom_call_target="tpu_custom_call" | custom-call | flops 12884901888 | bytes 40000000 | tf_op jit(solution)/shard_map/flat_weight_2/pallas_call | solution.py:692
  404.9 4.4 concatenate.100
  427.6 3.3 small_finish.1
  434.3 3.0 collective-permute-done.55
  444.9 2.9 collective-permute-done.59
  (362 shorter events, 125.1 us)
Async XLA Ops:
  14.9 24.6 %collective-permute-start.3 = (bf16[256,2,1024]{0,2,1:T(8,128)(2,1)}, bf16[256,2,1024]{0,2,1:T(8,128)(2,1)S(1)}, u32[]{:S(2)}, u32[]{:S(2)}) collective-permute-start(bf16[256,2,1024]{0,2,1:T(8,128)(2,1)} %copy.116), channel_id=1, source_target_pairs={{0,1},{1,0},{2,3},{3,2},{4,5},{5,4},{6,7},{7,6},{8,9},{9,8},{10,11... | collective-permute-start | bytes 3145736 | tf_op jit(solution)/shard_map/ppermute | solution.py:798
  17.1 24.0 %collective-permute-start = (bf16[9,32,256]{2,1,0:T(8,128)(2,1)}, bf16[9,32,256]{2,1,0:T(8,128)(2,1)}, u32[]{:S(2)}, u32[]{:S(2)}) collective-permute-start(bf16[9,32,256]{2,1,0:T(8,128)(2,1)} %get-tuple-element.291), channel_id=1, source_target_pairs={{0,8},{1,9},{2,10},{3,11},{4,12},{5,13},{6,14},{7,15},{8,0},{9,1},... | collective-permute-start | bytes 442376 | tf_op jit(solution)/shard_map/ppermute | solution.py:798
  21.9 20.8 %collective-permute-start.1 = (bf16[9,32,256]{2,1,0:T(8,128)(2,1)}, bf16[9,32,256]{2,1,0:T(8,128)(2,1)}, u32[]{:S(2)}, u32[]{:S(2)}) collective-permute-start(bf16[9,32,256]{2,1,0:T(8,128)(2,1)} %get-tuple-element.291), channel_id=1, source_target_pairs={{0,16},{1,17},{2,18},{3,19},{4,20},{5,21},{6,22},{7,23},{8,24},{9,... | collective-permute-start | bytes 442376 | tf_op jit(solution)/shard_map/ppermute | solution.py:798
  24.9 25.6 %collective-permute-start.12 = (bf16[2,12,32,256]{3,2,1,0:T(8,128)(2,1)}, bf16[2,12,32,256]{3,2,1,0:T(8,128)(2,1)}, u32[]{:S(2)}, u32[]{:S(2)}) collective-permute-start(bf16[2,12,32,256]{3,2,1,0:T(8,128)(2,1)} %pad_maximum_fusion.2.refs_11_), channel_id=1, source_target_pairs={{0,4},{1,5},{2,6},{3,7},{4,0},{5,1},{6,2},{7,3},{8,12},{9,13},{10,... | collective-permute-start | bytes 1179656 | tf_op jit(solution)/shard_map/ppermute | solution.py:798
  51.3 19.5 %collective-permute-start.11 = (bf16[2,12,32,256]{3,2,1,0:T(8,128)(2,1)}, bf16[2,12,32,256]{3,2,1,0:T(8,128)(2,1)}, u32[]{:S(2)}, u32[]{:S(2)}) collective-permute-start(bf16[2,12,32,256]{3,2,1,0:T(8,128)(2,1)} %pad_maximum_fusion.2.refs_11_), channel_id=1, source_target_pairs={{0,1},{1,0},{2,3},{3,2},{4,5},{5,4},{6,7},{7,6},{8,9},{9,8},{10,11... | collective-permute-start | bytes 1179656 | tf_op jit(solution)/shard_map/ppermute | solution.py:798
  75.8 34.8 %collective-permute-start.22 = (bf16[4,9,32,256]{3,2,1,0:T(8,128)(2,1)S(1)}, bf16[4,9,32,256]{3,2,1,0:T(8,128)(2,1)S(1)}, u32[]{:S(2)}, u32[]{:S(2)}) collective-permute-start(bf16[4,9,32,256]{3,2,1,0:T(8,128)(2,1)S(1)} %pad_maximum_fusion.refs_0_.refs_9_), channel_id=1, source_target_pairs={{0,5},{1,4},{2,7},{3,6},{4,1},{5,0},{6,3},{7,2},{8,13},{9,12},{10,... | collective-permute-start | bytes 1769480 | tf_op jit(solution)/shard_map/ppermute | solution.py:798
  76.2 34.4 %collective-permute-start.23 = (bf16[4,9,32,256]{3,2,1,0:T(8,128)(2,1)S(1)}, bf16[4,9,32,256]{3,2,1,0:T(8,128)(2,1)S(1)}, u32[]{:S(2)}, u32[]{:S(2)}) collective-permute-start(bf16[4,9,32,256]{3,2,1,0:T(8,128)(2,1)S(1)} %pad_maximum_fusion.refs_0_.refs_9_), channel_id=1, source_target_pairs={{0,1},{1,0},{2,3},{3,2},{4,5},{5,4},{6,7},{7,6},{8,9},{9,8},{10,11... | collective-permute-start | bytes 1769480 | tf_op jit(solution)/shard_map/ppermute | solution.py:798
  77.7 32.9 %collective-permute-start.24 = (bf16[4,9,32,256]{3,2,1,0:T(8,128)(2,1)S(1)}, bf16[4,9,32,256]{3,2,1,0:T(8,128)(2,1)S(1)}, u32[]{:S(2)}, u32[]{:S(2)}) collective-permute-start(bf16[4,9,32,256]{3,2,1,0:T(8,128)(2,1)S(1)} %pad_maximum_fusion.refs_0_.refs_9_), channel_id=1, source_target_pairs={{0,4},{1,5},{2,6},{3,7},{4,0},{5,1},{6,2},{7,3},{8,12},{9,13},{10,... | collective-permute-start | bytes 1769480 | tf_op jit(solution)/shard_map/ppermute | solution.py:798
  271.5 32.8 %collective-permute-start.30 = (bf16[16,9,32,256]{3,2,1,0:T(8,128)(2,1)}, bf16[16,9,32,256]{3,2,1,0:T(8,128)(2,1)}, u32[]{:S(2)}, u32[]{:S(2)}) collective-permute-start(bf16[16,9,32,256]{3,2,1,0:T(8,128)(2,1)} %get-tuple-element.103), channel_id=1, source_target_pairs={{0,2},{1,3},{2,0},{3,1},{4,6},{5,7},{6,4},{7,5},{8,10},{9,11},{10,... | collective-permute-start | bytes 7077896 | tf_op jit(solution)/shard_map/ppermute | solution.py:798
  296.7 36.3 %collective-permute-start.36 = (f32[16,512]{1,0:T(8,128)S(1)}, f32[16,512]{1,0:T(8,128)S(1)}, u32[]{:S(2)}, u32[]{:S(2)}) collective-permute-start(f32[16,512]{1,0:T(8,128)S(1)} %concatenate.94.refs_2_.refs_1_), channel_id=1, source_target_pairs={{0,16},{1,17},{2,18},{3,19},{4,20},{5,21},{6,22},{7,23},{8,24},{9,... | collective-permute-start | bytes 98312 | tf_op jit(solution)/shard_map/ppermute | solution.py:798
  297.8 35.3 %collective-permute-start.37 = (f32[16,512]{1,0:T(8,128)S(1)}, f32[16,512]{1,0:T(8,128)S(1)}, u32[]{:S(2)}, u32[]{:S(2)}) collective-permute-start(f32[16,512]{1,0:T(8,128)S(1)} %concatenate.94.refs_2_.refs_1_), channel_id=1, source_target_pairs={{0,24},{1,25},{2,26},{3,27},{4,28},{5,29},{6,30},{7,31},{8,16},{9,... | collective-permute-start | bytes 98312 | tf_op jit(solution)/shard_map/ppermute | solution.py:798
  302.0 31.7 %collective-permute-start.29 = (bf16[2,256,1024]{2,1,0:T(8,128)(2,1)}, bf16[2,256,1024]{2,1,0:T(8,128)(2,1)S(1)}, u32[]{:S(2)}, u32[]{:S(2)}) collective-permute-start(bf16[2,256,1024]{2,1,0:T(8,128)(2,1)} %dynamic-slice_convert_fusion.refs_3_), channel_id=1, source_target_pairs={{0,1},{1,0},{2,3},{3,2},{4,5},{5,4},{6,7},{7,6},{8,9},{9,8},{10,11... | collective-permute-start | bytes 3145736 | tf_op jit(solution)/shard_map/ppermute | solution.py:798
  310.5 30.6 %collective-permute-start.31 = (bf16[2,2,9,32,256]{4,3,2,1,0:T(8,128)(2,1)}, bf16[2,2,9,32,256]{4,3,2,1,0:T(8,128)(2,1)}, u32[]{:S(2)}, u32[]{:S(2)}) collective-permute-start(bf16[2,2,9,32,256]{4,3,2,1,0:T(8,128)(2,1)} %get-tuple-element.271.refs_0_), channel_id=1, source_target_pairs={{0,1},{1,0},{2,3},{3,2},{4,5},{5,4},{6,7},{7,6},{8,9},{9,8},{10,11... | collective-permute-start | bytes 1769480 | tf_op jit(solution)/shard_map/ppermute | solution.py:798
  312.0 29.0 %collective-permute-start.32 = (bf16[2,2,9,32,256]{4,3,2,1,0:T(8,128)(2,1)}, bf16[2,2,9,32,256]{4,3,2,1,0:T(8,128)(2,1)}, u32[]{:S(2)}, u32[]{:S(2)}) collective-permute-start(bf16[2,2,9,32,256]{4,3,2,1,0:T(8,128)(2,1)} %get-tuple-element.270.refs_1_), channel_id=1, source_target_pairs={{0,4},{1,5},{2,6},{3,7},{4,0},{5,1},{6,2},{7,3},{8,12},{9,13},{10,... | collective-permute-start | bytes 1769480 | tf_op jit(solution)/shard_map/ppermute | solution.py:798
  333.1 34.3 %collective-permute-start.42 = (f32[64,512]{1,0:T(8,128)S(1)}, f32[64,512]{1,0:T(8,128)S(1)}, u32[]{:S(2)}, u32[]{:S(2)}) collective-permute-start(f32[64,512]{1,0:T(8,128)S(1)} %concatenate.97.refs_2_), channel_id=1, source_target_pairs={{0,1},{1,0},{2,3},{3,2},{4,5},{5,4},{6,7},{7,6},{8,9},{9,8},{10,11... | collective-permute-start | bytes 393224 | tf_op jit(solution)/shard_map/ppermute | solution.py:798
  333.7 38.7 %collective-permute-start.41 = (bf16[16,3,32,256]{3,2,1,0:T(8,128)(2,1)}, bf16[16,3,32,256]{3,2,1,0:T(8,128)(2,1)}, u32[]{:S(2)}, u32[]{:S(2)}) collective-permute-start(bf16[16,3,32,256]{3,2,1,0:T(8,128)(2,1)} %get-tuple-element.119), channel_id=1, source_target_pairs={{0,2},{1,3},{2,0},{3,1},{4,6},{5,7},{6,4},{7,5},{8,10},{9,11},{10,... | collective-permute-start | bytes 2359304 | tf_op jit(solution)/shard_map/ppermute | solution.py:798
  345.3 31.4 %collective-permute-start.33 = (bf16[2,9,32,256]{3,2,1,0:T(8,128)(2,1)}, bf16[2,9,32,256]{3,2,1,0:T(8,128)(2,1)}, u32[]{:S(2)}, u32[]{:S(2)}) collective-permute-start(bf16[2,9,32,256]{3,2,1,0:T(8,128)(2,1)} %fusion.18.refs_0_), channel_id=1, source_target_pairs={{0,4},{1,5},{2,6},{3,7},{4,0},{5,1},{6,2},{7,3},{8,12},{9,13},{10,... | collective-permute-start | bytes 884744 | tf_op jit(solution)/shard_map/ppermute | solution.py:798
  371.3 32.1 %collective-permute-start.66 = (f32[128,512]{1,0:T(8,128)}, f32[128,512]{1,0:T(8,128)S(1)}, u32[]{:S(2)}, u32[]{:S(2)}) collective-permute-start(f32[128,512]{1,0:T(8,128)} %concatenate.98.refs_5_), channel_id=1, source_target_pairs={{0,4},{1,5},{2,6},{3,7},{4,0},{5,1},{6,2},{7,3},{8,12},{9,13},{10,... | collective-permute-start | bytes 786440 | tf_op jit(solution)/shard_map/ppermute | solution.py:798
  372.4 49.4 %collective-permute-start.50 = (bf16[16,3,32,256]{3,2,1,0:T(8,128)(2,1)}, bf16[16,3,32,256]{3,2,1,0:T(8,128)(2,1)}, u32[]{:S(2)}, u32[]{:S(2)}) collective-permute-start(bf16[16,3,32,256]{3,2,1,0:T(8,128)(2,1)} %get-tuple-element.129), channel_id=1, source_target_pairs={{0,2},{1,3},{2,0},{3,1},{4,6},{5,7},{6,4},{7,5},{8,10},{9,11},{10,... | collective-permute-start | bytes 2359304 | tf_op jit(solution)/shard_map/ppermute | solution.py:798
  375.2 34.2 %collective-permute-start.43 = (bf16[2,2,3,32,256]{4,3,2,1,0:T(8,128)(2,1)}, bf16[2,2,3,32,256]{4,3,2,1,0:T(8,128)(2,1)}, u32[]{:S(2)}, u32[]{:S(2)}) collective-permute-start(bf16[2,2,3,32,256]{4,3,2,1,0:T(8,128)(2,1)} %get-tuple-element.285.refs_3_), channel_id=1, source_target_pairs={{0,1},{1,0},{2,3},{3,2},{4,5},{5,4},{6,7},{7,6},{8,9},{9,8},{10,11... | collective-permute-start | bytes 589832 | tf_op jit(solution)/shard_map/ppermute | solution.py:798
  376.7 32.8 %collective-permute-start.44 = (bf16[2,2,3,32,256]{4,3,2,1,0:T(8,128)(2,1)}, bf16[2,2,3,32,256]{4,3,2,1,0:T(8,128)(2,1)}, u32[]{:S(2)}, u32[]{:S(2)}) collective-permute-start(bf16[2,2,3,32,256]{4,3,2,1,0:T(8,128)(2,1)} %get-tuple-element.284.refs_4_), channel_id=1, source_target_pairs={{0,4},{1,5},{2,6},{3,7},{4,0},{5,1},{6,2},{7,3},{8,12},{9,13},{10,... | collective-permute-start | bytes 589832 | tf_op jit(solution)/shard_map/ppermute | solution.py:798
  380.7 30.1 %collective-permute-start.39 = (bf16[9,32,256]{2,1,0:T(8,128)(2,1)}, bf16[9,32,256]{2,1,0:T(8,128)(2,1)S(1)}, u32[]{:S(2)}, u32[]{:S(2)}) collective-permute-start(bf16[9,32,256]{2,1,0:T(8,128)(2,1)} %get-tuple-element.287.refs_1_), channel_id=1, source_target_pairs={{0,16},{1,17},{2,18},{3,19},{4,20},{5,21},{6,22},{7,23},{8,24},{9,... | collective-permute-start | bytes 442376 | tf_op jit(solution)/shard_map/ppermute | solution.py:798
  410.7 29.8 %collective-permute-start.58 = (bf16[16,3,32,256]{3,2,1,0:T(8,128)(2,1)}, bf16[16,3,32,256]{3,2,1,0:T(8,128)(2,1)}, u32[]{:S(2)}, u32[]{:S(2)}) collective-permute-start(bf16[16,3,32,256]{3,2,1,0:T(8,128)(2,1)} %get-tuple-element.131), channel_id=1, source_target_pairs={{0,2},{1,3},{2,0},{3,1},{4,6},{5,7},{6,4},{7,5},{8,10},{9,11},{10,... | collective-permute-start | bytes 2359304 | tf_op jit(solution)/shard_map/ppermute | solution.py:798
  437.4 20.0 %collective-permute-start.56 = (bf16[3,32,256]{2,1,0:T(8,128)(2,1)S(1)}, bf16[3,32,256]{2,1,0:T(8,128)(2,1)S(1)}, u32[]{:S(2)}, u32[]{:S(2)}) collective-permute-start(bf16[3,32,256]{2,1,0:T(8,128)(2,1)S(1)} %get-tuple-element.294), channel_id=1, source_target_pairs={{0,16},{1,17},{2,18},{3,19},{4,20},{5,21},{6,22},{7,23},{8,24},{9,... | collective-permute-start | bytes 147464 | tf_op jit(solution)/shard_map/ppermute | solution.py:798
  (108 other events, 1925.0 us)

commit v3 on v2

--- a/solution.py
+++ b/solution.py
@@ -13,6 +13,7 @@
 
 PRECISE = lax.Precision.HIGHEST
 ROOT_TWO = 1.4142135623730951
+LOG_TWO = 0.6931471805599453
 BETA_ONE = 0.9
 BETA_TWO = 0.99
 LEARN_RATE = 0.3
@@ -52,16 +53,21 @@
     )
 
 
-def softplus(values):
-    return jnp.maximum(values, 0.0) + jnp.log(1.0 + jnp.exp(-jnp.abs(values)))
-
-
-def activate(values):
-    return (0.2 * ROOT_TWO) * values + (0.8 * ROOT_TWO) * softplus(values)
-
-
-def slope(values):
-    return 0.6 + 0.4 * jnp.tanh(0.5 * values)
+def half_tanh(values):
+    return jnp.tanh(0.5 * values)
+
+
+def leaky(values, half, scale):
+    line = (0.6 * scale) * values + (0.4 * scale) * jnp.abs(values)
+    return line + ((0.8 * scale * LOG_TWO) - (0.8 * scale) * jnp.log(1.0 + jnp.abs(half)))
+
+
+def slope(half):
+    return 0.6 + 0.4 * half
+
+
+def slope_of(style, half):
+    return (0.6 * ROOT_TWO) * style + ((0.4 * ROOT_TWO) * style) * half
 
 
 def side_copy(values, odd):
@@ -122,7 +128,7 @@
             ref[0, phase, copy, PAD + PIX :, :] = empty
 
 
-def place_of(device, shape, layout):
+def place_of(device, layout):
     across, rows, cols = layout
     row = pl.multiple_of((device // across) * rows, rows)
     col = pl.multiple_of((device % across) * cols, cols)
@@ -135,13 +141,18 @@
     copies = []
     for offsets, ref in zip(pieces, piece_refs):
         for index, offset in enumerate(offsets):
-            rows, cols = place_of(me ^ offset, target.shape, layout)
+            rows, cols = place_of(me ^ offset, layout)
             copies.append(
                 pltpu.make_async_copy(
                     ref.at[index], target.at[:, rows, cols], sems.at[len(copies)]
                 )
             )
     return copies
+
+
+def transpose_taps(weight_ref, out_ref):
+    for tap in range(9):
+        out_ref[tap] = jnp.transpose(weight_ref[tap])
 
 
 def first_step():
@@ -216,9 +227,10 @@
             raw = raw_buf[index % 2]
             raw_ref[0, 0, pl.ds(start, TILE), :] = raw
             noise = noise_cols[start : start + TILE, phase % 2 : phase % 2 + 1]
-            pre = raw * demod + noise + bias
+            pre = raw * demod + (noise + bias)
+            act = leaky(pre, half_tanh(pre), ROOT_TWO)
             write_map(
-                map_ref, 0, pl.ds(PAD + start, TILE), activate(pre) * style_two, phase % 2 == 1
+                map_ref, 0, pl.ds(PAD + start, TILE), act * style_two, phase % 2 == 1
             )
 
         steps = PIX // TILE
@@ -238,10 +250,12 @@
 
 def flat_forward(pieces, layout, *refs):
     count = len(pieces)
-    me_ref, scal_ref, map_ref, vec_ref, noise_ref, base_ref, mask_ref, critic_ref, rgb_ref = refs[:9]
-    piece_refs = refs[9 : 9 + count]
-    grad_ref, sums_ref, color_ref, whole_ref = refs[9 + count : 13 + count]
-    raw_buf, sq_buf, total_buf, weight_ref, sems, out_sem = refs[13 + count :]
+    me_ref, scal_ref, map_ref, vec_ref, noise_ref, base_ref, mask_ref, critic_ref, rgb_ref, rgb_cols_ref = refs[:10]
+    piece_refs = refs[10 : 10 + count]
+    grad_ref, sums_ref, color_ref, whole_ref = refs[10 + count : 14 + count]
+    raw_buf, act_buf, half_buf, low_buf, turned_ref, sq_buf, total_buf, weight_ref, sems, out_sem = refs[
+        14 + count :
+    ]
     row_parity = pl.program_id(1)
 
     @pl.when(first_step())
@@ -252,6 +266,7 @@
         for copy in copies:
             copy.wait()
         pltpu.make_async_copy(weight_ref, whole_ref, out_sem).start()
+        transpose_taps(weight_ref, turned_ref)
         square_sums(weight_ref, sq_buf)
 
     @pl.when(row_parity == 0)
@@ -280,27 +295,31 @@
         start = (index % per_phase) * TILE
         raw = None
         for tap, phase, copy, first in taps[index // per_phase]:
-            part = mul(tap_rows(map_ref, phase, copy, first, start, TILE), weight_ref[tap], NT)
+            part = mul(tap_rows(map_ref, phase, copy, first, start, TILE), turned_ref[tap], NN)
             raw = part if raw is None else raw + part
-        raw_buf[index % 2] = raw
-
-    def finish(index):
+        raw_buf[index % 3] = raw
+
+    def judge(index):
         col_parity = index // per_phase
         start = (index % per_phase) * TILE
-        raw = raw_buf[index % 2]
+        raw = raw_buf[index % 3]
         noise = noise_all[start : start + TILE, col_parity : col_parity + 1]
-        pre = raw * demod + strength * noise + bias
-        act = activate(pre)
+        pre = raw * demod + (strength * noise + bias)
+        half = half_tanh(pre)
+        act = leaky(pre, half, ROOT_TWO)
+        act_buf[index % 2] = act
+        half_buf[index % 2] = half
         modulated = (act * style_three).astype(jnp.bfloat16)
-        colors = mul(rgb, modulated, NT)[0:8] + base_ref[0, :, start : start + TILE]
+        colors = jnp.transpose(mul(modulated, rgb_cols_ref[...], NN))[0:8]
+        colors = colors + base_ref[0, :, start : start + TILE]
         hidden = mix[:, 3:4]
         for color in range(3):
             hidden = hidden + mix[:, color : color + 1] * colors[color : color + 1]
-        unit = 0.2 * hidden + 0.8 * softplus(hidden)
-        logits = column_sums(out * unit)
+        hidden_half = half_tanh(hidden)
+        logits = column_sums(out * leaky(hidden, hidden_half, 1.0))
         mask = mask_ref[0, 0, col_parity : col_parity + 1, start : start + TILE]
         grad_logits = -mask / (1.0 + jnp.exp(logits))
-        grad_hidden = out * grad_logits * slope(hidden)
+        grad_hidden = out * grad_logits * slope(hidden_half)
         grad_colors = jnp.concatenate(
             [column_sums(mix[:, color : color + 1] * grad_hidden) for color in range(3)]
             + [jnp.zeros((5, TILE), jnp.float32)],
@@ -308,11 +327,21 @@
         )
         for lane in range(0, TILE, 128):
             color_ref[0] += grad_colors[:, lane : lane + 128]
-        grad_low = jnp.concatenate(
+        low_buf[index % 2] = jnp.concatenate(
             [grad_colors, jnp.zeros((8, TILE), jnp.float32)], axis=0
         ).astype(jnp.bfloat16)
+
+    def finish(index):
+        col_parity = index // per_phase
+        start = (index % per_phase) * TILE
+        raw = raw_buf[index % 3]
+        act = act_buf[index % 2]
+        half = half_buf[index % 2]
+        grad_low = low_buf[index % 2]
+        noise = noise_all[start : start + TILE, col_parity : col_parity + 1]
+        modulated = (act * style_three).astype(jnp.bfloat16)
         grad_map = mul(grad_low, rgb, TN)
-        grad_pre = grad_map * (style_three * ROOT_TWO) * slope(pre)
+        grad_pre = grad_map * slope_of(style_three, half)
         write_map(grad_ref, col_parity, pl.ds(PAD + start, TILE), grad_pre * demod, col_parity == 1)
         add_rows(total_buf, 0, grad_map * act)
         add_rows(total_buf, 1, grad_pre * raw)
@@ -321,11 +350,13 @@
         total_buf[4] += mul(grad_low, modulated, NN)[0:8]
 
     steps = 2 * per_phase
-    for index in range(steps + 1):
+    for index in range(steps + 2):
         if index < steps:
             convolve(index)
-        if index > 0:
-            finish(index - 1)
+        if 0 < index <= steps:
+            judge(index - 1)
+        if index > 1:
+            finish(index - 2)
 
     @pl.when(row_parity == 1)
     def _():
@@ -349,20 +380,69 @@
 
 
 def spread_out(me, order, layout, acc_ref, weight_ref, squares, out_refs):
-    for tap in range(acc_ref.shape[0]):
+    for tap in range(weight_ref.shape[0]):
         acc_ref[tap] += 2.0 * weight_ref[tap].astype(jnp.float32) * squares
     if layout is None:
         out_refs[0][0] = acc_ref[...].astype(out_refs[0].dtype)
         return
     for offsets, out_ref in zip(order, out_refs):
         for index, offset in enumerate(offsets):
-            rows, cols = place_of(me ^ offset, acc_ref.shape, layout)
+            rows, cols = place_of(me ^ offset, layout)
             out_ref[index] = acc_ref[:, rows, cols].astype(out_ref.dtype)
+
+
+def stacked_rows(rows, count):
+    short = count - len(rows)
+    empty = [jnp.zeros((short, rows[0].shape[1]), rows[0].dtype)] if short else []
+    return jnp.concatenate(rows + empty)
+
+
+def small_planes(me, layout, lat_ref, sums_one_ref, sums_ref, feat_sums_ref, color_ref, acc_ref):
+    images = range(lat_ref.shape[0])
+    _, rows, cols = layout
+    chans = acc_ref.shape[2]
+    style_rows = [
+        [feat_sums_ref[image, 0:1, :] for image in images],
+        [sums_one_ref[image, 0:1, :] + sums_ref[image, 5:6, :] for image in images],
+        [sums_ref[image, 0:1, :] for image in images],
+    ]
+    latents = stacked_rows([lat_ref[image].astype(jnp.float32) for image in images], 16)
+    latents = latents.astype(jnp.bfloat16)
+    sums = []
+    for number in range(3):
+        grads = stacked_rows(style_rows[number], 16).astype(jnp.bfloat16)
+        acc_ref[3 + number] = mul(latents, grads, TN)
+        sums.append(column_sums(grads.astype(jnp.float32)))
+    sums.append(sum(sums_one_ref[image, 2:3, :] for image in images))
+    sums.append(sum(sums_ref[image, 2:3, :] for image in images))
+    for color in range(3):
+        row = 8 + color
+        sums.append(sum(sums_ref[image, row : row + 1, :] for image in images) * C ** (-0.5))
+    scalars = [
+        sum(sums_one_ref[image, 3:4, :] for image in images),
+        sum(sums_ref[image, 3:4, :] for image in images),
+    ] + [sum(color_ref[image, color : color + 1, :] for image in images) for color in range(3)]
+    lane = lax.broadcasted_iota(jnp.int32, (1, chans), 1) & (cols - 1)
+    row = jnp.zeros((1, chans), jnp.float32)
+    for number, values in enumerate(scalars):
+        total = jnp.sum(values, axis=1, keepdims=True)
+        row = jnp.where(lane == len(scalars) * me + number, total, row)
+    pieces = []
+    for _ in range(3):
+        piece = row.astype(jnp.bfloat16).astype(jnp.float32)
+        pieces.append(piece)
+        row = row - piece
+    block = jnp.concatenate([stacked_rows(sums, 16), stacked_rows(pieces, rows - 16)])
+    for start in range(0, chans, rows):
+        acc_ref[6, start : start + rows, :] = block
 
 
 def flat_weight(order, layout, part, waits, *refs):
     me_ref, grad_ref, map_ref, weight_ref, vec_ref, sums_ref = refs[waits : waits + 6]
-    out_refs, token_ref, acc_ref = refs[waits + 6 : -2], refs[-2], refs[-1]
+    token_ref, acc_ref = refs[-2:]
+    small = acc_ref.shape[0] > 3
+    small_refs = refs[waits + 6 : waits + 10] if small else ()
+    out_refs = refs[waits + 6 + len(small_refs) : -2]
     row_parity = pl.program_id(1)
     first = pl.multiple_of(PAD * ((row_parity + part + 1) >> 1), PAD)
 
@@ -384,6 +464,11 @@
             [sums_ref[image, 4:5, :] for image in images],
             [vec_ref[image, 1:2, :] * vec_ref[image, 1:2, :] for image in images],
         )
+        if small:
+            lat_ref, sums_one_ref, feat_sums_ref, color_ref = small_refs
+            small_planes(
+                me_ref[0], layout, lat_ref, sums_one_ref, sums_ref, feat_sums_ref, color_ref, acc_ref
+            )
         spread_out(me_ref[0], order, layout, acc_ref, weight_ref, squares, out_refs)
         token_ref[...] = squares[0:8, 0:128]
 
@@ -449,10 +534,11 @@
         grad_map = back_buf[index % 2]
         raw = raw_ref[0, col_parity, pl.ds(start, TILE), :]
         noise = noise_all[start : start + TILE, col_parity : col_parity + 1]
-        pre = raw * demod + strength * noise + bias
-        grad_pre = grad_map * (style_two * ROOT_TWO) * slope(pre)
+        pre = raw * demod + (strength * noise + bias)
+        half = half_tanh(pre)
+        grad_pre = grad_map * slope_of(style_two, half)
         write_map(out_ref, col_parity, pl.ds(PAD + start, TILE), grad_pre * demod, col_parity == 1)
-        add_rows(total_buf, 0, grad_map * activate(pre))
+        add_rows(total_buf, 0, grad_map * leaky(pre, half, ROOT_TWO))
         add_rows(total_buf, 1, grad_pre * raw)
         add_rows(total_buf, 2, grad_pre)
         add_rows(total_buf, 3, grad_pre * noise)
@@ -471,7 +557,10 @@
         sums_ref[0, 4:8, :] = jnp.zeros((4, sums_ref.shape[2]), jnp.float32)
 
 
-def up_back(_, grad_ref, feat_ref, vec_ref, sums_in_ref, sq_ref, weight_ref, out_ref, sums_ref):
+def up_back(layout, *refs):
+    _, me_ref, grad_ref, feat_ref, vec_ref, sums_in_ref, sq_ref, weight_ref = refs[:8]
+    sums_ref, turned_ref = refs[-2:]
+    out_refs = refs[8:-2]
     style_one = vec_ref[0, 0:1, :]
     total = None
     for start in range(0, PIX, TILE):
@@ -483,73 +572,53 @@
                 grad_map = part if grad_map is None else grad_map + part
         found = column_sums(grad_map * feat_ref[0, pl.ds(start, TILE), :].astype(jnp.float32))
         total = found if total is None else total + found
-        out_ref[0, :, pl.ds(start, TILE)] = jnp.transpose(grad_map * style_one)
+        turned = jnp.transpose(grad_map * style_one)
+        here = pl.ds(start, TILE)
+        if layout is None:
+            out_refs[0][0, :, here] = turned
+        else:
+            turned_ref[...] = turned
+            for offset, out_ref in zip((0, BIT_X), out_refs):
+                _, cols = place_of(me_ref[0] ^ offset, layout)
+                out_ref[0, :, here] = turned_ref[cols, :].astype(out_ref.dtype)
     coef = coef_of(vec_ref, sums_in_ref, 0)
     back = exact(jnp.broadcast_to(coef, (8, coef.shape[1])), sq_ref[...], NN)
     sums_ref[0] = total + 2.0 * style_one * back
 
 
-def small_finish(images, layout, gain, count, *refs):
-    across_count, rows_own, cols_own = layout
-    me_ref, row_refs = refs[0], refs[1 : 1 + count]
-    old_refs = refs[1 + count : 16 + count]
-    new_refs = refs[16 + count : 31 + count]
-    total_ref, cross_ref = refs[31 + count :]
-    device = me_ref[0]
-    rows, cols = place_of(device, None, layout)
-    each = total_ref.shape[0]
-    stacked = jnp.concatenate([ref[...] for ref in row_refs])
-    chans = stacked.shape[1]
-    total_ref[...] = jnp.sum(stacked.reshape(stacked.shape[0] // each, each, chans), axis=0)
-    row = lax.broadcasted_iota(jnp.int32, stacked.shape, 0) & (each - 1)
-    latent_row = 3 * images
-    latents = jnp.where((row >= latent_row) & (row < latent_row + images), stacked, 0.0)
-    latents = latents.astype(jnp.bfloat16)
-
-    def step(number, gradient, old=None, new=None):
-        found = adam_step(*[ref[...] if old is None else ref[old] for ref in old_refs[3 * number : 3 * number + 3]], gradient, float(STEP))
+def small_finish(gain, *refs):
+    planes_ref, pick_ref = refs[:2]
+    old_refs, new_refs = refs[2:17], refs[17:]
+
+    def step(number, gradient, old=slice(None)):
+        olds = [ref[old] for ref in old_refs[3 * number : 3 * number + 3]]
+        found = adam_step(*olds, gradient, float(STEP))
         for ref, value in zip(new_refs[3 * number : 3 * number + 3], found):
-            if old is None:
-                ref[...] = value
-            else:
-                ref[old] = value
+            ref[old] = value
 
     for number in range(3):
-        moved = pltpu.roll(stacked, latent_row - number * images, 0) if number < 3 else stacked
-        cross_ref[...] = mul(latents, moved.astype(jnp.bfloat16), TN)
-        step(0, cross_ref[rows, cols] * gain, number)
-    mine = total_ref[:, cols]
-    step(
-        1,
-        jnp.concatenate(
-            [
-                jnp.sum(mine[number * images : (number + 1) * images], axis=0, keepdims=True)
-                for number in range(3)
-            ]
-        ),
-    )
-    first = 4 * images
-    step(2, mine[first : first + 2])
-    step(3, mine[first + 2 : first + 5])
-    step(4, total_ref[first + 5 : first + 6, 0:5])
-
-
-def call_small_finish(me, row_arrays, olds, images, layout, gain):
-    chans = row_arrays[0].shape[1]
+        step(0, planes_ref[number] * gain, number)
+    step(1, planes_ref[3, 0:3, :])
+    step(2, planes_ref[3, 3:5, :])
+    step(3, planes_ref[3, 5:8, :])
+    row = planes_ref[3, 16:17, :] + planes_ref[3, 17:18, :] + planes_ref[3, 18:19, :]
+    sums = exact(jnp.broadcast_to(row, (8, row.shape[1])), pick_ref[...], NN)
+    step(4, sums[0:1, 0:5])
+
+
+def call_small_finish(planes, olds, gain, devices):
+    lanes = jnp.arange(planes.shape[2], dtype=jnp.int32)[:, None]
+    pick = (lanes % 5 == jnp.arange(128, dtype=jnp.int32)) & (lanes < 5 * devices)
     olds = [old if old.ndim > 1 else old[None] for old in olds]
     out_shape = tuple(jax.ShapeDtypeStruct(old.shape, old.dtype) for old in olds)
     found = pl.pallas_call(
-        functools.partial(small_finish, images, layout, gain, len(row_arrays)),
-        in_specs=[SMEM] + [pl.BlockSpec(memory_space=pltpu.VMEM)] * (len(row_arrays) + len(olds)),
+        functools.partial(small_finish, gain),
+        in_specs=[pl.BlockSpec(memory_space=pltpu.VMEM)] * (2 + len(olds)),
         out_specs=[pl.BlockSpec(memory_space=pltpu.VMEM)] * len(olds),
         out_shape=out_shape,
-        scratch_shapes=[
-            pltpu.VMEM((row_arrays[0].shape[0], chans), jnp.float32),
-            pltpu.VMEM((chans, chans), jnp.float32),
-        ],
         compiler_params=params(),
         name="small_finish",
-    )(me, *row_arrays, *olds)
+    )(planes, pick.astype(jnp.float32), *olds)
     return tuple(found[:-3]) + tuple(value[0] for value in found[-3:])
 
 
@@ -636,6 +705,7 @@
 def call_flat_forward(me, scalars, maps, vecs, noise, base, mask, critic, rgb, weight):
     images, chans = maps.shape[0], maps.shape[-1]
     arrays, layout = [array for _, array in weight[0]], weight[1]
+    rgb_cols = jnp.concatenate([jnp.transpose(rgb), jnp.zeros((chans, 112), rgb.dtype)], axis=1)
     out_shape = (
         jax.ShapeDtypeStruct((images, 4, 2, ROWS, chans), jnp.bfloat16),
         jax.ShapeDtypeStruct((images, 16, chans), jnp.float32),
@@ -655,6 +725,7 @@
             pl.BlockSpec((1, 1, 8, PIX), lambda image, parity: (image, parity, 0, 0)),
             whole(critic.shape),
             whole(rgb.shape),
+            whole(rgb_cols.shape),
         ]
         + [ANY] * len(arrays),
         out_specs=[
@@ -665,7 +736,11 @@
         ],
         out_shape=out_shape,
         scratch_shapes=[
+            pltpu.VMEM((3, TILE, chans), jnp.float32),
             pltpu.VMEM((2, TILE, chans), jnp.float32),
+            pltpu.VMEM((2, TILE, chans), jnp.float32),
+            pltpu.VMEM((2, 16, TILE), jnp.bfloat16),
+            pltpu.VMEM((9, chans, chans), jnp.bfloat16),
             pltpu.VMEM((chans, chans), jnp.float32),
             pltpu.VMEM((5, 8, chans), jnp.float32),
             pltpu.VMEM((9, chans, chans), jnp.bfloat16),
@@ -675,7 +750,7 @@
         compiler_params=params(),
         cost_estimate=cost(72 * images * PIX * chans * chans, 60e6),
         name="flat_forward",
-    )(me, scalars, maps, vecs, noise, base, mask, critic, rgb, *arrays)
+    )(me, scalars, maps, vecs, noise, base, mask, critic, rgb, rgb_cols, *arrays)
 
 
 def gradient_shapes(chans, taps, layout):
@@ -686,9 +761,10 @@
     return (jax.ShapeDtypeStruct(shape, jnp.float32), jax.ShapeDtypeStruct(shape, jnp.bfloat16))
 
 
-def call_flat_weight(me, after, grad, maps, weight, vecs, sums, order, layout, part):
+def call_flat_weight(me, after, grad, maps, weight, vecs, sums, order, layout, part, small=()):
     images, chans = maps.shape[0], maps.shape[-1]
-    out_shape = gradient_shapes(chans, 3, layout) + (jax.ShapeDtypeStruct((8, 128), jnp.float32),)
+    planes = 7 if small else 3
+    out_shape = gradient_shapes(chans, planes, layout) + (jax.ShapeDtypeStruct((8, 128), jnp.float32),)
     return pl.pallas_call(
         functools.partial(flat_weight, order, layout, part, len(after)),
         grid=(images, 2),
@@ -702,14 +778,15 @@
             pl.BlockSpec((3, chans, chans), lambda image, parity: (part, 0, 0)),
             whole(vecs.shape),
             whole(sums.shape),
-        ],
+        ]
+        + [whole(array.shape) for array in small],
         out_specs=[whole(s.shape) for s in out_shape],
         out_shape=out_shape,
-        scratch_shapes=[pltpu.VMEM((3, chans, chans), jnp.float32)],
+        scratch_shapes=[pltpu.VMEM((planes, chans, chans), jnp.float32)],
         compiler_params=params(),
         cost_estimate=cost(24 * images * PIX * chans * chans, 40e6),
         name="flat_weight_" + str(part),
-    )(*after, me, grad, maps, weight, vecs, sums)
+    )(*after, me, grad, maps, weight, vecs, sums, *small)
 
 
 def call_flat_back(scalars, grad, raw, vecs, noise, weight):
@@ -764,17 +841,22 @@
     )(me, grad, xs, weight, vecs, sums)
 
 
-def call_up_back(after, grad, feat, vecs, sums, squares, weight):
+def call_up_back(after, me, grad, feat, vecs, sums, squares, weight, layout):
     images, _, chans = feat.shape
-    out_shape = (
-        jax.ShapeDtypeStruct((images, chans, PIX), jnp.float32),
-        jax.ShapeDtypeStruct((images, 8, chans), jnp.float32),
-    )
+    if layout is None:
+        out_shape = (jax.ShapeDtypeStruct((images, chans, PIX), jnp.float32),)
+    else:
+        shape = (images, layout[2], PIX)
+        out_shape = (
+            jax.ShapeDtypeStruct(shape, jnp.float32), jax.ShapeDtypeStruct(shape, jnp.bfloat16)
+        )
+    out_shape += (jax.ShapeDtypeStruct((images, 8, chans), jnp.float32),)
     return pl.pallas_call(
-        up_back,
+        functools.partial(up_back, layout),
         grid=(images,),
         in_specs=[
             ANY,
+            SMEM,
             per_image(grad.shape),
             per_image(feat.shape),
             per_image(vecs.shape),
@@ -782,12 +864,13 @@
             whole(squares.shape),
             whole(weight.shape),
         ],
-        out_specs=[per_image(out_shape[0].shape), per_image(out_shape[1].shape)],
+        out_specs=[per_image(s.shape) for s in out_shape],
         out_shape=out_shape,
+        scratch_shapes=[pltpu.VMEM((chans, TILE), jnp.float32)],
         compiler_params=params(),
         cost_estimate=cost(18 * images * PIX * chans * chans, 30e6),
         name="up_back",
-    )(after, grad, feat, vecs, sums, squares, weight)
+    )(after, me, grad, feat, vecs, sums, squares, weight)
 
 
 BIT_X, BIT_CORE, BIT_Y, BIT_LOW, BIT_HIGH = 1, 2, 4, 8, 16
@@ -804,11 +887,11 @@
     return low, jnp.stack([move(block, BIT_HIGH), move(block, BIT_HIGH + BIT_LOW)])
 
 
-def gather_in_turn(low, high, devices, ahead):
+def gather_in_turn(low, high, devices, beside):
     move = lambda values, bits: across(values, bits, devices)
     high_y, low_y = move(high, BIT_Y), move(low, BIT_Y)
-    low_ahead, high_ahead, _ = lax.optimization_barrier((low, high, ahead))
-    low_x, high_x = move(low_ahead, BIT_X), move(high_ahead, BIT_X)
+    low_x, high_x = move(low, BIT_X), move(high, BIT_X)
+    (low_x, high_y), beside = lax.optimization_barrier(((low_x, high_y), beside))
     low_xy, high_xy = move(low_x, BIT_Y), move(high_y, BIT_X)
     found = []
     for offsets, arrays in zip(
@@ -816,7 +899,7 @@
     ):
         for bits, array in zip((0, BIT_X, BIT_Y, BIT_X + BIT_Y), arrays):
             found.append((tuple(o ^ bits for o in offsets), array))
-    return found
+    return found, beside
 
 
 def gather_at_once(along, devices):
@@ -839,29 +922,24 @@
     return values if token is None else lax.optimization_barrier((values, token))[0]
 
 
-def gather_rows(rows, devices):
-    move = lambda values, bits: across(values, bits, devices)
-    token = yield (rows,)
-    found = [rows] + tie([move(rows, b) for b in (BIT_LOW, BIT_HIGH, BIT_LOW + BIT_HIGH)], token)
-    for bits in (BIT_X, BIT_Y, BIT_CORE):
-        joined = jnp.concatenate(found)
-        token = yield (joined,)
-        found = found + tie([move(joined, bits)], token)
-    yield found
-
-
-def scatter_order():
-    kept = []
-    for high in (0, 1):
-        one, two = (BIT_X, BIT_Y) if high == 0 else (BIT_Y, BIT_X)
-        for a in (0, 1):
-            for b in (0, 1):
-                for low in (0, 1):
-                    kept.append(high * BIT_HIGH + low * BIT_LOW + a * one + b * two)
+PLANE_OFFSETS = (BIT_X, BIT_Y, BIT_X + BIT_Y)
+Z_ALL = Z_OFFSETS[0] + Z_OFFSETS[1]
+
+
+def scatter_order(at_once):
+    if at_once:
+        kept = [plane + z for plane in (0,) + PLANE_OFFSETS for z in Z_ALL]
+    else:
+        kept = []
+        for high in (0, 1):
+            one, two = (BIT_X, BIT_Y) if high == 0 else (BIT_Y, BIT_X)
+            for a in (0, 1):
+                for b in (0, 1):
+                    kept += [z + a * one + b * two for z in Z_OFFSETS[high]]
     return tuple(kept), tuple(offset ^ BIT_CORE for offset in kept)
 
 
-def scatter_blocks(kept, sent, devices):
+def scatter_blocks(kept, sent, devices, at_once):
     low = lambda values: values.astype(jnp.bfloat16)
 
     def swap(values, bits, token):
@@ -870,19 +948,29 @@
 
     token = yield (sent,)
     total = kept + swap((sent,), (BIT_CORE,), token)[0]
-    total = total.reshape((2, 2, 2, 2) + kept.shape[1:])
-    sends = low(total[0, 1]), low(total[1, 1])
+    if at_once:
+        total = total.reshape((4, 4) + kept.shape[1:])
+        sends = low(total[1]), low(total[2]), low(total[3])
+        token = yield sends
+        mine = total[0]
+        for found in swap(sends, PLANE_OFFSETS, token):
+            mine = mine + found
+        mine = [mine[0], mine[1], mine[2], mine[3]]
+    else:
+        total = total.reshape((2, 2, 2, 2) + kept.shape[1:])
+        sends = low(total[0, 1]), low(total[1, 1])
+        token = yield sends
+        found = swap(sends, (BIT_X, BIT_Y), token)
+        halves = total[0, 0] + found[0], total[1, 0] + found[1]
+        sends = low(halves[0][1]), low(halves[1][1])
+        token = yield sends
+        found = swap(sends, (BIT_Y, BIT_X), token)
+        halves = halves[0][0] + found[0], halves[1][0] + found[1]
+        mine = [halves[0][0], halves[0][1], halves[1][0], halves[1][1]]
+    sends = low(mine[1]), low(mine[2]), low(mine[3])
     token = yield sends
-    found = swap(sends, (BIT_X, BIT_Y), token)
-    halves = total[0, 0] + found[0], total[1, 0] + found[1]
-    sends = low(halves[0][1]), low(halves[1][1])
-    token = yield sends
-    found = swap(sends, (BIT_Y, BIT_X), token)
-    halves = halves[0][0] + found[0], halves[1][0] + found[1]
-    sends = low(halves[0][1]), low(halves[1][0]), low(halves[1][1])
-    token = yield sends
-    total = halves[0][0]
-    for found in swap(sends, (BIT_LOW, BIT_HIGH, BIT_HIGH + BIT_LOW), token):
+    total = mine[0]
+    for found in swap(sends, Z_ALL[1:], token):
         total = total + found
     yield total
 
@@ -979,14 +1067,11 @@
     ref_block = jnp.transpose(refiner, (1, 2, 0)).astype(jnp.bfloat16)
     small_own = jnp.concatenate([modbias, actbias, rgbmix], axis=0)
     if by_hand:
-        layout, order = (n_ch, rows_own, local_chans), scatter_order()
+        layout = (n_ch, rows_own, local_chans)
         other = lax.dynamic_slice_in_dim(features, images - first, images, 1)
         other = across(other, BIT_X, devices)
         up_low, up_high = gather_along_z(up_block, devices)
         ref_along = jnp.concatenate(gather_along_z(ref_block, devices))
-        up_weight_all = (
-            with_other_core(gather_in_turn(up_low, up_high, devices, other), devices), layout
-        )
         here = mine(features, 1)
         feat = jnp.where(
             ch_index == 0, jnp.concatenate([here, other]), jnp.concatenate([other, here])
@@ -997,10 +1082,8 @@
             jnp.concatenate([small_own, small_other], axis=1),
             jnp.concatenate([small_other, small_own], axis=1),
         )
-        ref_plane = gather_at_once(ref_along, devices)
-        ahead = (ref_along,)
     else:
-        layout, order, ahead = None, None, ()
+        layout, ahead = None, ()
         up_weight_all = ([((0,), gather_whole(up_block, n_img, n_ch))], None)
         ref_weight_all = ([((0,), gather_whole(ref_block, n_img, n_ch))], None)
         small = lax.all_gather(small_own, "ch", axis=1, tiled=True)
@@ -1033,6 +1116,13 @@
     critic = jnp.concatenate(
         [critic_mix, critic_bias[:, None], critic_out[:, None], jnp.zeros((critic_mix.shape[0], 3))], axis=1
     )
+    if by_hand:
+        beside = (feat, small, noise, mask, base, critic, rgb_low, ref_along)
+        found, beside = gather_in_turn(up_low, up_high, devices, beside)
+        feat, small, noise, mask, base, critic, rgb_low, ref_along = beside
+        up_weight_all = (with_other_core(found, devices), layout)
+        ref_plane = gather_at_once(ref_along, devices)
+        ahead = (ref_along,)
 
     raw_one, maps, xs, up_square, vecs, up_full = call_up_forward(
         ahead, me, scalars, feat, lat_own[:, None, :], small, noise, up_weight_all
@@ -1045,65 +1135,55 @@
         me, scalars, maps, vecs, noise, base, mask, critic, rgb_low, ref_weight_all
     )
     grad_one, sums_one = call_flat_back(scalars, grad_two, raw_one, vecs, noise, ref_full)
-    up_parts = call_up_weight(me, grad_one, xs, up_full, vecs, sums_one, order, layout)
-    feat_grad, feat_sums = call_up_back(
-        up_parts[0], grad_one, feat, vecs, sums_one, up_square, up_full
-    )
-
-    style_grads = jnp.stack(
-        [feat_sums[:, 0], sums_one[:, 0] + sums_two[:, 5], sums_two[:, 0]]
-    )
-    style_grads = style_grads.astype(jnp.bfloat16).astype(jnp.float32)
-    color_sum = jnp.sum(color_sums[:, 0:3], axis=(0, 2))
-    scalar_row = jnp.concatenate(
-        [
-            jnp.sum(sums_one[:, 3])[None],
-            jnp.sum(sums_two[:, 3])[None],
-            color_sum,
-            jnp.zeros((chans - 5,), jnp.float32),
-        ]
-    )
-    packed = jnp.concatenate(
-        [
-            style_grads.reshape(3 * images, chans),
-            lat_own.astype(jnp.float32),
-            jnp.sum(sums_one[:, 2], axis=0)[None],
-            jnp.sum(sums_two[:, 2], axis=0)[None],
-            jnp.sum(sums_two[:, 8:11], axis=0) * C ** (-0.5),
-            scalar_row[None],
-        ],
-        axis=0,
-    )
-    packed = padded(packed, 16)
-
-    def ref_part(after, part):
+    up_parts = call_up_weight(
+        me, grad_one, xs, up_full, vecs, sums_one, scatter_order(False), layout
+    )
+    *feat_grads, feat_sums = call_up_back(
+        up_parts[0], me, grad_one, feat, vecs, sums_one, up_square, up_full, layout
+    )
+
+    def ref_part(after, part, at_once=False, small=()):
         return call_flat_weight(
-            me, after, grad_two, maps, ref_full, vecs, sums_two, order, layout, part
+            me,
+            after,
+            grad_two,
+            maps,
+            ref_full,
+            vecs,
+            sums_two,
+            scatter_order(at_once),
+            layout,
+            part,
+            small,
         )
 
     if by_hand:
-        other = lax.dynamic_slice_in_dim(feat_grad, local_chans - col_start, local_chans, 1)
-        other = other.astype(jnp.bfloat16)
-        row_steps = gather_rows(packed, devices)
-        up_steps = scatter_blocks(*up_parts, devices)
+        kept_grad, other = feat_grads
+        small_sums = (lat_own[:, None, :], sums_one, feat_sums, color_sums)
+        up_steps = scatter_blocks(*up_parts, devices, False)
         next(up_steps)
-        kept, sent, token = ref_part(up_steps.send(feat_sums) + next(row_steps) + (other,), 0)
-        other = tie(across(other, BIT_X, devices), token)
-        steps = [scatter_blocks(kept, sent, devices)]
+        kept, sent, token = ref_part(up_steps.send(feat_sums) + (other,), 0, small=small_sums)
+        other = across(other, BIT_X, devices)
+        first_steps = scatter_blocks(kept, sent, devices, False)
+        next(first_steps)
+        kept, sent, token = ref_part(up_steps.send(token) + (token,), 1, True)
+        steps = [scatter_blocks(kept, sent, devices, True)]
         next(steps[0])
-        kept, sent, token = ref_part(up_steps.send(token) + row_steps.send(token) + (token,), 1)
-        steps.append(scatter_blocks(kept, sent, devices))
+        kept, sent, token = ref_part(
+            up_steps.send(token) + first_steps.send(token) + (token,), 2, True
+        )
+        steps.append(scatter_blocks(kept, sent, devices, True))
         next(steps[1])
-        kept, sent, token = ref_part(
-            up_steps.send(token) + steps[0].send(token) + row_steps.send(token) + (token,), 2
-        )
-        steps.append(scatter_blocks(kept, sent, devices))
-        up_grad = up_steps.send(token)
-        row_steps.send(token)
-        all_rows = next(row_steps)
+        last = steps[1].send(None)
+        first_steps.send(token)
         steps[0].send(token)
-        next(steps[1])
-        ref_grad = jnp.concatenate([list(step)[-1] for step in steps])
+        first_steps.send(last)
+        steps[0].send(last)
+        up_grad = up_steps.send(last)
+        last = steps[1].send(None)
+        other = tie(other, last)
+        first_grad, next_grad = first_steps.send(last), steps[0].send(last)
+        ref_grad = jnp.concatenate([first_grad[0:3], next_grad, steps[1].send(None)])
     else:
         up_grad = scatter_whole(up_parts[0], n_img, n_ch, rows_own, local_chans)
         ref_grad = jnp.concatenate(
@@ -1116,13 +1196,12 @@
     ref_grad = jnp.transpose(ref_grad, (2, 0, 1))
 
     if by_hand:
-        kept = my_chans(feat_grad, 1)
         other = other.astype(jnp.float32)
         feat_grad = jnp.where(
-            ch_index == 0, jnp.concatenate([kept, other]), jnp.concatenate([other, kept])
+            ch_index == 0, jnp.concatenate([kept_grad, other]), jnp.concatenate([other, kept_grad])
         )
     else:
-        feat_grad = lax.all_gather(feat_grad, "ch", axis=0, tiled=True)[::share] * share
+        feat_grad = lax.all_gather(feat_grads[0], "ch", axis=0, tiled=True)[::share] * share
         feat_grad = my_chans(feat_grad, 1)
     features_grad = jnp.transpose(feat_grad, (1, 0, 2))
 
@@ -1146,10 +1225,33 @@
         scalars_square,
     )
     if by_hand:
-        small_new = call_small_finish(
-            me, all_rows, small_old, images, layout, style_gain
-        )
+        small_new = call_small_finish(first_grad[3:7], small_old, style_gain, devices)
     else:
+        style_grads = jnp.stack(
+            [feat_sums[:, 0], sums_one[:, 0] + sums_two[:, 5], sums_two[:, 0]]
+        )
+        style_grads = style_grads.astype(jnp.bfloat16).astype(jnp.float32)
+        color_sum = jnp.sum(color_sums[:, 0:3], axis=(0, 2))
+        scalar_row = jnp.concatenate(
+            [
+                jnp.sum(sums_one[:, 3])[None],
+                jnp.sum(sums_two[:, 3])[None],
+                color_sum,
+                jnp.zeros((chans - 5,), jnp.float32),
+            ]
+        )
+        packed = jnp.concatenate(
+            [
+                style_grads.reshape(3 * images, chans),
+                lat_own.astype(jnp.float32),
+                jnp.sum(sums_one[:, 2], axis=0)[None],
+                jnp.sum(sums_two[:, 2], axis=0)[None],
+                jnp.sum(sums_two[:, 8:11], axis=0) * C ** (-0.5),
+                scalar_row[None],
+            ],
+            axis=0,
+        )
+        packed = padded(packed, 16)
         every = lax.all_gather(packed, BOTH, axis=0, tiled=False)
         first_sum = 4 * images
         sums = jnp.sum(every[:, first_sum : first_sum + 6], axis=0)

time: 469 us -> 443 us (0.945)
  local copies, waits for them, and re-layouts: 42.8 us -> 24.7 us
  waiting for transfers between devices: 49.2 us -> 55.8 us
  Pallas kernels: 269 us -> 263 us
  other arithmetic: 32.8 us -> 27.7 us
    concatenate x3, local copies, waits for them, and re-layouts: 8.25 us -> 0.93 us  [the longest x1 0.68 us: call_flat_forward(): jnp.concatenate([jnp.transpose(rgb), jnp.zeros((chans, 112), rgb.dtype)],...]
    ppermute x68 -> x60, waiting for transfers between devices: 49.2 us -> 55.8 us  [across(): lax.ppermute(values, BOTH, [(device, device ^ bits) for device in range(d...]
    pallas_call x1, Pallas kernels: 74.4 us -> 68.3 us  [call_flat_forward(): pl.pallas_call(functools.partial(flat_forward, offsets_of(weight), layout...]
    ppermute x68 -> x60, starting transfers between devices: 66.2 us -> 63.1 us  [across(): lax.ppermute(values, BOTH, [(device, device ^ bits) for device in range(d...]
    unnamed x134 -> x99, local copies, waits for them, and re-layouts: 13.3 us -> 10.3 us
  transfers between devices with their start and end apart: 68 -> 60, of which waited for: 21 -> 14; matrix products, arithmetic and copies ran while one was open for 15% -> 11% of each run, Pallas kernels for 24% -> 26%
where the time goes in v3:
time: 443 us; the launch traced here: 437 us
  Pallas kernels  263 us (59%)
  starting transfers between devices  63.1 us (14%)
  waiting for transfers between devices  55.8 us (13%)
  other arithmetic  27.7 us (6%)
  local copies, waits for them, and re-layouts  24.7 us (6%)
    pallas_call x1, Pallas kernels, call_flat_forward(): pl.pallas_call(functools.partial(flat_forward, offsets_of(weight), layout...  68.3 us
    pallas_call x3, Pallas kernels, call_flat_weight(): pl.pallas_call(functools.partial(flat_weight, order, layout, part, len(af...  63.6 us
    ppermute x60, starting transfers between devices, across(): lax.ppermute(values, BOTH, [(device, device ^ bits) for device in range(d...  63.1 us
    pallas_call x1, Pallas kernels, call_flat_back(): pl.pallas_call(flat_back, grid=(images, 2), in_specs=[SMEM, per_image(gra...  58.7 us
    ppermute x60, waiting for transfers between devices, across(): lax.ppermute(values, BOTH, [(device, device ^ bits) for device in range(d...  55.8 us
    pallas_call x1, Pallas kernels, call_up_forward(): pl.pallas_call(functools.partial(up_forward, offsets_of(weight), layout,...  30.5 us
    pallas_call x1, Pallas kernels, call_up_weight(): pl.pallas_call(functools.partial(up_weight, order, layout), grid=(images,...  21 us
    pallas_call x1, Pallas kernels, call_up_back(): pl.pallas_call(functools.partial(up_back, layout), grid=(images,), in_spe...  19 us
  transfers between devices with their start and end apart: 60, of which 14 were waited for; matrix products, arithmetic and copies ran while one was open for 11% of the time, Pallas kernels for 26%

profile of v3, /device:TPU:0, one launch (start us, length us, event | category | flops | bytes accessed | tf_op | source)
XLA Modules:
  0.0 437.3 jit_solution(6750279118355681058)
XLA Ops:
  2.6 4.1 collective-permute-start.2
  8.3 4.4 %constant_dynamic-slice_fusion.4 = (bf16[256,2,1024]{2,1,0:T(2,128)(2,1)S(1)}, bf16[256,2,1024]{2,1,0:T(2,128)(2,1)S(1)}) fusion(bf16[256,4,1024]{2,1,0:T(4,128)(2,1)} %param.30, s32[]{:T(128)S(6)} %select_n.107, s32[]{:T(128)S(6)} %select_n.108), kind=kLoop, calls=%fused_computation.134 | loop fusion | bytes 4194312 | tf_op jit(solution)/shard_map/dynamic_slice | solution.py:1061
  23.0 16.8 %collective-permute-done.6 = f32[8,256]{1,0:T(8,128)S(1)} collective-permute-done((f32[8,256]{1,0:T(8,128)S(1)}, f32[8,256]{1,0:T(8,128)S(1)}, u32[]{:S(2)}, u32[]{:S(2)}) %collective-permute-start.6) | collective-permute-done | bytes 8224 | tf_op jit(solution)/shard_map/ppermute | solution.py:881
  49.8 4.5 %collective-permute-done.8 = bf16[9,32,256]{2,1,0:T(8,128)(2,1)S(1)} collective-permute-done((bf16[9,32,256]{2,1,0:T(8,128)(2,1)}, bf16[9,32,256]{2,1,0:T(8,128)(2,1)S(1)}, u32[]{:S(2)}, u32[]{:S(2)}) %collective-permute-start.8) | collective-permute-done | bytes 147488 | tf_op jit(solution)/shard_map/ppermute | solution.py:881
  57.6 3.3 fusion.1.refs_3_
  61.6 4.3 collective-permute-done.1.refs_8_
  69.6 7.4 %collective-permute-done.11.refs_10_ = bf16[2,12,32,256]{3,2,1,0:T(8,128)(2,1)} collective-permute-done((bf16[2,12,32,256]{3,2,1,0:T(8,128)(2,1)}, bf16[2,12,32,256]{3,2,1,0:T(8,128)(2,1)}, u32[]{:S(2)}, u32[]{:S(2)}) %collective-permute-start.11) | collective-permute-done | bytes 393248 | tf_op jit(solution)/shard_map/ppermute | solution.py:881
  83.3 30.5 %up_forward.1 = (f32[2,4,1024,512]{3,2,1,0:T(8,128)}, bf16[2,4,2,1088,512]{4,3,2,1,0:T(8,128)(2,1)}, bf16[2,2,1056,512]{3,2,1,0:T(8,128)(2,1)}, f32[512,512]{1,0...) custom-call(bf16[4,9,32,256]{3,2,1,0:T(8,128)(2,1)} %copy-done.12, s32[1]{0:T(128)} %bitcast.refs_1_.refs_0_.refs_3_.refs_6_, ...), custom_call_target="tpu_custom_call" | custom-call | flops 9663676416 | bytes 60000000 | tf_op jit(solution)/shard_map/up_forward/pallas_call | solution.py:669
  118.7 68.3 %flat_forward.1 = (bf16[2,4,2,1088,512]{4,3,2,1,0:T(8,128)(2,1)}, f32[2,16,512]{2,1,0:T(8,128)}, f32[2,8,128]{2,1,0:T(8,128)}, bf16[9,512,512]{2,1,0:T(8,128)(2,1)}) custom-call(s32[1]{0:T(128)} %bitcast.refs_1_.refs_0_.refs_3_.refs_6_, f32[5]{0:T(128)} %scal_ref.1, bf16[2,4,2,1088,512]{4,3,2,1,0:T(8,128)(2,1)} %get-tuple-element.107.refs_2_.refs_5_.refs_8_, ...), custom_call_target="tpu_custom_call" | custom-call | flops 38654705664 | bytes 60000000 | tf_op jit(solution)/shard_map/flat_forward/pallas_call | solution.py:715
  187.0 58.7 %flat_back.1 = (bf16[2,4,2,1056,512]{4,3,2,1,0:T(8,128)(2,1)}, f32[2,8,512]{2,1,0:T(8,128)}) custom-call(f32[5]{0:T(128)} %scal_ref.1, bf16[2,4,2,1088,512]{4,3,2,1,0:T(8,128)(2,1)} %get-tuple-element.117.grad_ref.refs_4_.refs_7_, f32[2,4,1024,512]{3,2,1,0:T(8,128)} %get-tuple-element.118.raw_ref, ...), custom_call_target="tpu_custom_call" | custom-call | flops 38654705664 | bytes 60000000 | tf_op jit(solution)/shard_map/flat_back/pallas_call | solution.py:798
  245.8 21.0 %up_weight.1 = (f32[16,9,32,256]{3,2,1,0:T(8,128)}, bf16[16,9,32,256]{3,2,1,0:T(8,128)(2,1)}) custom-call(s32[1]{0:T(128)} %bitcast.refs_1_.refs_0_.refs_3_.refs_6_, bf16[2,4,2,1056,512]{4,3,2,1,0:T(8,128)(2,1)} %get-tuple-element.120.refs_1_.refs_2_, bf16[2,2,1056,512]{3,2,1,0:T(8,128)(2,1)} %get-tuple-element.121.refs_2_, ...), custom_call_target="tpu_custom_call" | custom-call | flops 9663676416 | bytes 30000000 | tf_op jit(solution)/shard_map/up_weight/pallas_call | solution.py:824
  267.7 19.0 %up_back.1 = (f32[2,256,1024]{2,1,0:T(8,128)}, bf16[2,256,1024]{2,1,0:T(8,128)(2,1)}, f32[2,8,512]{2,1,0:T(8,128)}) custom-call(f32[16,9,32,256]{3,2,1,0:T(8,128)} %get-tuple-element.124.refs_0_, s32[1]{0:T(128)} %bitcast.refs_1_.refs_0_.refs_3_.refs_6_, bf16[2,4,2,1056,512]{4,3,2,1,0:T(8,128)(2,1)} %get-tuple-element.120.refs_1_.refs_2_, ...), custom_call_target="tpu_custom_call" | custom-call | flops 9663676416 | bytes 30000000 | tf_op jit(solution)/shard_map/up_back/pallas_call | solution.py:854
  288.2 3.2 convert_add_fusion
  295.1 22.5 %flat_weight_0.1 = (f32[16,7,32,256]{3,2,1,0:T(8,128)}, bf16[16,7,32,256]{3,2,1,0:T(8,128)(2,1)}, f32[8,128]{1,0:T(8,128)}) custom-call(bf16[2,2,9,32,256]{4,3,2,1,0:T(8,128)(2,1)} %copy-done.15, bf16[2,2,9,32,256]{4,3,2,1,0:T(8,128)(2,1)} %copy-done.14, bf16[2,256,1024]{2,1,0:T(8,128)(2,1)} %get-tuple-element.127.refs_2_, ...), custom_call_target="tpu_custom_call" | custom-call | flops 12884901888 | bytes 40000000 | tf_op jit(solution)/shard_map/flat_weight_0/pallas_call | solution.py:768
  317.6 7.4 %collective-permute-done.31 = bf16[2,2,9,32,256]{4,3,2,1,0:T(8,128)(2,1)S(1)} collective-permute-done((bf16[2,2,9,32,256]{4,3,2,1,0:T(8,128)(2,1)S(1)}, bf16[2,2,9,32,256]{4,3,2,1,0:T(8,128)(2,1)S(1)}, u32[]{:S(2)}, u32[]{:S(2)}) %collective-permute-start.31) | collective-permute-done | bytes 589856 | tf_op jit(solution)/shard_map/ppermute | solution.py:881
  329.6 20.5 %flat_weight_1.1 = (f32[16,3,32,256]{3,2,1,0:T(8,128)}, bf16[16,3,32,256]{3,2,1,0:T(8,128)(2,1)}, f32[8,128]{1,0:T(8,128)}) custom-call(bf16[2,9,32,256]{3,2,1,0:T(8,128)(2,1)} %copy-done.21, bf16[2,9,32,256]{3,2,1,0:T(8,128)(2,1)} %copy-done.20, f32[8,128]{1,0:T(8,128)} %get-tuple-element.133.refs_2_, s32[1]{0:T(128)} %bitcast.refs_1_.refs_0_.refs_3_.refs_6_, ...), custom_call_target="tpu_custom_call" | custom-call | flops 12884901888 | bytes 40000000 | tf_op jit(solution)/shard_map/flat_weight_1/pallas_call | solution.py:768
  351.8 3.5 convert_add_fusion.1
  358.6 20.6 %flat_weight_2.1 = (f32[16,3,32,256]{3,2,1,0:T(8,128)}, bf16[16,3,32,256]{3,2,1,0:T(8,128)(2,1)}, f32[8,128]{1,0:T(8,128)}) custom-call(bf16[9,32,256]{2,1,0:T(8,128)(2,1)} %fusion.33.refs_0_, bf16[9,32,256]{2,1,0:T(8,128)(2,1)} %copy-done.27, bf16[9,32,256]{2,1,0:T(8,128)(2,1)} %get-tuple-element.276.refs_2_, ...), custom_call_target="tpu_custom_call" | custom-call | flops 12884901888 | bytes 40000000 | tf_op jit(solution)/shard_map/flat_weight_2/pallas_call | solution.py:768
  386.7 5.2 %collective-permute-done.45 = bf16[2,7,32,256]{3,2,1,0:T(8,128)(2,1)S(1)} collective-permute-done((bf16[2,7,32,256]{3,2,1,0:T(8,128)(2,1)S(1)}, bf16[2,7,32,256]{3,2,1,0:T(8,128)(2,1)S(1)}, u32[]{:S(2)}, u32[]{:S(2)}) %collective-permute-start.45) | collective-permute-done | bytes 229408 | tf_op jit(solution)/shard_map/ppermute | solution.py:881
  395.3 2.2 collective-permute-start.42
  397.5 4.8 %collective-permute-done.52 = bf16[4,3,32,256]{3,2,1,0:T(8,128)(2,1)S(1)} collective-permute-done((bf16[4,3,32,256]{3,2,1,0:T(8,128)(2,1)S(1)}, bf16[4,3,32,256]{3,2,1,0:T(8,128)(2,1)S(1)}, u32[]{:S(2)}, u32[]{:S(2)}) %collective-permute-start.52) | collective-permute-done | bytes 196640 | tf_op jit(solution)/shard_map/ppermute | solution.py:881
  402.3 2.7 collective-permute-start.40
  411.6 2.3 collective-permute-start.49
  429.0 4.7 %copy.96 = f32[256,4,1024]{2,1,0:T(4,128)} copy(f32[256,4,1024]{2,0,1:T(8,128)S(1)} %fusion) | data formatting | bytes 8388608
  (293 shorter events, 93.2 us)
Async XLA Ops:
  2.6 39.0 %collective-permute-start.2 = (bf16[12,32,256]{2,1,0:T(8,128)(2,1)S(1)}, bf16[12,32,256]{2,1,0:T(8,128)(2,1)}, u32[]{:S(2)}, u32[]{:S(2)}) collective-permute-start(bf16[12,32,256]{2,1,0:T(8,128)(2,1)S(1)} %pad_maximum_fusion.3), channel_id=1, source_target_pairs={{0,16},{1,17},{2,18},{3,19},{4,20},{5,21},{6,22},{7,23},{8,24},{9,... | collective-permute-start | bytes 589832 | tf_op jit(solution)/shard_map/ppermute | solution.py:881
  6.7 36.6 %collective-permute-start.3 = (bf16[12,32,256]{2,1,0:T(8,128)(2,1)S(1)}, bf16[12,32,256]{2,1,0:T(8,128)(2,1)}, u32[]{:S(2)}, u32[]{:S(2)}) collective-permute-start(bf16[12,32,256]{2,1,0:T(8,128)(2,1)S(1)} %pad_maximum_fusion.3), channel_id=1, source_target_pairs={{0,24},{1,25},{2,26},{3,27},{4,28},{5,29},{6,30},{7,31},{8,16},{9,... | collective-permute-start | bytes 589832 | tf_op jit(solution)/shard_map/ppermute | solution.py:881
  8.1 37.5 %collective-permute-start = (bf16[12,32,256]{2,1,0:T(8,128)(2,1)S(1)}, bf16[12,32,256]{2,1,0:T(8,128)(2,1)S(1)}, u32[]{:S(2)}, u32[]{:S(2)}) collective-permute-start(bf16[12,32,256]{2,1,0:T(8,128)(2,1)S(1)} %pad_maximum_fusion.3), channel_id=1, source_target_pairs={{0,8},{1,9},{2,10},{3,11},{4,12},{5,13},{6,14},{7,15},{8,0},{9,1},... | collective-permute-start | bytes 589832 | tf_op jit(solution)/shard_map/ppermute | solution.py:881
  15.0 41.0 %collective-permute-start.5 = (bf16[256,2,1024]{0,2,1:T(8,128)(2,1)}, bf16[256,2,1024]{0,2,1:T(8,128)(2,1)}, u32[]{:S(2)}, u32[]{:S(2)}) collective-permute-start(bf16[256,2,1024]{0,2,1:T(8,128)(2,1)} %copy.103), channel_id=1, source_target_pairs={{0,1},{1,0},{2,3},{3,2},{4,5},{5,4},{6,7},{7,6},{8,9},{9,8},{10,11... | collective-permute-start | bytes 3145736 | tf_op jit(solution)/shard_map/ppermute | solution.py:881
  16.5 23.2 %collective-permute-start.6 = (f32[8,256]{1,0:T(8,128)S(1)}, f32[8,256]{1,0:T(8,128)S(1)}, u32[]{:S(2)}, u32[]{:S(2)}) collective-permute-start(f32[8,256]{1,0:T(8,128)S(1)} %pad_maximum_fusion.5), channel_id=1, source_target_pairs={{0,1},{1,0},{2,3},{3,2},{4,5},{5,4},{6,7},{7,6},{8,9},{9,8},{10,11... | collective-permute-start | bytes 24584 | tf_op jit(solution)/shard_map/ppermute | solution.py:881
  45.6 15.3 %collective-permute-start.4 = (bf16[2,12,32,256]{3,2,1,0:T(8,128)(2,1)S(1)}, bf16[2,12,32,256]{3,2,1,0:T(8,128)(2,1)}, u32[]{:S(2)}, u32[]{:S(2)}) collective-permute-start(bf16[2,12,32,256]{3,2,1,0:T(8,128)(2,1)S(1)} %pad_maximum_fusion.2.refs_11_), channel_id=1, source_target_pairs={{0,4},{1,5},{2,6},{3,7},{4,0},{5,1},{6,2},{7,3},{8,12},{9,13},{10,... | collective-permute-start | bytes 1179656 | tf_op jit(solution)/shard_map/ppermute | solution.py:881
  54.3 13.2 %collective-permute-start.18 = (bf16[2,12,32,256]{3,2,1,0:T(8,128)(2,1)S(1)}, bf16[2,12,32,256]{3,2,1,0:T(8,128)(2,1)S(1)}, u32[]{:S(2)}, u32[]{:S(2)}) collective-permute-start(bf16[2,12,32,256]{3,2,1,0:T(8,128)(2,1)S(1)} %pad_maximum_fusion.2.refs_11_), channel_id=1, source_target_pairs={{0,2},{1,3},{2,0},{3,1},{4,6},{5,7},{6,4},{7,5},{8,10},{9,11},{10,... | collective-permute-start | bytes 1179656 | tf_op jit(solution)/shard_map/ppermute | solution.py:881
  79.5 34.3 %collective-permute-start.22 = (bf16[4,9,32,256]{3,2,1,0:T(8,128)(2,1)S(1)}, bf16[4,9,32,256]{3,2,1,0:T(8,128)(2,1)S(1)}, u32[]{:S(2)}, u32[]{:S(2)}) collective-permute-start(bf16[4,9,32,256]{3,2,1,0:T(8,128)(2,1)S(1)} %pad_maximum_fusion.refs_0_.refs_10_), channel_id=1, source_target_pairs={{0,5},{1,4},{2,7},{3,6},{4,1},{5,0},{6,3},{7,2},{8,13},{9,12},{10,... | collective-permute-start | bytes 1769480 | tf_op jit(solution)/shard_map/ppermute | solution.py:881
  81.3 32.6 %collective-permute-start.23 = (bf16[4,9,32,256]{3,2,1,0:T(8,128)(2,1)S(1)}, bf16[4,9,32,256]{3,2,1,0:T(8,128)(2,1)S(1)}, u32[]{:S(2)}, u32[]{:S(2)}) collective-permute-start(bf16[4,9,32,256]{3,2,1,0:T(8,128)(2,1)S(1)} %pad_maximum_fusion.refs_0_.refs_10_), channel_id=1, source_target_pairs={{0,1},{1,0},{2,3},{3,2},{4,5},{5,4},{6,7},{7,6},{8,9},{9,8},{10,11... | collective-permute-start | bytes 1769480 | tf_op jit(solution)/shard_map/ppermute | solution.py:881
  82.1 31.8 %collective-permute-start.24 = (bf16[4,9,32,256]{3,2,1,0:T(8,128)(2,1)S(1)}, bf16[4,9,32,256]{3,2,1,0:T(8,128)(2,1)S(1)}, u32[]{:S(2)}, u32[]{:S(2)}) collective-permute-start(bf16[4,9,32,256]{3,2,1,0:T(8,128)(2,1)S(1)} %pad_maximum_fusion.refs_0_.refs_10_), channel_id=1, source_target_pairs={{0,4},{1,5},{2,6},{3,7},{4,0},{5,1},{6,2},{7,3},{8,12},{9,13},{10,... | collective-permute-start | bytes 1769480 | tf_op jit(solution)/shard_map/ppermute | solution.py:881
  266.7 21.4 %collective-permute-start.30 = (bf16[16,9,32,256]{3,2,1,0:T(8,128)(2,1)}, bf16[16,9,32,256]{3,2,1,0:T(8,128)(2,1)S(1)}, u32[]{:S(2)}, u32[]{:S(2)}) collective-permute-start(bf16[16,9,32,256]{3,2,1,0:T(8,128)(2,1)} %get-tuple-element.128), channel_id=1, source_target_pairs={{0,2},{1,3},{2,0},{3,1},{4,6},{5,7},{6,4},{7,5},{8,10},{9,11},{10,... | collective-permute-start | bytes 7077896 | tf_op jit(solution)/shard_map/ppermute | solution.py:881
  286.7 139.2 %collective-permute-start.29 = (bf16[2,256,1024]{2,1,0:T(8,128)(2,1)}, bf16[2,256,1024]{2,1,0:T(8,128)(2,1)}, u32[]{:S(2)}, u32[]{:S(2)}) collective-permute-start(bf16[2,256,1024]{2,1,0:T(8,128)(2,1)} %get-tuple-element.127.refs_2_), channel_id=1, source_target_pairs={{0,1},{1,0},{2,3},{3,2},{4,5},{5,4},{6,7},{7,6},{8,9},{9,8},{10,11... | collective-permute-start | bytes 3145736 | tf_op jit(solution)/shard_map/ppermute | solution.py:881
  293.6 31.5 %collective-permute-start.31 = (bf16[2,2,9,32,256]{4,3,2,1,0:T(8,128)(2,1)S(1)}, bf16[2,2,9,32,256]{4,3,2,1,0:T(8,128)(2,1)S(1)}, u32[]{:S(2)}, u32[]{:S(2)}) collective-permute-start(bf16[2,2,9,32,256]{4,3,2,1,0:T(8,128)(2,1)S(1)} %get-tuple-element.265.refs_0_), channel_id=1, source_target_pairs={{0,1},{1,0},{2,3},{3,2},{4,5},{5,4},{6,7},{7,6},{8,9},{9,8},{10,11... | collective-permute-start | bytes 1769480 | tf_op jit(solution)/shard_map/ppermute | solution.py:881
  294.3 30.7 %collective-permute-start.32 = (bf16[2,2,9,32,256]{4,3,2,1,0:T(8,128)(2,1)S(1)}, bf16[2,2,9,32,256]{4,3,2,1,0:T(8,128)(2,1)S(1)}, u32[]{:S(2)}, u32[]{:S(2)}) collective-permute-start(bf16[2,2,9,32,256]{4,3,2,1,0:T(8,128)(2,1)S(1)} %get-tuple-element.264.refs_1_), channel_id=1, source_target_pairs={{0,4},{1,5},{2,6},{3,7},{4,0},{5,1},{6,2},{7,3},{8,12},{9,13},{10,... | collective-permute-start | bytes 1769480 | tf_op jit(solution)/shard_map/ppermute | solution.py:881
  317.6 34.1 %collective-permute-start.35 = (bf16[16,7,32,256]{3,2,1,0:T(8,128)(2,1)}, bf16[16,7,32,256]{3,2,1,0:T(8,128)(2,1)}, u32[]{:S(2)}, u32[]{:S(2)}) collective-permute-start(bf16[16,7,32,256]{3,2,1,0:T(8,128)(2,1)} %get-tuple-element.140), channel_id=1, source_target_pairs={{0,2},{1,3},{2,0},{3,1},{4,6},{5,7},{6,4},{7,5},{8,10},{9,11},{10,... | collective-permute-start | bytes 5505032 | tf_op jit(solution)/shard_map/ppermute | solution.py:881
  327.4 22.7 %collective-permute-start.33 = (bf16[2,9,32,256]{3,2,1,0:T(8,128)(2,1)S(1)}, bf16[2,9,32,256]{3,2,1,0:T(8,128)(2,1)S(1)}, u32[]{:S(2)}, u32[]{:S(2)}) collective-permute-start(bf16[2,9,32,256]{3,2,1,0:T(8,128)(2,1)S(1)} %fusion.21.refs_0_), channel_id=1, source_target_pairs={{0,4},{1,5},{2,6},{3,7},{4,0},{5,1},{6,2},{7,3},{8,12},{9,13},{10,... | collective-permute-start | bytes 884744 | tf_op jit(solution)/shard_map/ppermute | solution.py:881
  328.2 21.9 %collective-permute-start.34 = (bf16[2,9,32,256]{3,2,1,0:T(8,128)(2,1)S(1)}, bf16[2,9,32,256]{3,2,1,0:T(8,128)(2,1)S(1)}, u32[]{:S(2)}, u32[]{:S(2)}) collective-permute-start(bf16[2,9,32,256]{3,2,1,0:T(8,128)(2,1)S(1)} %fusion.22.refs_1_), channel_id=1, source_target_pairs={{0,1},{1,0},{2,3},{3,2},{4,5},{5,4},{6,7},{7,6},{8,9},{9,8},{10,11... | collective-permute-start | bytes 884744 | tf_op jit(solution)/shard_map/ppermute | solution.py:881
  350.1 29.0 %collective-permute-start.50 = (bf16[16,3,32,256]{3,2,1,0:T(8,128)(2,1)}, bf16[16,3,32,256]{3,2,1,0:T(8,128)(2,1)}, u32[]{:S(2)}, u32[]{:S(2)}) collective-permute-start(bf16[16,3,32,256]{3,2,1,0:T(8,128)(2,1)} %get-tuple-element.157), channel_id=1, source_target_pairs={{0,2},{1,3},{2,0},{3,1},{4,6},{5,7},{6,4},{7,5},{8,10},{9,11},{10,... | collective-permute-start | bytes 2359304 | tf_op jit(solution)/shard_map/ppermute | solution.py:881
  350.9 55.1 %collective-permute-start.41 = (bf16[9,32,256]{2,1,0:T(8,128)(2,1)S(1)}, bf16[9,32,256]{2,1,0:T(8,128)(2,1)S(1)}, u32[]{:S(2)}, u32[]{:S(2)}) collective-permute-start(bf16[9,32,256]{2,1,0:T(8,128)(2,1)S(1)} %get-tuple-element.277.refs_1_), channel_id=1, source_target_pairs={{0,16},{1,17},{2,18},{3,19},{4,20},{5,21},{6,22},{7,23},{8,24},{9,... | collective-permute-start | bytes 442376 | tf_op jit(solution)/shard_map/ppermute | solution.py:881
  356.7 24.5 %collective-permute-start.43 = (bf16[2,2,7,32,256]{4,3,2,1,0:T(8,128)(2,1)}, bf16[2,2,7,32,256]{4,3,2,1,0:T(8,128)(2,1)}, u32[]{:S(2)}, u32[]{:S(2)}) collective-permute-start(bf16[2,2,7,32,256]{4,3,2,1,0:T(8,128)(2,1)} %get-tuple-element.269.refs_3_), channel_id=1, source_target_pairs={{0,1},{1,0},{2,3},{3,2},{4,5},{5,4},{6,7},{7,6},{8,9},{9,8},{10,11... | collective-permute-start | bytes 1376264 | tf_op jit(solution)/shard_map/ppermute | solution.py:881
  357.8 24.9 %collective-permute-start.44 = (bf16[2,2,7,32,256]{4,3,2,1,0:T(8,128)(2,1)}, bf16[2,2,7,32,256]{4,3,2,1,0:T(8,128)(2,1)}, u32[]{:S(2)}, u32[]{:S(2)}) collective-permute-start(bf16[2,2,7,32,256]{4,3,2,1,0:T(8,128)(2,1)} %get-tuple-element.268.refs_4_), channel_id=1, source_target_pairs={{0,4},{1,5},{2,6},{3,7},{4,0},{5,1},{6,2},{7,3},{8,12},{9,13},{10,... | collective-permute-start | bytes 1376264 | tf_op jit(solution)/shard_map/ppermute | solution.py:881
  381.2 14.1 %collective-permute-start.51 = (bf16[4,3,32,256]{3,2,1,0:T(8,128)(2,1)S(1)}, bf16[4,3,32,256]{3,2,1,0:T(8,128)(2,1)S(1)}, u32[]{:S(2)}, u32[]{:S(2)}) collective-permute-start(bf16[4,3,32,256]{3,2,1,0:T(8,128)(2,1)S(1)} %get-tuple-element.272), channel_id=1, source_target_pairs={{0,1},{1,0},{2,3},{3,2},{4,5},{5,4},{6,7},{7,6},{8,9},{9,8},{10,11... | collective-permute-start | bytes 589832 | tf_op jit(solution)/shard_map/ppermute | solution.py:881
  421.5 14.4 %collective-permute-start.57 = (bf16[3,32,256]{2,1,0:T(8,128)(2,1)S(1)}, bf16[3,32,256]{2,1,0:T(8,128)(2,1)S(1)}, u32[]{:S(2)}, u32[]{:S(2)}) collective-permute-start(bf16[3,32,256]{2,1,0:T(8,128)(2,1)S(1)} %get-tuple-element.289), channel_id=1, source_target_pairs={{0,8},{1,9},{2,10},{3,11},{4,12},{5,13},{6,14},{7,15},{8,0},{9,1},... | collective-permute-start | bytes 147464 | tf_op jit(solution)/shard_map/ppermute | solution.py:881
  422.5 13.4 %collective-permute-start.58 = (bf16[3,32,256]{2,1,0:T(8,128)(2,1)S(1)}, bf16[3,32,256]{2,1,0:T(8,128)(2,1)S(1)}, u32[]{:S(2)}, u32[]{:S(2)}) collective-permute-start(bf16[3,32,256]{2,1,0:T(8,128)(2,1)S(1)} %get-tuple-element.288), channel_id=1, source_target_pairs={{0,16},{1,17},{2,18},{3,19},{4,20},{5,21},{6,22},{7,23},{8,24},{9,... | collective-permute-start | bytes 147464 | tf_op jit(solution)/shard_map/ppermute | solution.py:881
  (85 other events, 691.8 us)
